TPU v7x, 512 devices: a whole 4x4x16 slice. The times are simulated.
512 devices in a mesh: gx: 4 (over x), gy: 4 (over y), gz: 32 (over z, core).
Axes of the slice: x: 4, y: 4, z: 16, core: 2. Of those that a mesh axis runs over, the one named last changes fastest.
Arguments:
- populations: float32 [19, 8, 64, 4096], P(None, 'gx', 'gy', 'gz'), may hold values from 0.005 to 0.8, as said below
- porosity: float32 [8, 64, 4096], P('gx', 'gy', 'gz'), may hold values from 0.05 to 0.45
- solid: int32 [8, 64, 4096], P('gx', 'gy', 'gz'), may hold values 0 or 1
- seed_adjoint: float32 [19, 8, 64, 4096], P(None, 'gx', 'gy', 'gz'), may hold values from -60 to 60
Outputs:
- porosity_grad: float32 [8, 64, 4096], P('gx', 'gy', 'gz')
- initial_adjoint: float32 [19, 8, 64, 4096], P(None, 'gx', 'gy', 'gz')
Inputs may be any that keep to these rules, and one draw needn't show every extreme that they name: `populations`: every population is positive.
All inputs are finite; a program needn't handle non-finite values. No bound on the sum of `solid` on one device may be relied on, other than what follows from the above.
Results may differ from a plain program's by a relative error of at most 0.0003.
Values sent between devices are 32-bit elements; how exact they have to be, the bound alone decides.
No kernel may reach another device: no remote copies, remote signals or barrier semaphores. Data moves between devices by JAX's collectives and lax.ppermute only.
A program may use at most 64 MiB of HBM per device.

v0:
```python
import jax
import jax.numpy as jnp
from jax import lax
from jax.sharding import PartitionSpec as P

STEPS = 3


VELOCITIES = [
    [0, 0, 0],
    [1, 0, 0],
    [-1, 0, 0],
    [0, 1, 0],
    [0, -1, 0],
    [0, 0, 1],
    [0, 0, -1],
    [1, 1, 0],
    [-1, -1, 0],
    [1, -1, 0],
    [-1, 1, 0],
    [1, 0, 1],
    [-1, 0, -1],
    [1, 0, -1],
    [-1, 0, 1],
    [0, 1, 1],
    [0, -1, -1],
    [0, 1, -1],
    [0, -1, 1],
]
OPPOSITE = [0, 2, 1, 4, 3, 6, 5, 8, 7, 10, 9, 12, 11, 14, 13, 16, 15, 18, 17]
LATTICE_WEIGHTS = [1.0 / 3.0] + [1.0 / 18.0] * 6 + [1.0 / 36.0] * 12
OMEGA = 1.25


def extended(shard, sides, width):
    for axis, dim in sides:
        count, length = (lax.axis_size(axis), shard.shape[dim])
        up = [(i, (i + 1) % count) for i in range(count)]
        down = [(j, i) for i, j in up]
        last = lax.slice_in_dim(shard, length - width, length, axis=dim)
        leading = lax.slice_in_dim(shard, 0, width, axis=dim)
        before = lax.ppermute(last, axis, up)
        after = lax.ppermute(leading, axis, down)
        shard = jnp.concatenate([before, shard, after], axis=dim)
    return shard


def relax_collision(field, porosity, solid):
    dtype = field.dtype
    vel_table = jnp.asarray(VELOCITIES, dtype=dtype)
    weight_table = jnp.asarray(LATTICE_WEIGHTS, dtype=dtype).reshape(19, 1, 1, 1)
    density = jnp.sum(field, axis=0)
    momentum = jnp.tensordot(vel_table.T, field, axes=1, precision=lax.Precision.HIGHEST)
    velocity = momentum / density
    projected = jnp.tensordot(vel_table, velocity, axes=1, precision=lax.Precision.HIGHEST)
    speed_sq = jnp.sum(velocity * velocity, axis=0)
    equilibrium = (
        weight_table
        * density
        * (1.0 + 3.0 * projected + 4.5 * projected * projected - 1.5 * speed_sq)
    )
    relaxed = field - OMEGA * (field - equilibrium)
    bounced = jnp.stack([field[index] for index in OPPOSITE])
    blocking = jnp.where(solid == 1, jnp.ones_like(porosity), porosity)
    return (1.0 - blocking) * relaxed + blocking * bounced


def translate(field, sign):
    padded = extended(field, (("gx", 1), ("gy", 2), ("gz", 3)), 1)
    size_x, size_y, size_z = (field.shape[1], field.shape[2], field.shape[3])
    pieces = []
    for index, vel in enumerate(VELOCITIES):
        start_x = 1 - sign * vel[0]
        start_y = 1 - sign * vel[1]
        start_z = 1 - sign * vel[2]
        pieces.append(
            padded[
                index,
                start_x : start_x + size_x,
                start_y : start_y + size_y,
                start_z : start_z + size_z,
            ]
        )
    return jnp.stack(pieces)


def body(populations, porosity, solid, seed_adjoint):
    state_history = [populations]
    current = populations
    for lattice_update in range(STEPS):
        current = translate(relax_collision(current, porosity, solid), 1)
        state_history.append(current)
    adjoint = seed_adjoint
    gradient = jnp.zeros_like(porosity)
    for lattice_update in range(STEPS - 1, -1, -1):
        pulled = translate(adjoint, -1)
        unused_value, backward_pullback = jax.vjp(
            lambda flow_field, porosity_field: relax_collision(flow_field, porosity_field, solid),
            state_history[lattice_update],
            porosity,
        )
        adjoint, grad_part = backward_pullback(pulled)
        gradient = gradient + grad_part
    return (gradient, adjoint)


def solution(mesh):
    in_specs = (
        P(None, "gx", "gy", "gz"),
        P("gx", "gy", "gz"),
        P("gx", "gy", "gz"),
        P(None, "gx", "gy", "gz"),
    )
    out_specs = (P("gx", "gy", "gz"), P(None, "gx", "gy", "gz"))
    return jax.shard_map(body, mesh=mesh, in_specs=in_specs, out_specs=out_specs, check_vma=False)
```

profile of v0, /device:TPU:8, one launch (start us, length us, event | category | flops | bytes accessed | tf_op | source)
XLA Modules:
  0.0 179.7 jit_solution(17467320688593257980)
XLA Ops:
  7.1 4.8 %collective-permute-start.7 = (f32[19,1,16,128]{3,0,2,1:T(8,128)S(1)}, f32[19,1,16,128]{3,0,2,1:T(8,128)S(1)}, u32[]{:S(2)}, u32[]{:S(2)}) collective-permute-start(f32[19,1,16,128]{3,0,2,1:T(8,128)S(1)} %get-tuple-element.185), channel_id=1, source_target_pairs={{128,0},{256,128},{384,256},{0,384},{129,1},{257,129},{385,257},{1... | collective-permute-start | bytes 466952 | tf_op jit(solution)/shard_map/ppermute | solution.py:43
  11.9 1.9 %collective-permute-start.6 = (f32[19,1,16,128]{3,0,2,1:T(8,128)S(1)}, f32[19,1,16,128]{3,0,2,1:T(8,128)S(1)}, u32[]{:S(2)}, u32[]{:S(2)}) collective-permute-start(f32[19,1,16,128]{3,0,2,1:T(8,128)S(1)} %get-tuple-element.184), channel_id=1, source_target_pairs={{0,128},{128,256},{256,384},{384,0},{1,129},{129,257},{257,385},{3... | collective-permute-start | bytes 466952 | tf_op jit(solution)/shard_map/ppermute | solution.py:42
  14.1 2.7 %collective-permute-start.1 = (f32[19,1,16,128]{3,0,2,1:T(8,128)S(1)}, f32[19,1,16,128]{3,0,2,1:T(8,128)S(1)}, u32[]{:S(2)}, u32[]{:S(2)}) collective-permute-start(f32[19,1,16,128]{3,0,2,1:T(8,128)S(1)} %get-tuple-element.206), channel_id=1, source_target_pairs={{0,128},{128,256},{256,384},{384,0},{1,129},{129,257},{257,385},{3... | collective-permute-start | bytes 466952 | tf_op jit(solution)/shard_map/ppermute | solution.py:42
  16.7 4.4 %collective-permute-start = (f32[19,1,16,128]{3,0,2,1:T(8,128)S(1)}, f32[19,1,16,128]{3,0,2,1:T(8,128)S(1)}, u32[]{:S(2)}, u32[]{:S(2)}) collective-permute-start(f32[19,1,16,128]{3,0,2,1:T(8,128)S(1)} %get-tuple-element.207), channel_id=1, source_target_pairs={{128,0},{256,128},{384,256},{0,384},{129,1},{257,129},{385,257},{1... | collective-permute-start | bytes 466952 | tf_op jit(solution)/shard_map/ppermute | solution.py:43
  22.8 5.9 %collective-permute-start.9 = (f32[19,4,1,128]{3,0,2,1:T(8,128)S(1)}, f32[19,4,1,128]{3,0,2,1:T(8,128)S(1)}, u32[]{:S(2)}, u32[]{:S(2)}) collective-permute-start(f32[19,4,1,128]{3,0,2,1:T(8,128)S(1)} %get-tuple-element.130), channel_id=1, source_target_pairs={{32,0},{64,32},{96,64},{0,96},{33,1},{65,33},{97,65},{1,97},{34,2}... | collective-permute-start | bytes 116744 | tf_op jit(solution)/shard_map/ppermute | solution.py:43
  28.8 1.9 %collective-permute-start.8 = (f32[19,4,1,128]{3,0,2,1:T(8,128)S(1)}, f32[19,4,1,128]{3,0,2,1:T(8,128)S(1)}, u32[]{:S(2)}, u32[]{:S(2)}) collective-permute-start(f32[19,4,1,128]{3,0,2,1:T(8,128)S(1)} %get-tuple-element.129), channel_id=1, source_target_pairs={{0,32},{32,64},{64,96},{96,0},{1,33},{33,65},{65,97},{97,1},{2,34}... | collective-permute-start | bytes 116744 | tf_op jit(solution)/shard_map/ppermute | solution.py:42
  32.9 3.9 %collective-permute-start.2 = (f32[19,4,1,128]{3,0,2,1:T(8,128)}, f32[19,4,1,128]{3,0,2,1:T(8,128)}, u32[]{:S(2)}, u32[]{:S(2)}) collective-permute-start(f32[19,4,1,128]{3,0,2,1:T(8,128)} %get-tuple-element.132), channel_id=1, source_target_pairs={{32,0},{64,32},{96,64},{0,96},{33,1},{65,33},{97,65},{1,97},{34,2}... | collective-permute-start | bytes 116744 | tf_op jit(solution)/shard_map/ppermute | solution.py:43
  36.8 1.9 %collective-permute-start.3 = (f32[19,4,1,128]{3,0,2,1:T(8,128)}, f32[19,4,1,128]{3,0,2,1:T(8,128)}, u32[]{:S(2)}, u32[]{:S(2)}) collective-permute-start(f32[19,4,1,128]{3,0,2,1:T(8,128)} %get-tuple-element.131), channel_id=1, source_target_pairs={{0,32},{32,64},{64,96},{96,0},{1,33},{33,65},{65,97},{97,1},{2,34}... | collective-permute-start | bytes 116744 | tf_op jit(solution)/shard_map/ppermute | solution.py:42
  42.6 3.9 %collective-permute-start.11 = (f32[19,4,18,1]{0,1,3,2:T(4,128)}, f32[19,4,18,1]{0,1,3,2:T(4,128)}, u32[]{:S(2)}, u32[]{:S(2)}) collective-permute-start(f32[19,4,18,1]{0,1,3,2:T(4,128)} %copy.79), channel_id=1, source_target_pairs={{1,0},{2,1},{3,2},{4,3},{5,4},{6,5},{7,6},{8,7},{9,8},{10,9},{11,1... | collective-permute-start | bytes 16424 | tf_op jit(solution)/shard_map/ppermute | solution.py:43
  48.8 3.7 %collective-permute-start.4 = (f32[19,4,18,1]{0,1,3,2:T(4,128)}, f32[19,4,18,1]{0,1,3,2:T(4,128)}, u32[]{:S(2)}, u32[]{:S(2)}) collective-permute-start(f32[19,4,18,1]{0,1,3,2:T(4,128)} %copy.50), channel_id=1, source_target_pairs={{1,0},{2,1},{3,2},{4,3},{5,4},{6,5},{7,6},{8,7},{9,8},{10,9},{11,1... | collective-permute-start | bytes 16424 | tf_op jit(solution)/shard_map/ppermute | solution.py:43
  56.3 2.5 %multiply_divide_fusion.1 = (f32[1,2,16,128]{3,0,2,1:T(1,128)}, f32[1,2,16,128]{3,0,2,1:T(1,128)}, f32[1,2,16,128]{3,0,2,1:T(1,128)}, f32[1,2,16,128]{3,0,2,1:T(...) fusion(f32[19,2,16,128]{3,0,2,1:T(8,128)S(1)} %get-tuple-elemen, ...), kind=kLoop, calls=%fused_computation.286 | loop fusion | flops 368640 | bytes 2936832 | tf_op jit(solution)/shard_map/jvp()/div | solution.py:54
  59.7 2.9 %stack.28 = f32[19,2,16,128]{3,0,2,1:T(8,128)S(1)} concatenate(f32[1,2,16,128]{3,0,2,1:T(1,128)} %slice.694, f32[1,2,16,128]{3,0,2,1:T(1,128)} %get-tuple-element.39, f32[1,2,16,128]{3,0,2,1:T(1,128)} %get-tuple-element.38, f32[1,2,16,128]{3,0,2,1:T(1,128)} %get-tuple-element.37, f32[1,2,16,128]{3,0,2,1:T(1,128)} %get-tuple-element.36, f32[1,2,16,128]{3,0,2,1:T(1,128)} %get-tuple-element.35, ...), dimensions={0} | concatenate | bytes 622592 | tf_op jit(solution)/shard_map/stack | solution.py:84
  67.1 2.8 %collective-permute-start.12 = (f32[19,1,16,128]{3,0,2,1:T(8,128)}, f32[19,1,16,128]{3,0,2,1:T(8,128)S(1)}, u32[]{:S(2)}, u32[]{:S(2)}) collective-permute-start(f32[19,1,16,128]{3,0,2,1:T(8,128)} %get-tuple-element.183), channel_id=1, source_target_pairs={{128,0},{256,128},{384,256},{0,384},{129,1},{257,129},{385,257},{1... | collective-permute-start | bytes 466952 | tf_op jit(solution)/shard_map/ppermute | solution.py:43
  70.0 3.0 %collective-permute-start.13 = (f32[19,1,16,128]{3,0,2,1:T(8,128)}, f32[19,1,16,128]{3,0,2,1:T(8,128)}, u32[]{:S(2)}, u32[]{:S(2)}) collective-permute-start(f32[19,1,16,128]{3,0,2,1:T(8,128)} %get-tuple-element.182), channel_id=1, source_target_pairs={{0,128},{128,256},{256,384},{384,0},{1,129},{129,257},{257,385},{3... | collective-permute-start | bytes 466952 | tf_op jit(solution)/shard_map/ppermute | solution.py:42
  79.8 4.6 %collective-permute-start.14 = (f32[19,4,1,128]{3,0,2,1:T(8,128)S(1)}, f32[19,4,1,128]{3,0,2,1:T(8,128)S(1)}, u32[]{:S(2)}, u32[]{:S(2)}) collective-permute-start(f32[19,4,1,128]{3,0,2,1:T(8,128)S(1)} %get-tuple-element.128), channel_id=1, source_target_pairs={{32,0},{64,32},{96,64},{0,96},{33,1},{65,33},{97,65},{1,97},{34,2}... | collective-permute-start | bytes 116744 | tf_op jit(solution)/shard_map/ppermute | solution.py:43
  84.4 2.1 %collective-permute-start.15 = (f32[19,4,1,128]{3,0,2,1:T(8,128)S(1)}, f32[19,4,1,128]{3,0,2,1:T(8,128)S(1)}, u32[]{:S(2)}, u32[]{:S(2)}) collective-permute-start(f32[19,4,1,128]{3,0,2,1:T(8,128)S(1)} %get-tuple-element.127), channel_id=1, source_target_pairs={{0,32},{32,64},{64,96},{96,0},{1,33},{33,65},{65,97},{97,1},{2,34}... | collective-permute-start | bytes 116744 | tf_op jit(solution)/shard_map/ppermute | solution.py:42
  87.5 4.1 %collective-permute-done.15 = f32[19,4,1,128]{3,0,2,1:T(8,128)S(1)} collective-permute-done((f32[19,4,1,128]{3,0,2,1:T(8,128)S(1)}, f32[19,4,1,128]{3,0,2,1:T(8,128)S(1)}, u32[]{:S(2)}, u32[]{:S(2)}) %collective-permute-start.15) | collective-permute-done | bytes 38944 | tf_op jit(solution)/shard_map/ppermute | solution.py:42
  93.8 2.3 %copy.83 = f32[19,4,18,1]{0,1,3,2:T(4,128)} copy(f32[19,4,18,1]{3,0,2,1:T(8,128)} %get-tuple-element.96) | data formatting | bytes 10944 | tf_op jit(solution)/shard_map/slice | solution.py:40
  97.2 3.0 %collective-permute-start.16 = (f32[19,4,18,1]{0,1,3,2:T(4,128)}, f32[19,4,18,1]{0,1,3,2:T(4,128)S(1)}, u32[]{:S(2)}, u32[]{:S(2)}) collective-permute-start(f32[19,4,18,1]{0,1,3,2:T(4,128)} %copy.81), channel_id=1, source_target_pairs={{1,0},{2,1},{3,2},{4,3},{5,4},{6,5},{7,6},{8,7},{9,8},{10,9},{11,1... | collective-permute-start | bytes 16424 | tf_op jit(solution)/shard_map/ppermute | solution.py:43
  112.6 2.3 %collective-permute-start.18 = (f32[19,1,16,128]{3,0,2,1:T(8,128)S(1)}, f32[19,1,16,128]{3,0,2,1:T(8,128)S(1)}, u32[]{:S(2)}, u32[]{:S(2)}) collective-permute-start(f32[19,1,16,128]{3,0,2,1:T(8,128)S(1)} %get-tuple-element.180), channel_id=1, source_target_pairs={{128,0},{256,128},{384,256},{0,384},{129,1},{257,129},{385,257},{1... | collective-permute-start | bytes 466952 | tf_op jit(solution)/shard_map/ppermute | solution.py:43
  115.0 3.5 %collective-permute-start.19 = (f32[19,1,16,128]{3,0,2,1:T(8,128)S(1)}, f32[19,1,16,128]{3,0,2,1:T(8,128)S(1)}, u32[]{:S(2)}, u32[]{:S(2)}) collective-permute-start(f32[19,1,16,128]{3,0,2,1:T(8,128)S(1)} %get-tuple-element.179), channel_id=1, source_target_pairs={{0,128},{128,256},{256,384},{384,0},{1,129},{129,257},{257,385},{3... | collective-permute-start | bytes 466952 | tf_op jit(solution)/shard_map/ppermute | solution.py:42
  120.2 3.5 %collective-permute-done.19 = f32[19,1,16,128]{3,0,2,1:T(8,128)S(1)} collective-permute-done((f32[19,1,16,128]{3,0,2,1:T(8,128)S(1)}, f32[19,1,16,128]{3,0,2,1:T(8,128)S(1)}, u32[]{:S(2)}, u32[]{:S(2)}) %collective-permute-start.19) | collective-permute-done | bytes 155680 | tf_op jit(solution)/shard_map/ppermute | solution.py:42
  123.7 5.1 %collective-permute-start.20 = (f32[19,4,1,128]{3,0,2,1:T(8,128)S(1)}, f32[19,4,1,128]{3,0,2,1:T(8,128)S(1)}, u32[]{:S(2)}, u32[]{:S(2)}) collective-permute-start(f32[19,4,1,128]{3,0,2,1:T(8,128)S(1)} %get-tuple-element.126), channel_id=1, source_target_pairs={{32,0},{64,32},{96,64},{0,96},{33,1},{65,33},{97,65},{1,97},{34,2}... | collective-permute-start | bytes 116744 | tf_op jit(solution)/shard_map/ppermute | solution.py:43
  128.9 2.1 %collective-permute-start.21 = (f32[19,4,1,128]{3,0,2,1:T(8,128)S(1)}, f32[19,4,1,128]{3,0,2,1:T(8,128)S(1)}, u32[]{:S(2)}, u32[]{:S(2)}) collective-permute-start(f32[19,4,1,128]{3,0,2,1:T(8,128)S(1)} %get-tuple-element.125), channel_id=1, source_target_pairs={{0,32},{32,64},{64,96},{96,0},{1,33},{33,65},{65,97},{97,1},{2,34}... | collective-permute-start | bytes 116744 | tf_op jit(solution)/shard_map/ppermute | solution.py:42
  131.0 3.8 %collective-permute-done.21 = f32[19,4,1,128]{3,0,2,1:T(8,128)S(1)} collective-permute-done((f32[19,4,1,128]{3,0,2,1:T(8,128)S(1)}, f32[19,4,1,128]{3,0,2,1:T(8,128)S(1)}, u32[]{:S(2)}, u32[]{:S(2)}) %collective-permute-start.21) | collective-permute-done | bytes 38944 | tf_op jit(solution)/shard_map/ppermute | solution.py:42
  138.5 2.4 %collective-permute-done.23 = f32[19,4,18,1]{0,1,3,2:T(4,128)S(1)} collective-permute-done((f32[19,4,18,1]{0,1,3,2:T(4,128)S(1)}, f32[19,4,18,1]{0,1,3,2:T(4,128)S(1)}, u32[]{:S(2)}, u32[]{:S(2)}) %collective-permute-start.23) | collective-permute-done | bytes 5504 | tf_op jit(solution)/shard_map/ppermute | solution.py:42
  148.6 3.9 %collective-permute-start.25 = (f32[19,1,16,128]{3,0,2,1:T(8,128)S(1)}, f32[19,1,16,128]{3,0,2,1:T(8,128)S(1)}, u32[]{:S(2)}, u32[]{:S(2)}) collective-permute-start(f32[19,1,16,128]{3,0,2,1:T(8,128)S(1)} %get-tuple-element.157), channel_id=1, source_target_pairs={{0,128},{128,256},{256,384},{384,0},{1,129},{129,257},{257,385},{3... | collective-permute-start | bytes 466952 | tf_op jit(solution)/shard_map/ppermute | solution.py:42
  154.2 3.1 %collective-permute-done.25 = f32[19,1,16,128]{3,0,2,1:T(8,128)S(1)} collective-permute-done((f32[19,1,16,128]{3,0,2,1:T(8,128)S(1)}, f32[19,1,16,128]{3,0,2,1:T(8,128)S(1)}, u32[]{:S(2)}, u32[]{:S(2)}) %collective-permute-start.25) | collective-permute-done | bytes 155680 | tf_op jit(solution)/shard_map/ppermute | solution.py:42
  157.4 3.1 %collective-permute-start.26 = (f32[19,4,1,128]{3,0,2,1:T(8,128)S(1)}, f32[19,4,1,128]{3,0,2,1:T(8,128)S(1)}, u32[]{:S(2)}, u32[]{:S(2)}) collective-permute-start(f32[19,4,1,128]{3,0,2,1:T(8,128)S(1)} %get-tuple-element.123), channel_id=1, source_target_pairs={{32,0},{64,32},{96,64},{0,96},{33,1},{65,33},{97,65},{1,97},{34,2}... | collective-permute-start | bytes 116744 | tf_op jit(solution)/shard_map/ppermute | solution.py:43
  160.5 2.7 %collective-permute-start.27 = (f32[19,4,1,128]{3,0,2,1:T(8,128)S(1)}, f32[19,4,1,128]{3,0,2,1:T(8,128)S(1)}, u32[]{:S(2)}, u32[]{:S(2)}) collective-permute-start(f32[19,4,1,128]{3,0,2,1:T(8,128)S(1)} %get-tuple-element.122), channel_id=1, source_target_pairs={{0,32},{32,64},{64,96},{96,0},{1,33},{33,65},{65,97},{97,1},{2,34}... | collective-permute-start | bytes 116744 | tf_op jit(solution)/shard_map/ppermute | solution.py:42
  163.3 3.1 %collective-permute-done.27 = f32[19,4,1,128]{3,0,2,1:T(8,128)S(1)} collective-permute-done((f32[19,4,1,128]{3,0,2,1:T(8,128)S(1)}, f32[19,4,1,128]{3,0,2,1:T(8,128)S(1)}, u32[]{:S(2)}, u32[]{:S(2)}) %collective-permute-start.27) | collective-permute-done | bytes 38944 | tf_op jit(solution)/shard_map/ppermute | solution.py:42
  170.1 2.4 %collective-permute-done.29 = f32[19,4,18,1]{0,1,3,2:T(4,128)S(1)} collective-permute-done((f32[19,4,18,1]{0,1,3,2:T(4,128)S(1)}, f32[19,4,18,1]{0,1,3,2:T(4,128)S(1)}, u32[]{:S(2)}, u32[]{:S(2)}) %collective-permute-start.29) | collective-permute-done | bytes 5504 | tf_op jit(solution)/shard_map/ppermute | solution.py:42
  (263 shorter events, 74.1 us)
Async XLA Ops:
  7.1 14.7 %collective-permute-start.7 = (f32[19,1,16,128]{3,0,2,1:T(8,128)S(1)}, f32[19,1,16,128]{3,0,2,1:T(8,128)S(1)}, u32[]{:S(2)}, u32[]{:S(2)}) collective-permute-start(f32[19,1,16,128]{3,0,2,1:T(8,128)S(1)} %get-tuple-element.185), channel_id=1, source_target_pairs={{128,0},{256,128},{384,256},{0,384},{129,1},{257,129},{385,257},{1... | collective-permute-start | bytes 466952 | tf_op jit(solution)/shard_map/ppermute | solution.py:43
  11.9 10.9 %collective-permute-start.6 = (f32[19,1,16,128]{3,0,2,1:T(8,128)S(1)}, f32[19,1,16,128]{3,0,2,1:T(8,128)S(1)}, u32[]{:S(2)}, u32[]{:S(2)}) collective-permute-start(f32[19,1,16,128]{3,0,2,1:T(8,128)S(1)} %get-tuple-element.184), channel_id=1, source_target_pairs={{0,128},{128,256},{256,384},{384,0},{1,129},{129,257},{257,385},{3... | collective-permute-start | bytes 466952 | tf_op jit(solution)/shard_map/ppermute | solution.py:42
  14.1 16.6 %collective-permute-start.1 = (f32[19,1,16,128]{3,0,2,1:T(8,128)S(1)}, f32[19,1,16,128]{3,0,2,1:T(8,128)S(1)}, u32[]{:S(2)}, u32[]{:S(2)}) collective-permute-start(f32[19,1,16,128]{3,0,2,1:T(8,128)S(1)} %get-tuple-element.206), channel_id=1, source_target_pairs={{0,128},{128,256},{256,384},{384,0},{1,129},{129,257},{257,385},{3... | collective-permute-start | bytes 466952 | tf_op jit(solution)/shard_map/ppermute | solution.py:42
  16.7 14.9 %collective-permute-start = (f32[19,1,16,128]{3,0,2,1:T(8,128)S(1)}, f32[19,1,16,128]{3,0,2,1:T(8,128)S(1)}, u32[]{:S(2)}, u32[]{:S(2)}) collective-permute-start(f32[19,1,16,128]{3,0,2,1:T(8,128)S(1)} %get-tuple-element.207), channel_id=1, source_target_pairs={{128,0},{256,128},{384,256},{0,384},{129,1},{257,129},{385,257},{1... | collective-permute-start | bytes 466952 | tf_op jit(solution)/shard_map/ppermute | solution.py:43
  22.8 16.0 %copy-start.2 = (f32[19,1,16,128]{3,0,2,1:T(8,128)}, f32[19,1,16,128]{3,0,2,1:T(8,128)S(1)}, u32[]{:S(2)}) copy-start(f32[19,1,16,128]{3,0,2,1:T(8,128)S(1)} %collective-permute-done.6) | copy-start | bytes 466948
  22.8 15.9 %collective-permute-start.9 = (f32[19,4,1,128]{3,0,2,1:T(8,128)S(1)}, f32[19,4,1,128]{3,0,2,1:T(8,128)S(1)}, u32[]{:S(2)}, u32[]{:S(2)}) collective-permute-start(f32[19,4,1,128]{3,0,2,1:T(8,128)S(1)} %get-tuple-element.130), channel_id=1, source_target_pairs={{32,0},{64,32},{96,64},{0,96},{33,1},{65,33},{97,65},{1,97},{34,2}... | collective-permute-start | bytes 116744 | tf_op jit(solution)/shard_map/ppermute | solution.py:43
  28.8 10.0 %collective-permute-start.8 = (f32[19,4,1,128]{3,0,2,1:T(8,128)S(1)}, f32[19,4,1,128]{3,0,2,1:T(8,128)S(1)}, u32[]{:S(2)}, u32[]{:S(2)}) collective-permute-start(f32[19,4,1,128]{3,0,2,1:T(8,128)S(1)} %get-tuple-element.129), channel_id=1, source_target_pairs={{0,32},{32,64},{64,96},{96,0},{1,33},{33,65},{65,97},{97,1},{2,34}... | collective-permute-start | bytes 116744 | tf_op jit(solution)/shard_map/ppermute | solution.py:42
  32.9 13.6 %collective-permute-start.2 = (f32[19,4,1,128]{3,0,2,1:T(8,128)}, f32[19,4,1,128]{3,0,2,1:T(8,128)}, u32[]{:S(2)}, u32[]{:S(2)}) collective-permute-start(f32[19,4,1,128]{3,0,2,1:T(8,128)} %get-tuple-element.132), channel_id=1, source_target_pairs={{32,0},{64,32},{96,64},{0,96},{33,1},{65,33},{97,65},{1,97},{34,2}... | collective-permute-start | bytes 116744 | tf_op jit(solution)/shard_map/ppermute | solution.py:43
  36.8 9.7 %collective-permute-start.3 = (f32[19,4,1,128]{3,0,2,1:T(8,128)}, f32[19,4,1,128]{3,0,2,1:T(8,128)}, u32[]{:S(2)}, u32[]{:S(2)}) collective-permute-start(f32[19,4,1,128]{3,0,2,1:T(8,128)} %get-tuple-element.131), channel_id=1, source_target_pairs={{0,32},{32,64},{64,96},{96,0},{1,33},{33,65},{65,97},{97,1},{2,34}... | collective-permute-start | bytes 116744 | tf_op jit(solution)/shard_map/ppermute | solution.py:42
  41.5 12.2 %collective-permute-start.10 = (f32[19,4,18,1]{0,1,3,2:T(4,128)}, f32[19,4,18,1]{0,1,3,2:T(4,128)}, u32[]{:S(2)}, u32[]{:S(2)}) collective-permute-start(f32[19,4,18,1]{0,1,3,2:T(4,128)} %copy.77), channel_id=1, source_target_pairs={{0,1},{1,2},{2,3},{3,4},{4,5},{5,6},{6,7},{7,8},{8,9},{9,10},{10,1... | collective-permute-start | bytes 16424 | tf_op jit(solution)/shard_map/ppermute | solution.py:42
  42.6 12.4 %collective-permute-start.11 = (f32[19,4,18,1]{0,1,3,2:T(4,128)}, f32[19,4,18,1]{0,1,3,2:T(4,128)}, u32[]{:S(2)}, u32[]{:S(2)}) collective-permute-start(f32[19,4,18,1]{0,1,3,2:T(4,128)} %copy.79), channel_id=1, source_target_pairs={{1,0},{2,1},{3,2},{4,3},{5,4},{6,5},{7,6},{8,7},{9,8},{10,9},{11,1... | collective-permute-start | bytes 16424 | tf_op jit(solution)/shard_map/ppermute | solution.py:43
  48.8 24.8 %collective-permute-start.4 = (f32[19,4,18,1]{0,1,3,2:T(4,128)}, f32[19,4,18,1]{0,1,3,2:T(4,128)}, u32[]{:S(2)}, u32[]{:S(2)}) collective-permute-start(f32[19,4,18,1]{0,1,3,2:T(4,128)} %copy.50), channel_id=1, source_target_pairs={{1,0},{2,1},{3,2},{4,3},{5,4},{6,5},{7,6},{8,7},{9,8},{10,9},{11,1... | collective-permute-start | bytes 16424 | tf_op jit(solution)/shard_map/ppermute | solution.py:43
  53.7 21.3 %collective-permute-start.5 = (f32[19,4,18,1]{0,1,3,2:T(4,128)}, f32[19,4,18,1]{0,1,3,2:T(4,128)}, u32[]{:S(2)}, u32[]{:S(2)}) collective-permute-start(f32[19,4,18,1]{0,1,3,2:T(4,128)} %copy.52), channel_id=1, source_target_pairs={{0,1},{1,2},{2,3},{3,4},{4,5},{5,6},{6,7},{7,8},{8,9},{9,10},{10,1... | collective-permute-start | bytes 16424 | tf_op jit(solution)/shard_map/ppermute | solution.py:42
  67.1 10.2 %collective-permute-start.12 = (f32[19,1,16,128]{3,0,2,1:T(8,128)}, f32[19,1,16,128]{3,0,2,1:T(8,128)S(1)}, u32[]{:S(2)}, u32[]{:S(2)}) collective-permute-start(f32[19,1,16,128]{3,0,2,1:T(8,128)} %get-tuple-element.183), channel_id=1, source_target_pairs={{128,0},{256,128},{384,256},{0,384},{129,1},{257,129},{385,257},{1... | collective-permute-start | bytes 466952 | tf_op jit(solution)/shard_map/ppermute | solution.py:43
  70.0 9.1 %collective-permute-start.13 = (f32[19,1,16,128]{3,0,2,1:T(8,128)}, f32[19,1,16,128]{3,0,2,1:T(8,128)}, u32[]{:S(2)}, u32[]{:S(2)}) collective-permute-start(f32[19,1,16,128]{3,0,2,1:T(8,128)} %get-tuple-element.182), channel_id=1, source_target_pairs={{0,128},{128,256},{256,384},{384,0},{1,129},{129,257},{257,385},{3... | collective-permute-start | bytes 466952 | tf_op jit(solution)/shard_map/ppermute | solution.py:42
  79.8 7.7 %collective-permute-start.14 = (f32[19,4,1,128]{3,0,2,1:T(8,128)S(1)}, f32[19,4,1,128]{3,0,2,1:T(8,128)S(1)}, u32[]{:S(2)}, u32[]{:S(2)}) collective-permute-start(f32[19,4,1,128]{3,0,2,1:T(8,128)S(1)} %get-tuple-element.128), channel_id=1, source_target_pairs={{32,0},{64,32},{96,64},{0,96},{33,1},{65,33},{97,65},{1,97},{34,2}... | collective-permute-start | bytes 116744 | tf_op jit(solution)/shard_map/ppermute | solution.py:43
  84.4 7.2 %collective-permute-start.15 = (f32[19,4,1,128]{3,0,2,1:T(8,128)S(1)}, f32[19,4,1,128]{3,0,2,1:T(8,128)S(1)}, u32[]{:S(2)}, u32[]{:S(2)}) collective-permute-start(f32[19,4,1,128]{3,0,2,1:T(8,128)S(1)} %get-tuple-element.127), channel_id=1, source_target_pairs={{0,32},{32,64},{64,96},{96,0},{1,33},{33,65},{65,97},{97,1},{2,34}... | collective-permute-start | bytes 116744 | tf_op jit(solution)/shard_map/ppermute | solution.py:42
  96.1 6.5 %collective-permute-start.17 = (f32[19,4,18,1]{0,1,3,2:T(4,128)}, f32[19,4,18,1]{0,1,3,2:T(4,128)}, u32[]{:S(2)}, u32[]{:S(2)}) collective-permute-start(f32[19,4,18,1]{0,1,3,2:T(4,128)} %copy.83), channel_id=1, source_target_pairs={{0,1},{1,2},{2,3},{3,4},{4,5},{5,6},{6,7},{7,8},{8,9},{9,10},{10,1... | collective-permute-start | bytes 16424 | tf_op jit(solution)/shard_map/ppermute | solution.py:42
  97.2 6.7 %collective-permute-start.16 = (f32[19,4,18,1]{0,1,3,2:T(4,128)}, f32[19,4,18,1]{0,1,3,2:T(4,128)S(1)}, u32[]{:S(2)}, u32[]{:S(2)}) collective-permute-start(f32[19,4,18,1]{0,1,3,2:T(4,128)} %copy.81), channel_id=1, source_target_pairs={{1,0},{2,1},{3,2},{4,3},{5,4},{6,5},{7,6},{8,7},{9,8},{10,9},{11,1... | collective-permute-start | bytes 16424 | tf_op jit(solution)/shard_map/ppermute | solution.py:43
  112.6 7.6 %collective-permute-start.18 = (f32[19,1,16,128]{3,0,2,1:T(8,128)S(1)}, f32[19,1,16,128]{3,0,2,1:T(8,128)S(1)}, u32[]{:S(2)}, u32[]{:S(2)}) collective-permute-start(f32[19,1,16,128]{3,0,2,1:T(8,128)S(1)} %get-tuple-element.180), channel_id=1, source_target_pairs={{128,0},{256,128},{384,256},{0,384},{129,1},{257,129},{385,257},{1... | collective-permute-start | bytes 466952 | tf_op jit(solution)/shard_map/ppermute | solution.py:43
  115.0 8.8 %collective-permute-start.19 = (f32[19,1,16,128]{3,0,2,1:T(8,128)S(1)}, f32[19,1,16,128]{3,0,2,1:T(8,128)S(1)}, u32[]{:S(2)}, u32[]{:S(2)}) collective-permute-start(f32[19,1,16,128]{3,0,2,1:T(8,128)S(1)} %get-tuple-element.179), channel_id=1, source_target_pairs={{0,128},{128,256},{256,384},{384,0},{1,129},{129,257},{257,385},{3... | collective-permute-start | bytes 466952 | tf_op jit(solution)/shard_map/ppermute | solution.py:42
  123.7 7.3 %collective-permute-start.20 = (f32[19,4,1,128]{3,0,2,1:T(8,128)S(1)}, f32[19,4,1,128]{3,0,2,1:T(8,128)S(1)}, u32[]{:S(2)}, u32[]{:S(2)}) collective-permute-start(f32[19,4,1,128]{3,0,2,1:T(8,128)S(1)} %get-tuple-element.126), channel_id=1, source_target_pairs={{32,0},{64,32},{96,64},{0,96},{33,1},{65,33},{97,65},{1,97},{34,2}... | collective-permute-start | bytes 116744 | tf_op jit(solution)/shard_map/ppermute | solution.py:43
  128.9 6.0 %collective-permute-start.21 = (f32[19,4,1,128]{3,0,2,1:T(8,128)S(1)}, f32[19,4,1,128]{3,0,2,1:T(8,128)S(1)}, u32[]{:S(2)}, u32[]{:S(2)}) collective-permute-start(f32[19,4,1,128]{3,0,2,1:T(8,128)S(1)} %get-tuple-element.125), channel_id=1, source_target_pairs={{0,32},{32,64},{64,96},{96,0},{1,33},{33,65},{65,97},{97,1},{2,34}... | collective-permute-start | bytes 116744 | tf_op jit(solution)/shard_map/ppermute | solution.py:42
  135.8 1.6 collective-permute-start.22
  136.3 4.6 %collective-permute-start.23 = (f32[19,4,18,1]{0,1,3,2:T(4,128)S(1)}, f32[19,4,18,1]{0,1,3,2:T(4,128)S(1)}, u32[]{:S(2)}, u32[]{:S(2)}) collective-permute-start(f32[19,4,18,1]{0,1,3,2:T(4,128)S(1)} %copy.87), channel_id=1, source_target_pairs={{0,1},{1,2},{2,3},{3,4},{4,5},{5,6},{6,7},{7,8},{8,9},{9,10},{10,1... | collective-permute-start | bytes 16424 | tf_op jit(solution)/shard_map/ppermute | solution.py:42
  146.6 7.6 %collective-permute-start.24 = (f32[19,1,16,128]{3,0,2,1:T(8,128)S(1)}, f32[19,1,16,128]{3,0,2,1:T(8,128)S(1)}, u32[]{:S(2)}, u32[]{:S(2)}) collective-permute-start(f32[19,1,16,128]{3,0,2,1:T(8,128)S(1)} %get-tuple-element.158), channel_id=1, source_target_pairs={{128,0},{256,128},{384,256},{0,384},{129,1},{257,129},{385,257},{1... | collective-permute-start | bytes 466952 | tf_op jit(solution)/shard_map/ppermute | solution.py:43
  148.6 14.7 %copy-start.39 = (f32[2,16,128]{2,1,0:T(8,128)S(1)}, f32[2,16,128]{2,1,0:T(8,128)}, u32[]{:S(2)}) copy-start(f32[2,16,128]{2,1,0:T(8,128)} %copy-done.38) | copy-start | bytes 49156
  148.6 8.8 %collective-permute-start.25 = (f32[19,1,16,128]{3,0,2,1:T(8,128)S(1)}, f32[19,1,16,128]{3,0,2,1:T(8,128)S(1)}, u32[]{:S(2)}, u32[]{:S(2)}) collective-permute-start(f32[19,1,16,128]{3,0,2,1:T(8,128)S(1)} %get-tuple-element.157), channel_id=1, source_target_pairs={{0,128},{128,256},{256,384},{384,0},{1,129},{129,257},{257,385},{3... | collective-permute-start | bytes 466952 | tf_op jit(solution)/shard_map/ppermute | solution.py:42
  157.4 6.0 %collective-permute-start.26 = (f32[19,4,1,128]{3,0,2,1:T(8,128)S(1)}, f32[19,4,1,128]{3,0,2,1:T(8,128)S(1)}, u32[]{:S(2)}, u32[]{:S(2)}) collective-permute-start(f32[19,4,1,128]{3,0,2,1:T(8,128)S(1)} %get-tuple-element.123), channel_id=1, source_target_pairs={{32,0},{64,32},{96,64},{0,96},{33,1},{65,33},{97,65},{1,97},{34,2}... | collective-permute-start | bytes 116744 | tf_op jit(solution)/shard_map/ppermute | solution.py:43
  160.5 6.0 %collective-permute-start.27 = (f32[19,4,1,128]{3,0,2,1:T(8,128)S(1)}, f32[19,4,1,128]{3,0,2,1:T(8,128)S(1)}, u32[]{:S(2)}, u32[]{:S(2)}) collective-permute-start(f32[19,4,1,128]{3,0,2,1:T(8,128)S(1)} %get-tuple-element.122), channel_id=1, source_target_pairs={{0,32},{32,64},{64,96},{96,0},{1,33},{33,65},{65,97},{97,1},{2,34}... | collective-permute-start | bytes 116744 | tf_op jit(solution)/shard_map/ppermute | solution.py:42
  167.4 1.6 collective-permute-start.28
  167.9 4.6 %collective-permute-start.29 = (f32[19,4,18,1]{0,1,3,2:T(4,128)S(1)}, f32[19,4,18,1]{0,1,3,2:T(4,128)S(1)}, u32[]{:S(2)}, u32[]{:S(2)}) collective-permute-start(f32[19,4,18,1]{0,1,3,2:T(4,128)S(1)} %copy.91), channel_id=1, source_target_pairs={{0,1},{1,2},{2,3},{3,4},{4,5},{5,6},{6,7},{7,8},{8,9},{9,10},{10,1... | collective-permute-start | bytes 16424 | tf_op jit(solution)/shard_map/ppermute | solution.py:42
  (64 other events, 114.8 us)
where the time goes:
time: 182 us; the launch traced here: 180 us
  starting transfers between devices  76.3 us (42%)
  local copies, waits for them, and re-layouts  46.1 us (25%)
  waiting for transfers between devices  30 us (16%)
  other arithmetic  15.6 us (9%)
  matrix products  9.69 us (5%)
  between operations  1.92 us (1%)
    ppermute x15, starting transfers between devices, extended(): after = lax.ppermute(leading, axis, down)  49.5 us
    ppermute x15, starting transfers between devices, extended(): before = lax.ppermute(last, axis, up)  26.8 us
    ppermute x15, waiting for transfers between devices, extended(): before = lax.ppermute(last, axis, up)  25.4 us
    unnamed x134, local copies, waits for them, and re-layouts  14 us
    slice x14, local copies, waits for them, and re-layouts, extended(): last = lax.slice_in_dim(shard, length - width, length, axis=dim)  8.01 us
    concatenate x18, other arithmetic, extended(): shard = jnp.concatenate([before, shard, after], axis=dim)  7.55 us
    slice x7, local copies, waits for them, and re-layouts, extended(): leading = lax.slice_in_dim(shard, 0, width, axis=dim)  5.98 us
    dot_general x7, matrix products, relax_collision(): jnp.tensordot(vel_table, velocity, axes=1, precision=lax.Precision.HIGHEST)  5.32 us
  transfers between devices with their start and end apart: 30, of which 14 were waited for; matrix products, arithmetic and copies ran while one was open for 17% of the time, Pallas kernels for 0%

commit v1 on v0

v1 whole, which is shorter than its diff:
```python
import jax
import jax.numpy as jnp
from jax import lax
from jax.experimental import pallas as pl
from jax.experimental.pallas import tpu as pltpu
from jax.sharding import PartitionSpec as P

INTERPRET = False

VEL = [
    (0, 0, 0),
    (1, 0, 0), (-1, 0, 0), (0, 1, 0), (0, -1, 0), (0, 0, 1), (0, 0, -1),
    (1, 1, 0), (-1, -1, 0), (1, -1, 0), (-1, 1, 0),
    (1, 0, 1), (-1, 0, -1), (1, 0, -1), (-1, 0, 1),
    (0, 1, 1), (0, -1, -1), (0, 1, -1), (0, -1, 1),
]
OPP = [0, 2, 1, 4, 3, 6, 5, 8, 7, 10, 9, 12, 11, 14, 13, 16, 15, 18, 17]
WEIGHT = [1.0 / 3.0] + [1.0 / 18.0] * 6 + [1.0 / 36.0] * 12
OMEGA = 1.25
Q = 19
XP = [i for i in range(Q) if VEL[i][0] == 1]
X0 = [i for i in range(Q) if VEL[i][0] == 0]
XM = [i for i in range(Q) if VEL[i][0] == -1]
PAIRS = [i for i in range(1, Q, 2)]

ROWS, OWN, LANES, RIM = 24, 16, 128, 4
FIELDS = 2 * Q + 1
ZTILES = -(-2 * FIELDS // 32)


def total(terms):
    terms = list(terms)
    while len(terms) > 1:
        terms = [a + b for a, b in zip(terms[::2], terms[1::2])] + (terms[-1:] if len(terms) % 2 else [])
    return terms[0]


def signed(values, axis):
    plus = total(values[i] for i in range(Q) if VEL[i][axis] == 1)
    minus = total(values[i] for i in range(Q) if VEL[i][axis] == -1)
    return plus - minus


def project(vector, i):
    out = None
    for axis in range(3):
        c = VEL[i][axis]
        if c == 0:
            continue
        if out is None:
            out = vector[axis] if c == 1 else -vector[axis]
        else:
            out = out + vector[axis] if c == 1 else out - vector[axis]
    return out


def moments(f):
    rho = total(f)
    inv = 1.0 / rho
    return rho, [signed(f, axis) * inv for axis in range(3)]


def collide(f, rho, u, blocking, want):
    keep = 1.0 - blocking
    own = (1.0 - OMEGA) * keep
    scale = OMEGA * keep * rho
    base = 1.0 - 1.5 * (u[0] * u[0] + u[1] * u[1] + u[2] * u[2])
    out = {}
    if 0 in want:
        out[0] = (own + blocking) * f[0] + (WEIGHT[0] * scale) * base
    for i in PAIRS:
        j = i + 1
        if i not in want and j not in want:
            continue
        s = WEIGHT[i] * scale
        p = project(u, i)
        even = s * (base + 4.5 * (p * p))
        odd = s * (3.0 * p)
        if i in want:
            out[i] = own * f[i] + blocking * f[j] + (even + odd)
        if j in want:
            out[j] = own * f[j] + blocking * f[i] + (even - odd)
    return out


def adjoint(b, u, blocking, want, f=None, rho=None):
    keep = 1.0 - blocking
    own = (1.0 - OMEGA) * keep
    mix = OMEGA * keep
    base = 1.0 - 1.5 * (u[0] * u[0] + u[1] * u[1] + u[2] * u[2])
    sums = {i: b[i] + b[i + 1] for i in PAIRS}
    diffs = {i: b[i] - b[i + 1] for i in PAIRS}
    weighted = total(
        [WEIGHT[0] * b[0], WEIGHT[1] * total(sums[i] for i in PAIRS[:3]), WEIGHT[7] * total(sums[i] for i in PAIRS[3:])]
    )
    value = []
    slope = [[], [], []]
    for i in PAIRS:
        p = project(u, i)
        ps = p * sums[i]
        d3 = 3.0 * diffs[i]
        value.append((WEIGHT[i] * p) * (d3 + 4.5 * ps))
        g = WEIGHT[i] * (d3 + 9.0 * ps)
        for axis in range(3):
            if VEL[i][axis]:
                slope[axis].append(g if VEL[i][axis] == 1 else -g)
    energy = base * weighted + total(value)
    v = [total(slope[axis]) - 3.0 * (u[axis] * weighted) for axis in range(3)]
    common = mix * (energy - (v[0] * u[0] + v[1] * u[1] + v[2] * u[2]))
    mv = [mix * v[axis] for axis in range(3)]
    out = {}
    if 0 in want:
        out[0] = (own + blocking) * b[0] + common
    for i in PAIRS:
        j = i + 1
        if i not in want and j not in want:
            continue
        p = project(mv, i)
        if i in want:
            out[i] = own * b[i] + blocking * b[j] + (common + p)
        if j in want:
            out[j] = own * b[j] + blocking * b[i] + (common - p)
    if f is None:
        return out
    part = total(b[i] * (f[OPP[i]] - (1.0 - OMEGA) * f[i]) for i in range(Q))
    return out, part - (OMEGA * rho) * energy


def column(shape):
    return lax.broadcasted_iota(jnp.int32, shape, len(shape) - 1)


def turn(tile, shift, axis):
    shift = shift % tile.shape[axis]
    return tile if shift == 0 else pltpu.roll(tile, shift, axis)


def moved(main, rim, i, sign):
    y, z = sign * VEL[i][1], sign * VEL[i][2]
    if y:
        main, rim = turn(main, y, 0), turn(rim, y, 0)
    if z:
        at = column(main.shape)
        edge = at == (0 if z == 1 else LANES - 1)
        main, rim = turn(main, z, 1), turn(rim, z, 1)
        main, rim = jnp.where(edge, rim, main), jnp.where(edge, main, rim)
    return main, rim


def pack(ref, tiles):
    n = len(tiles)
    at = column((ROWS, LANES)) // 8
    for k, (main, _) in enumerate(tiles):
        ref[k] = main()
    for first in range(0, n, 16):
        joined = None
        for k in range(first, min(first + 16, n)):
            piece = turn(tiles[k][1](), 8 * (k - first) + 4, 1)
            joined = piece if joined is None else jnp.where(at == k - first, piece, joined)
        ref[n + first // 16] = joined


def unpack(ref, n, k):
    return ref[k], turn(ref[n + k // 16], -(8 * (k % 16) + 4), 1)


def packed(n):
    return n + -(-n // 16)


UP1 = [("g", 0, i) for i in XP] + [("g", 1, i) for i in XP] + [("g", 1, i) for i in X0] + [("s", 1, i) for i in XM] + [("b", 1, 0)]
DOWN1 = [("g", 1, i) for i in XM] + [("g", 0, i) for i in XM] + [("g", 0, i) for i in X0] + [("s", 0, i) for i in XP] + [("b", 0, 0)]
UP2 = [("a", 0, i) for i in XM] + [("a", 1, i) for i in X0] + [("a", 1, i) for i in XM]
DOWN2 = [("a", 1, i) for i in XP] + [("a", 0, i) for i in X0] + [("a", 0, i) for i in XP]
FROM1 = {(kind, layer - 2, i): ("l", k) for k, (kind, layer, i) in enumerate(UP1)}
FROM1.update({(kind, layer + 2, i): ("r", k) for k, (kind, layer, i) in enumerate(DOWN1)})
FROM2 = {(kind, layer - 2, i): ("l", k) for k, (kind, layer, i) in enumerate(UP2)}
FROM2.update({(kind, layer + 2, i): ("r", k) for k, (kind, layer, i) in enumerate(DOWN2)})


def call(kernel, outs, scratch=()):
    return pl.pallas_call(
        kernel,
        out_shape=[jax.ShapeDtypeStruct(shape, jnp.float32) for shape in outs],
        scratch_shapes=[pltpu.VMEM(shape, jnp.float32) for shape in scratch],
        compiler_params=None if INTERPRET else pltpu.CompilerParams(vmem_limit_bytes=40 * 2**20),
        interpret=INTERPRET,
    )


def rows_kernel(f_ref, por_ref, solid_ref, seed_ref, up_ref, down_ref):
    for k in range(FIELDS):
        for layer in range(2):
            if k < Q:
                low, high = f_ref[k, layer, 0:4, :], f_ref[k, layer, 12:16, :]
            elif k < 2 * Q:
                low, high = seed_ref[k - Q, layer, 0:4, :], seed_ref[k - Q, layer, 12:16, :]
            else:
                blocking = jnp.where(solid_ref[layer] == 1, 1.0, por_ref[layer])
                low, high = blocking[0:4], blocking[12:16]
            up_ref[k, 4 * layer : 4 * layer + 4, :] = high
            down_ref[k, 4 * layer : 4 * layer + 4, :] = low


def columns_kernel(f_ref, por_ref, solid_ref, seed_ref, below_ref, above_ref, main_ref, up_ref, down_ref):
    at = column((ROWS, LANES)) // 4
    high = low = None
    for k in range(FIELDS):
        for layer in range(2):
            if k < Q:
                own = f_ref[k, layer]
            elif k < 2 * Q:
                own = seed_ref[k - Q, layer]
            else:
                own = jnp.where(solid_ref[layer] == 1, 1.0, por_ref[layer])
            rows = slice(4 * layer, 4 * layer + 4)
            tile = jnp.concatenate([own, above_ref[k, rows, :], below_ref[k, rows, :]], axis=0)
            main_ref[k, layer] = tile
            slot = (2 * k + layer) % 32
            piece_up, piece_down = turn(tile, 4 * slot + 4, 1), turn(tile, 4 * slot, 1)
            high = piece_up if slot == 0 else jnp.where(at == slot, piece_up, high)
            low = piece_down if slot == 0 else jnp.where(at == slot, piece_down, low)
            if slot == 31 or 2 * k + layer == 2 * FIELDS - 1:
                up_ref[(2 * k + layer) // 32] = high
                down_ref[(2 * k + layer) // 32] = low


def tiles_loop(count, body):
    def step(n, carry):
        body(n // 3, pl.multiple_of((n % 3) * 8, 8))
        return carry

    lax.fori_loop(0, count, step, 0)


def first_kernel(main_ref, before_ref, beyond_ref, g_ref, s_ref, b_ref, up_ref, down_ref, f_scr):
    at = column((ROWS, LANES))
    for k in range(FIELDS):
        for layer in range(2):
            n = 2 * k + layer
            slot, tile = n % 32, n // 32
            before = turn(before_ref[tile], -(4 * slot + 4), 1)
            beyond = turn(beyond_ref[tile], -4 * slot, 1)
            rim = jnp.where(at < RIM, beyond, before)
            if k < Q:
                f_scr[k, layer, 0] = main_ref[k, layer]
                f_scr[k, layer, 1] = rim
            elif k < 2 * Q:
                s_ref[k - Q, layer, 0] = main_ref[k, layer]
                s_ref[k - Q, layer, 1] = rim
            else:
                b_ref[layer, 0] = main_ref[k, layer]
                b_ref[layer, 1] = rim

    for layer in range(2):

        def body(lane, row, layer=layer):
            f = [f_scr[i, layer, lane, pl.ds(row, 8), :] for i in range(Q)]
            rho, u = moments(f)
            g = collide(f, rho, u, b_ref[layer, lane, pl.ds(row, 8), :], range(Q))
            for i in range(Q):
                g_ref[i, layer, lane, pl.ds(row, 8), :] = g[i]

        tiles_loop(6, body)

    def tile(field):
        kind, layer, i = field
        if kind == "g":
            return (lambda: g_ref[i, layer, 0]), (lambda: g_ref[i, layer, 1])
        if kind == "s":
            return (lambda: s_ref[i, layer, 0]), (lambda: s_ref[i, layer, 1])
        return (lambda: b_ref[layer, 0]), (lambda: b_ref[layer, 1])

    pack(up_ref, [tile(field) for field in UP1])
    pack(down_ref, [tile(field) for field in DOWN1])


def middle_kernel(
    g_ref, s_ref, b_ref, left_ref, right_ref,
    a_ref, u_ref, b4_ref, f1_ref, grad_ref, up_ref, down_ref,
    f_scr, g_scr, adj_scr,
):
    def got(kind, x, i):
        if x in (0, 1):
            ref = {"g": g_ref, "s": s_ref}[kind]
            return ref[i, x, 0], ref[i, x, 1]
        side, k = FROM1[(kind, x, i)]
        return unpack(left_ref, len(UP1), k) if side == "l" else unpack(right_ref, len(DOWN1), k)

    for i in range(Q):
        for n in range(4):
            main, rim = moved(*got("g", n - 1 - VEL[i][0], i), i, 1)
            f_scr[i, n, 0] = main
            f_scr[i, n, 1] = rim
            if n in (1, 2):
                f1_ref[i, n - 1] = main[0:OWN]
    for n in range(4):
        if n in (1, 2):
            b4_ref[n, 0] = b_ref[n - 1, 0]
            b4_ref[n, 1] = b_ref[n - 1, 1]
        else:
            main, rim = got("b", n - 1, 0)
            b4_ref[n, 0] = main
            b4_ref[n, 1] = rim

    for n, want in ((0, XP), (1, range(Q)), (2, range(Q)), (3, XM)):

        def body(lane, row, n=n, want=want):
            f = [f_scr[i, n, lane, pl.ds(row, 8), :] for i in range(Q)]
            rho, u = moments(f)
            for axis in range(3):
                u_ref[axis, n, lane, pl.ds(row, 8), :] = u[axis]
            g = collide(f, rho, u, b4_ref[n, lane, pl.ds(row, 8), :], want)
            for i in want:
                g_scr[i, n, lane, pl.ds(row, 8), :] = g[i]

        tiles_loop(6, body)

    for i in range(Q):
        for layer in range(2):
            n = layer + 1 - VEL[i][0]
            main, rim = moved(g_scr[i, n, 0], g_scr[i, n, 1], i, 1)
            f_scr[i, layer, 0] = main
            f_scr[i, layer, 1] = rim
            main, rim = moved(*got("s", layer + VEL[i][0], i), i, -1)
            adj_scr[i, layer, 0] = main
            adj_scr[i, layer, 1] = rim

    for layer in range(2):

        def body(lane, row, layer=layer, first=0):
            f = [f_scr[i, layer, lane, pl.ds(row, 8), :] for i in range(Q)]
            b = [adj_scr[i, layer, lane, pl.ds(row, 8), :] for i in range(Q)]
            rho, u = moments(f)
            a, grad = adjoint(b, u, b_ref[layer, lane, pl.ds(row, 8), :], range(Q), f, rho)
            for i in range(Q):
                a_ref[i, layer, lane, pl.ds(row, 8), :] = a[i]
            grad_ref[layer, lane, pl.ds(row, 8), :] = grad

        tiles_loop(6, body)

    def tile(field):
        _, layer, i = field
        return (lambda: a_ref[i, layer, 0]), (lambda: a_ref[i, layer, 1])

    pack(up_ref, [tile(field) for field in UP2])
    pack(down_ref, [tile(field) for field in DOWN2])


def last_kernel(
    a_ref, u_ref, b4_ref, f1_ref, grad_ref, left_ref, right_ref, f_ref, solid_ref,
    out_grad_ref, out_ref,
    b_scr, a_scr,
):
    def got(x, i):
        if x in (0, 1):
            return a_ref[i, x, 0], a_ref[i, x, 1]
        side, k = FROM2[("a", x, i)]
        return unpack(left_ref, len(UP2), k) if side == "l" else unpack(right_ref, len(DOWN2), k)

    for i in range(Q):
        for n in range(4):
            main, rim = moved(*got(n - 1 + VEL[i][0], i), i, -1)
            b_scr[i, n, 0] = main
            b_scr[i, n, 1] = rim

    for n, want in ((0, XM), (1, range(Q)), (2, range(Q)), (3, XP)):

        def body(lane, row, n=n, want=want):
            b = [b_scr[i, n, lane, pl.ds(row, 8), :] for i in range(Q)]
            u = [u_ref[axis, n, lane, pl.ds(row, 8), :] for axis in range(3)]
            a = adjoint(b, u, b4_ref[n, lane, pl.ds(row, 8), :], want)
            for i in want:
                a_scr[i, n, lane, pl.ds(row, 8), :] = a[i]

        tiles_loop(6, body)

    def own(n, carry):
        layer, row = n // 2, pl.multiple_of((n % 2) * 8, 8)
        f = [f1_ref[i, layer, pl.ds(row, 8), :] for i in range(Q)]
        b = [b_scr[i, layer + 1, 0, pl.ds(row, 8), :] for i in range(Q)]
        rho, u = moments(f)
        _, grad = adjoint(b, u, b4_ref[layer + 1, 0, pl.ds(row, 8), :], (), f, rho)
        out_grad_ref[layer, pl.ds(row, 8), :] = grad + grad_ref[layer, 0, pl.ds(row, 8), :]
        return carry

    lax.fori_loop(0, 4, own, 0)

    for i in range(Q):
        for layer in range(2):
            n = layer + 1 + VEL[i][0]
            main, _ = moved(a_scr[i, n, 0], a_scr[i, n, 1], i, -1)
            b_scr[i, layer, 0] = main

    def final(n, carry):
        layer, row = n // 2, pl.multiple_of((n % 2) * 8, 8)
        f = [f_ref[i, layer, pl.ds(row, 8), :] for i in range(Q)]
        b = [b_scr[i, layer, 0, pl.ds(row, 8), :] for i in range(Q)]
        rho, u = moments(f)
        a, grad = adjoint(b, u, b4_ref[layer + 1, 0, pl.ds(row, 8), :], range(Q), f, rho)
        for i in range(Q):
            out_ref[i, layer, pl.ds(row, 8), :] = a[i]
        grad = grad + out_grad_ref[layer, pl.ds(row, 8), :]
        out_grad_ref[layer, pl.ds(row, 8), :] = jnp.where(solid_ref[layer, pl.ds(row, 8), :] == 1, 0.0, grad)
        return carry

    lax.fori_loop(0, 4, final, 0)


def both_ways(up, down, axis):
    count = lax.axis_size(axis)
    ring = [(i, (i + 1) % count) for i in range(count)]
    return lax.ppermute(up, axis, ring), lax.ppermute(down, axis, [(j, i) for i, j in ring])


def body(populations, porosity, solid, seed_adjoint):
    layer = (2, 2, ROWS, LANES)
    inputs = (populations, porosity, solid, seed_adjoint)
    up, down = call(rows_kernel, [(FIELDS, 8, LANES)] * 2)(*inputs)
    below, above = both_ways(up, down, "gy")
    main, up, down = call(columns_kernel, [(FIELDS, 2, ROWS, LANES)] + [(ZTILES, ROWS, LANES)] * 2)(*inputs, below, above)
    before, beyond = both_ways(up, down, "gz")
    g, s, b, up, down = call(
        first_kernel,
        [(Q,) + layer, (Q,) + layer, layer] + [(packed(len(UP1)), ROWS, LANES)] * 2,
        [(Q,) + layer],
    )(main, before, beyond)
    left, right = both_ways(up, down, "gx")
    wide = (4, 2, ROWS, LANES)
    a, u, b4, f1, grad, up, down = call(
        middle_kernel,
        [(Q,) + layer, (3,) + wide, wide, (Q, 2, OWN, LANES), layer] + [(packed(len(UP2)), ROWS, LANES)] * 2,
        [(Q,) + wide, (Q,) + wide, (Q,) + layer],
    )(g, s, b, left, right)
    left, right = both_ways(up, down, "gx")
    gradient, adjoint_out = call(
        last_kernel, [(2, OWN, LANES), (Q, 2, OWN, LANES)], [(Q,) + wide, (Q,) + wide]
    )(a, u, b4, f1, grad, left, right, populations, solid)
    return gradient, adjoint_out


def solution(mesh):
    field, cell = P(None, "gx", "gy", "gz"), P("gx", "gy", "gz")
    return jax.shard_map(
        body, mesh=mesh, in_specs=(field, cell, cell, field), out_specs=(cell, field), check_vma=False
    )
```

time: 182 us -> 59.3 us (0.33)
  the two profiles are of different devices: /device:TPU:8 before, /device:TPU:24 now
where the time goes in v1:
time: 59.3 us; the launch traced here: 58.6 us
  starting transfers between devices  26.5 us (45%)
  waiting for transfers between devices  17.9 us (30%)
  Pallas kernels  10.2 us (17%)
  local copies, waits for them, and re-layouts  3.37 us (6%)
  between operations  0.72 us (1%)
    ppermute x4, starting transfers between devices, both_ways(): lax.ppermute(up, axis, ring)  14.2 us
    ppermute x4, starting transfers between devices, both_ways(): lax.ppermute(down, axis, [(j, i) for i, j in ring])  12.3 us
    ppermute x4, waiting for transfers between devices, both_ways(): lax.ppermute(down, axis, [(j, i) for i, j in ring])  9.88 us
    ppermute x4, waiting for transfers between devices, both_ways(): lax.ppermute(up, axis, ring)  8 us
    pallas_call x1, Pallas kernels, body(): call(middle_kernel, [(Q,) + layer, (3,) + wide, wide, (Q, 2, OWN, LANES),...  4.17 us
    pallas_call x1, Pallas kernels, body(): call(last_kernel, [(2, OWN, LANES), (Q, 2, OWN, LANES)], [(Q,) + wide, (Q...  3.98 us
    unnamed x12, local copies, waits for them, and re-layouts  3.37 us
    pallas_call x1, Pallas kernels, body(): call(first_kernel, [(Q,) + layer, (Q,) + layer, layer] + [(packed(len(UP1...  1.37 us
  transfers between devices with their start and end apart: 8, of which 7 were waited for; matrix products, arithmetic and copies ran while one was open for 0% of the time, Pallas kernels for 0%

profile of v1, /device:TPU:24, one launch (start us, length us, event | category | flops | bytes accessed | tf_op | source)
XLA Modules:
  0.0 58.6 jit_solution(5132476899913467468)
XLA Ops:
  0.6 0.0 copy-start
  0.6 1.0 %copy-done = f32[19,2,16,128]{3,2,1,0:T(8,128)S(1)} copy-done((f32[19,2,16,128]{3,2,1,0:T(8,128)S(1)}, f32[19,2,16,128]{3,2,1,0:T(8,128)}, u32[]{:S(2)}) %copy-start) | copy-done | bytes 311320
  1.6 0.0 copy-start.2
  1.6 1.0 %copy-done.2 = f32[19,2,16,128]{3,2,1,0:T(8,128)S(1)} copy-done((f32[19,2,16,128]{3,2,1,0:T(8,128)S(1)}, f32[19,2,16,128]{3,2,1,0:T(8,128)}, u32[]{:S(2)}) %copy-start.2) | copy-done | bytes 311320
  2.6 0.0 copy-start.3
  2.6 0.7 %copy-done.3 = s32[2,16,128]{2,1,0:T(8,128)S(1)} copy-done((s32[2,16,128]{2,1,0:T(8,128)S(1)}, s32[2,16,128]{2,1,0:T(8,128)}, u32[]{:S(2)}) %copy-start.3) | copy-done | bytes 16408
  3.3 0.0 copy-start.5
  3.3 0.7 %copy-done.5 = f32[2,16,128]{2,1,0:T(8,128)S(1)} copy-done((f32[2,16,128]{2,1,0:T(8,128)S(1)}, f32[2,16,128]{2,1,0:T(8,128)}, u32[]{:S(2)}) %copy-start.5) | copy-done | bytes 16408
  4.0 0.1 shard_map.59
  4.1 7.5 %collective-permute-start = (f32[39,8,128]{2,1,0:T(8,128)S(1)}, f32[39,8,128]{2,1,0:T(8,128)S(1)}, u32[]{:S(2)}, u32[]{:S(2)}) collective-permute-start(f32[39,8,128]{2,1,0:T(8,128)S(1)} %get-tuple-element.19), channel_id=1, source_target_pairs={{0,32},{32,64},{64,96},{96,0},{1,33},{33,65},{65,97},{97,1},{2,34}... | collective-permute-start | bytes 479240 | tf_op jit(solution)/shard_map/ppermute | solution.py:413
  11.6 1.9 %collective-permute-start.1 = (f32[39,8,128]{2,1,0:T(8,128)S(1)}, f32[39,8,128]{2,1,0:T(8,128)S(1)}, u32[]{:S(2)}, u32[]{:S(2)}) collective-permute-start(f32[39,8,128]{2,1,0:T(8,128)S(1)} %get-tuple-element.20), channel_id=1, source_target_pairs={{32,0},{64,32},{96,64},{0,96},{33,1},{65,33},{97,65},{1,97},{34,2}... | collective-permute-start | bytes 479240 | tf_op jit(solution)/shard_map/ppermute | solution.py:413
  13.5 0.8 %collective-permute-done.below_ref = f32[39,8,128]{2,1,0:T(8,128)S(1)} collective-permute-done((f32[39,8,128]{2,1,0:T(8,128)S(1)}, f32[39,8,128]{2,1,0:T(8,128)S(1)}, u32[]{:S(2)}, u32[]{:S(2)}) %collective-permute-start) | collective-permute-done | bytes 159776 | tf_op jit(solution)/shard_map/ppermute | solution.py:413
  14.3 5.6 %collective-permute-done.1.above_ref = f32[39,8,128]{2,1,0:T(8,128)S(1)} collective-permute-done((f32[39,8,128]{2,1,0:T(8,128)S(1)}, f32[39,8,128]{2,1,0:T(8,128)S(1)}, u32[]{:S(2)}, u32[]{:S(2)}) %collective-permute-start.1) | collective-permute-done | bytes 159776 | tf_op jit(solution)/shard_map/ppermute | solution.py:413
  20.0 0.6 shard_map.60
  20.5 0.0 collective-permute-start.2
  20.6 2.9 %collective-permute-start.3 = (f32[3,24,128]{2,1,0:T(8,128)S(1)}, f32[3,24,128]{2,1,0:T(8,128)S(1)}, u32[]{:S(2)}, u32[]{:S(2)}) collective-permute-start(f32[3,24,128]{2,1,0:T(8,128)S(1)} %get-tuple-element.23), channel_id=1, source_target_pairs={{1,0},{2,1},{3,2},{4,3},{5,4},{6,5},{7,6},{8,7},{9,8},{10,9},{11,1... | collective-permute-start | bytes 110600 | tf_op jit(solution)/shard_map/ppermute | solution.py:413
  23.5 1.6 %collective-permute-done.2.before_ref = f32[3,24,128]{2,1,0:T(8,128)S(1)} collective-permute-done((f32[3,24,128]{2,1,0:T(8,128)S(1)}, f32[3,24,128]{2,1,0:T(8,128)S(1)}, u32[]{:S(2)}, u32[]{:S(2)}) %collective-permute-start.2) | collective-permute-done | bytes 36896 | tf_op jit(solution)/shard_map/ppermute | solution.py:413
  25.1 0.0 collective-permute-done.3.beyond_ref
  25.1 1.4 %shard_map.61 = (f32[19,2,2,24,128]{4,3,2,1,0:T(8,128)S(1)}, f32[19,2,2,24,128]{4,3,2,1,0:T(8,128)S(1)}, f32[2,2,24,128]{3,2,1,0:T(8,128)S(1)}, f32[27,24,128]{2,1,0:T(8,128)S(1)}, f32[27,24,128]{2,1,0:T(8,128)S(1)}) custom-call(f32[39,2,24,128]{3,2,1,0:T(8,128)S(1)} %get-tuple-element.21.main_ref, f32[3,24,128]{2,1,0:T(8,128)S(1)} %collective-permute-done.2.before_ref, ...), custom_call_target="tpu_custom_call" | custom-call | tf_op jit(solution)/shard_map/pallas_call | solution.py:423
  26.5 3.3 %collective-permute-start.4 = (f32[27,24,128]{2,1,0:T(8,128)S(1)}, f32[27,24,128]{2,1,0:T(8,128)S(1)}, u32[]{:S(2)}, u32[]{:S(2)}) collective-permute-start(f32[27,24,128]{2,1,0:T(8,128)S(1)} %get-tuple-element.27), channel_id=1, source_target_pairs={{0,128},{128,256},{256,384},{384,0},{1,129},{129,257},{257,385},{3... | collective-permute-start | bytes 995336 | tf_op jit(solution)/shard_map/ppermute | solution.py:413
  29.8 3.8 %collective-permute-start.5 = (f32[27,24,128]{2,1,0:T(8,128)S(1)}, f32[27,24,128]{2,1,0:T(8,128)S(1)}, u32[]{:S(2)}, u32[]{:S(2)}) collective-permute-start(f32[27,24,128]{2,1,0:T(8,128)S(1)} %get-tuple-element.28), channel_id=1, source_target_pairs={{128,0},{256,128},{384,256},{0,384},{129,1},{257,129},{385,257},{1... | collective-permute-start | bytes 995336 | tf_op jit(solution)/shard_map/ppermute | solution.py:413
  33.6 3.2 %collective-permute-done.4.left_ref = f32[27,24,128]{2,1,0:T(8,128)S(1)} collective-permute-done((f32[27,24,128]{2,1,0:T(8,128)S(1)}, f32[27,24,128]{2,1,0:T(8,128)S(1)}, u32[]{:S(2)}, u32[]{:S(2)}) %collective-permute-start.4) | collective-permute-done | bytes 331808 | tf_op jit(solution)/shard_map/ppermute | solution.py:413
  36.7 2.1 %collective-permute-done.5.right_ref = f32[27,24,128]{2,1,0:T(8,128)S(1)} collective-permute-done((f32[27,24,128]{2,1,0:T(8,128)S(1)}, f32[27,24,128]{2,1,0:T(8,128)S(1)}, u32[]{:S(2)}, u32[]{:S(2)}) %collective-permute-start.5) | collective-permute-done | bytes 331808 | tf_op jit(solution)/shard_map/ppermute | solution.py:413
  38.8 0.0 copy-start.1
  38.8 4.2 %shard_map.62 = (f32[19,2,2,24,128]{4,3,2,1,0:T(8,128)S(1)}, f32[3,4,2,24,128]{4,3,2,1,0:T(8,128)S(1)}, f32[4,2,24,128]{3,2,1,0:T(8,128)S(1)}, f32[19,2,16,128]{...) custom-call(f32[19,2,2,24,128]{4,3,2,1,0:T(8,128)S(1)} %get-tuple-elemen, ...), custom_call_target="tpu_custom_call" | custom-call | tf_op jit(solution)/shard_map/pallas_call | solution.py:430
  43.0 3.4 %collective-permute-start.6 = (f32[21,24,128]{2,1,0:T(8,128)S(1)}, f32[21,24,128]{2,1,0:T(8,128)S(1)}, u32[]{:S(2)}, u32[]{:S(2)}) collective-permute-start(f32[21,24,128]{2,1,0:T(8,128)S(1)} %get-tuple-element.34), channel_id=1, source_target_pairs={{0,128},{128,256},{256,384},{384,0},{1,129},{129,257},{257,385},{3... | collective-permute-start | bytes 774152 | tf_op jit(solution)/shard_map/ppermute | solution.py:413
  46.4 3.7 %collective-permute-start.7 = (f32[21,24,128]{2,1,0:T(8,128)S(1)}, f32[21,24,128]{2,1,0:T(8,128)S(1)}, u32[]{:S(2)}, u32[]{:S(2)}) collective-permute-start(f32[21,24,128]{2,1,0:T(8,128)S(1)} %get-tuple-element.35), channel_id=1, source_target_pairs={{128,0},{256,128},{384,256},{0,384},{129,1},{257,129},{385,257},{1... | collective-permute-start | bytes 774152 | tf_op jit(solution)/shard_map/ppermute | solution.py:413
  50.1 2.4 %collective-permute-done.6.left_ref = f32[21,24,128]{2,1,0:T(8,128)S(1)} collective-permute-done((f32[21,24,128]{2,1,0:T(8,128)S(1)}, f32[21,24,128]{2,1,0:T(8,128)S(1)}, u32[]{:S(2)}, u32[]{:S(2)}) %collective-permute-start.6) | collective-permute-done | bytes 258080 | tf_op jit(solution)/shard_map/ppermute | solution.py:413
  52.4 2.2 %collective-permute-done.7.right_ref = f32[21,24,128]{2,1,0:T(8,128)S(1)} collective-permute-done((f32[21,24,128]{2,1,0:T(8,128)S(1)}, f32[21,24,128]{2,1,0:T(8,128)S(1)}, u32[]{:S(2)}, u32[]{:S(2)}) %collective-permute-start.7) | collective-permute-done | bytes 258080 | tf_op jit(solution)/shard_map/ppermute | solution.py:413
  54.6 0.0 copy-done.1
  54.6 0.0 copy-done.4
  54.6 4.0 %shard_map.63 = (f32[2,16,128]{2,1,0:T(8,128)}, f32[19,2,16,128]{3,2,1,0:T(8,128)}) custom-call(f32[19,2,2,24,128]{4,3,2,1,0:T(8,128)S(1)} %get-tuple-element.29.a_ref, f32[3,4,2,24,128]{4,3,2,1,0:T(8,128)S(1)} %get-tuple-element.30.u_ref, f32[4,2,24,128]{3,2,1,0:T(8,128)S(1)} %get-tuple-element.31.b4_ref, f32[19,2,16,128]{3,2,1,0:T(8,128)S(1)} %get-tuple-element.32.f1_ref, ...), custom_call_target="tpu_custom_call" | custom-call | tf_op jit(solution)/shard_map/pallas_call | solution.py:436
  (1 shorter events, 0.0 us)
Async XLA Ops:
  0.6 1.0 %copy-start = (f32[19,2,16,128]{3,2,1,0:T(8,128)S(1)}, f32[19,2,16,128]{3,2,1,0:T(8,128)}, u32[]{:S(2)}) copy-start(f32[19,2,16,128]{3,2,1,0:T(8,128)} %f_ref.5) | copy-start | bytes 933892
  1.6 1.0 %copy-start.2 = (f32[19,2,16,128]{3,2,1,0:T(8,128)S(1)}, f32[19,2,16,128]{3,2,1,0:T(8,128)}, u32[]{:S(2)}) copy-start(f32[19,2,16,128]{3,2,1,0:T(8,128)} %seed_ref.3) | copy-start | bytes 933892
  2.6 0.7 %copy-start.3 = (s32[2,16,128]{2,1,0:T(8,128)S(1)}, s32[2,16,128]{2,1,0:T(8,128)}, u32[]{:S(2)}) copy-start(s32[2,16,128]{2,1,0:T(8,128)} %solid_ref.5) | copy-start | bytes 49156
  3.3 0.7 %copy-start.5 = (f32[2,16,128]{2,1,0:T(8,128)S(1)}, f32[2,16,128]{2,1,0:T(8,128)}, u32[]{:S(2)}) copy-start(f32[2,16,128]{2,1,0:T(8,128)} %por_ref.3) | copy-start | bytes 49156
  4.1 10.3 %collective-permute-start = (f32[39,8,128]{2,1,0:T(8,128)S(1)}, f32[39,8,128]{2,1,0:T(8,128)S(1)}, u32[]{:S(2)}, u32[]{:S(2)}) collective-permute-start(f32[39,8,128]{2,1,0:T(8,128)S(1)} %get-tuple-element.19), channel_id=1, source_target_pairs={{0,32},{32,64},{64,96},{96,0},{1,33},{33,65},{65,97},{97,1},{2,34}... | collective-permute-start | bytes 479240 | tf_op jit(solution)/shard_map/ppermute | solution.py:413
  11.6 8.4 %collective-permute-start.1 = (f32[39,8,128]{2,1,0:T(8,128)S(1)}, f32[39,8,128]{2,1,0:T(8,128)S(1)}, u32[]{:S(2)}, u32[]{:S(2)}) collective-permute-start(f32[39,8,128]{2,1,0:T(8,128)S(1)} %get-tuple-element.20), channel_id=1, source_target_pairs={{32,0},{64,32},{96,64},{0,96},{33,1},{65,33},{97,65},{1,97},{34,2}... | collective-permute-start | bytes 479240 | tf_op jit(solution)/shard_map/ppermute | solution.py:413
  20.5 4.6 %collective-permute-start.2 = (f32[3,24,128]{2,1,0:T(8,128)S(1)}, f32[3,24,128]{2,1,0:T(8,128)S(1)}, u32[]{:S(2)}, u32[]{:S(2)}) collective-permute-start(f32[3,24,128]{2,1,0:T(8,128)S(1)} %get-tuple-element.22), channel_id=1, source_target_pairs={{0,1},{1,2},{2,3},{3,4},{4,5},{5,6},{6,7},{7,8},{8,9},{9,10},{10,1... | collective-permute-start | bytes 110600 | tf_op jit(solution)/shard_map/ppermute | solution.py:413
  20.6 4.6 %collective-permute-start.3 = (f32[3,24,128]{2,1,0:T(8,128)S(1)}, f32[3,24,128]{2,1,0:T(8,128)S(1)}, u32[]{:S(2)}, u32[]{:S(2)}) collective-permute-start(f32[3,24,128]{2,1,0:T(8,128)S(1)} %get-tuple-element.23), channel_id=1, source_target_pairs={{1,0},{2,1},{3,2},{4,3},{5,4},{6,5},{7,6},{8,7},{9,8},{10,9},{11,1... | collective-permute-start | bytes 110600 | tf_op jit(solution)/shard_map/ppermute | solution.py:413
  26.5 10.2 %collective-permute-start.4 = (f32[27,24,128]{2,1,0:T(8,128)S(1)}, f32[27,24,128]{2,1,0:T(8,128)S(1)}, u32[]{:S(2)}, u32[]{:S(2)}) collective-permute-start(f32[27,24,128]{2,1,0:T(8,128)S(1)} %get-tuple-element.27), channel_id=1, source_target_pairs={{0,128},{128,256},{256,384},{384,0},{1,129},{129,257},{257,385},{3... | collective-permute-start | bytes 995336 | tf_op jit(solution)/shard_map/ppermute | solution.py:413
  29.8 9.0 %collective-permute-start.5 = (f32[27,24,128]{2,1,0:T(8,128)S(1)}, f32[27,24,128]{2,1,0:T(8,128)S(1)}, u32[]{:S(2)}, u32[]{:S(2)}) collective-permute-start(f32[27,24,128]{2,1,0:T(8,128)S(1)} %get-tuple-element.28), channel_id=1, source_target_pairs={{128,0},{256,128},{384,256},{0,384},{129,1},{257,129},{385,257},{1... | collective-permute-start | bytes 995336 | tf_op jit(solution)/shard_map/ppermute | solution.py:413
  38.8 15.8 %copy-start.1 = (f32[19,2,16,128]{3,2,1,0:T(8,128)S(1)}, f32[19,2,16,128]{3,2,1,0:T(8,128)}, u32[]{:S(2)}) copy-start(f32[19,2,16,128]{3,2,1,0:T(8,128)} %f_ref.5) | copy-start | bytes 933892
  38.8 15.8 %copy-start.4 = (s32[2,16,128]{2,1,0:T(8,128)S(1)}, s32[2,16,128]{2,1,0:T(8,128)}, u32[]{:S(2)}) copy-start(s32[2,16,128]{2,1,0:T(8,128)} %solid_ref.5) | copy-start | bytes 49156
  43.0 9.4 %collective-permute-start.6 = (f32[21,24,128]{2,1,0:T(8,128)S(1)}, f32[21,24,128]{2,1,0:T(8,128)S(1)}, u32[]{:S(2)}, u32[]{:S(2)}) collective-permute-start(f32[21,24,128]{2,1,0:T(8,128)S(1)} %get-tuple-element.34), channel_id=1, source_target_pairs={{0,128},{128,256},{256,384},{384,0},{1,129},{129,257},{257,385},{3... | collective-permute-start | bytes 774152 | tf_op jit(solution)/shard_map/ppermute | solution.py:413
  46.4 8.2 %collective-permute-start.7 = (f32[21,24,128]{2,1,0:T(8,128)S(1)}, f32[21,24,128]{2,1,0:T(8,128)S(1)}, u32[]{:S(2)}, u32[]{:S(2)}) collective-permute-start(f32[21,24,128]{2,1,0:T(8,128)S(1)} %get-tuple-element.35), channel_id=1, source_target_pairs={{128,0},{256,128},{384,256},{0,384},{129,1},{257,129},{385,257},{1... | collective-permute-start | bytes 774152 | tf_op jit(solution)/shard_map/ppermute | solution.py:413

commit v2 on v1

v2 whole, which is shorter than its diff:
```python
import jax
import jax.numpy as jnp
from jax import lax
from jax.experimental import pallas as pl
from jax.experimental.pallas import tpu as pltpu
from jax.sharding import PartitionSpec as P

INTERPRET = False

VEL = [
    (0, 0, 0),
    (1, 0, 0), (-1, 0, 0), (0, 1, 0), (0, -1, 0), (0, 0, 1), (0, 0, -1),
    (1, 1, 0), (-1, -1, 0), (1, -1, 0), (-1, 1, 0),
    (1, 0, 1), (-1, 0, -1), (1, 0, -1), (-1, 0, 1),
    (0, 1, 1), (0, -1, -1), (0, 1, -1), (0, -1, 1),
]
OPP = [0, 2, 1, 4, 3, 6, 5, 8, 7, 10, 9, 12, 11, 14, 13, 16, 15, 18, 17]
WEIGHT = [1.0 / 3.0] + [1.0 / 18.0] * 6 + [1.0 / 36.0] * 12
OMEGA = 1.25
Q = 19
XP = [i for i in range(Q) if VEL[i][0] == 1]
X0 = [i for i in range(Q) if VEL[i][0] == 0]
XM = [i for i in range(Q) if VEL[i][0] == -1]
PAIRS = [i for i in range(1, Q, 2)]

ROWS, OWN, LANES, RIM = 24, 16, 128, 4
FIELDS = 2 * Q + 1
ZTILES = -(-2 * FIELDS // 32)


def total(terms):
    terms = list(terms)
    while len(terms) > 1:
        terms = [a + b for a, b in zip(terms[::2], terms[1::2])] + (terms[-1:] if len(terms) % 2 else [])
    return terms[0]


def signed(values, axis):
    plus = total(values[i] for i in range(Q) if VEL[i][axis] == 1)
    minus = total(values[i] for i in range(Q) if VEL[i][axis] == -1)
    return plus - minus


def project(vector, i):
    out = None
    for axis in range(3):
        c = VEL[i][axis]
        if c == 0:
            continue
        if out is None:
            out = vector[axis] if c == 1 else -vector[axis]
        else:
            out = out + vector[axis] if c == 1 else out - vector[axis]
    return out


def moments(f):
    rho = total(f)
    inv = 1.0 / rho
    return rho, [signed(f, axis) * inv for axis in range(3)]


def moments_from(level, f):
    plus, minus = total(f[i] for i in XP), total(f[i] for i in XM)
    rho = level[0] + (plus + minus)
    inv = 1.0 / rho
    along = [level[axis] + total(f[i] if VEL[i][axis] == 1 else -f[i] for i in XP + XM if VEL[i][axis]) for axis in (1, 2)]
    return rho, [(plus - minus) * inv, along[0] * inv, along[1] * inv]


def collide(f, rho, u, blocking, want):
    keep = 1.0 - blocking
    own = (1.0 - OMEGA) * keep
    scale = OMEGA * keep * rho
    base = 1.0 - 1.5 * (u[0] * u[0] + u[1] * u[1] + u[2] * u[2])
    out = {}
    if 0 in want:
        out[0] = (own + blocking) * f[0] + (WEIGHT[0] * scale) * base
    for i in PAIRS:
        j = i + 1
        if i not in want and j not in want:
            continue
        s = WEIGHT[i] * scale
        p = project(u, i)
        even = s * (base + 4.5 * (p * p))
        odd = s * (3.0 * p)
        if i in want:
            out[i] = own * f[i] + blocking * f[j] + (even + odd)
        if j in want:
            out[j] = own * f[j] + blocking * f[i] + (even - odd)
    return out


def flow(b, u):
    base = 1.0 - 1.5 * (u[0] * u[0] + u[1] * u[1] + u[2] * u[2])
    weighted, value, slope = [], [], [[], [], []]
    if 0 in b:
        weighted.append(WEIGHT[0] * b[0])
    faces, edges = [], []
    for i in PAIRS:
        j = i + 1
        if i not in b and j not in b:
            continue
        p = project(u, i)
        if i in b and j in b:
            even, odd = b[i] + b[j], b[i] - b[j]
        elif i in b:
            even, odd = b[i], b[i]
        else:
            even, odd = b[j], -b[j]
        (faces if i < 7 else edges).append(even)
        ps = p * even
        d3 = 3.0 * odd
        value.append((WEIGHT[i] * p) * (d3 + 4.5 * ps))
        g = WEIGHT[i] * (d3 + 9.0 * ps)
        for axis in range(3):
            if VEL[i][axis]:
                slope[axis].append(g if VEL[i][axis] == 1 else -g)
    weighted = total(weighted + [WEIGHT[1] * total(faces), WEIGHT[7] * total(edges)])
    return [base * weighted + total(value)] + [total(slope[axis]) - 3.0 * (u[axis] * weighted) for axis in range(3)]


def back(b, sums, u, blocking, want):
    energy, *v = sums
    keep = 1.0 - blocking
    own = (1.0 - OMEGA) * keep
    mix = OMEGA * keep
    common = mix * (energy - (v[0] * u[0] + v[1] * u[1] + v[2] * u[2]))
    mv = [mix * v[axis] for axis in range(3)]
    out = {}
    if 0 in want:
        out[0] = (own + blocking) * b[0] + common
    for i in PAIRS:
        j = i + 1
        if i not in want and j not in want:
            continue
        p = project(mv, i)
        if i in want:
            out[i] = own * b[i] + blocking * b[j] + (common + p)
        if j in want:
            out[j] = own * b[j] + blocking * b[i] + (common - p)
    return out


def gradient_of(b, f, rho, energy):
    return total(b[i] * (f[OPP[i]] - (1.0 - OMEGA) * f[i]) for i in range(Q)) - (OMEGA * rho) * energy


def column(shape):
    return lax.broadcasted_iota(jnp.int32, shape, len(shape) - 1)


def turn(tile, shift, axis):
    shift = shift % tile.shape[axis]
    return tile if shift == 0 else pltpu.roll(tile, shift, axis)


def moved(main, rim, i, sign):
    y, z = sign * VEL[i][1], sign * VEL[i][2]
    if y:
        main, rim = turn(main, y, 0), turn(rim, y, 0)
    if z:
        at = column(main.shape)
        edge = at == (0 if z == 1 else LANES - 1)
        main, rim = turn(main, z, 1), turn(rim, z, 1)
        main, rim = jnp.where(edge, rim, main), jnp.where(edge, main, rim)
    return main, rim


def pack(ref, tiles):
    n = len(tiles)
    at = column((ROWS, LANES)) // 8
    for k, (main, _) in enumerate(tiles):
        ref[k] = main()
    for first in range(0, n, 16):
        joined = None
        for k in range(first, min(first + 16, n)):
            piece = turn(tiles[k][1](), 8 * (k - first) + 4, 1)
            joined = piece if joined is None else jnp.where(at == k - first, piece, joined)
        ref[n + first // 16] = joined


def unpack(ref, n, k):
    return ref[k], turn(ref[n + k // 16], -(8 * (k % 16) + 4), 1)


def packed(n):
    return n + -(-n // 16)


def rims(ref, n, out_ref):
    for k in range(n):
        out_ref[k] = unpack(ref, n, k)[1]


SEND1, SEND2 = 19, 14


def call(kernel, outs, scratch=(), more=(), space=None, cost=1000):
    specs = {} if space is None else {"in_specs": [pl.BlockSpec(memory_space=s) for s in space]}
    return pl.pallas_call(
        kernel,
        out_shape=[jax.ShapeDtypeStruct(shape, jnp.float32) for shape in outs],
        scratch_shapes=[pltpu.VMEM(shape, jnp.float32) for shape in scratch] + list(more),
        compiler_params=None if INTERPRET else pltpu.CompilerParams(vmem_limit_bytes=40 * 2**20),
        cost_estimate=pl.CostEstimate(flops=cost * 2000, bytes_accessed=cost * 1000, transcendentals=0),
        interpret=INTERPRET,
        **specs,
    )


def rows_kernel(f_hbm, por_hbm, solid_hbm, seed_hbm, up_ref, down_ref, f_ref, por_ref, seed_ref, solid_ref, sems):
    copies = [
        pltpu.make_async_copy(src, dst, sems.at[k])
        for k, (src, dst) in enumerate(
            [(f_hbm, f_ref), (seed_hbm, seed_ref), (por_hbm, por_ref), (solid_hbm, solid_ref)]
        )
    ]
    for copy in copies:
        copy.start()

    def send(k, layer, tile):
        up_ref[k, 4 * layer : 4 * layer + 4, :] = tile(12)
        down_ref[k, 4 * layer : 4 * layer + 4, :] = tile(0)

    copies[0].wait()
    for k in range(Q):
        for layer in range(2):
            send(k, layer, lambda row: f_ref[k, layer, row : row + 4, :])
    copies[1].wait()
    for k in range(Q):
        for layer in range(2):
            send(k + Q, layer, lambda row: seed_ref[k, layer, row : row + 4, :])
    copies[2].wait()
    copies[3].wait()
    for layer in range(2):
        send(2 * Q, layer, lambda row: jnp.where(solid_ref[layer, row : row + 4, :] == 1, 1.0, por_ref[layer, row : row + 4, :]))


def columns_kernel(f_ref, por_ref, solid_ref, seed_ref, below_ref, above_ref, main_ref, up_ref, down_ref):
    at = column((ROWS, LANES)) // 4
    high = low = None
    for k in range(FIELDS):
        for layer in range(2):
            if k < Q:
                own = f_ref[k, layer]
            elif k < 2 * Q:
                own = seed_ref[k - Q, layer]
            else:
                own = jnp.where(solid_ref[layer] == 1, 1.0, por_ref[layer])
            rows = slice(4 * layer, 4 * layer + 4)
            tile = jnp.concatenate([own, above_ref[k, rows, :], below_ref[k, rows, :]], axis=0)
            main_ref[k, layer] = tile
            slot = (2 * k + layer) % 32
            piece_up, piece_down = turn(tile, 4 * slot + 4, 1), turn(tile, 4 * slot, 1)
            high = piece_up if slot == 0 else jnp.where(at == slot, piece_up, high)
            low = piece_down if slot == 0 else jnp.where(at == slot, piece_down, low)
            if slot == 31 or 2 * k + layer == 2 * FIELDS - 1:
                up_ref[(2 * k + layer) // 32] = high
                down_ref[(2 * k + layer) // 32] = low


def tiles_loop(count, body):
    def step(n, carry):
        body(n // 3, pl.multiple_of((n % 3) * 8, 8))
        return carry

    lax.fori_loop(0, count, step, 0)


def main_kernel(main_ref, g_ref):
    for layer in range(2):

        def body(_, row, layer=layer):
            f = [main_ref[i, layer, pl.ds(row, 8), :] for i in range(Q)]
            rho, u = moments(f)
            g = collide(f, rho, u, main_ref[2 * Q, layer, pl.ds(row, 8), :], range(Q))
            for i in range(Q):
                g_ref[i, layer, pl.ds(row, 8), :] = g[i]

        tiles_loop(3, body)


def first_kernel(
    main_ref, g_ref, before_ref, beyond_ref,
    f1_ref, edge_ref, level_ref, s_ref, b_ref, up_ref, down_ref,
    f_scr, g_scr,
):
    at = column((ROWS, LANES))
    for k in range(FIELDS):
        for layer in range(2):
            n = 2 * k + layer
            slot, tile = n % 32, n // 32
            before = turn(before_ref[tile], -(4 * slot + 4), 1)
            beyond = turn(beyond_ref[tile], -4 * slot, 1)
            rim = jnp.where(at < RIM, beyond, before)
            if k < Q:
                f_scr[k, layer] = rim
            elif k < 2 * Q:
                s_ref[k - Q, layer] = rim
            else:
                b_ref[layer, 0] = main_ref[k, layer]
                b_ref[layer, 1] = rim

    for layer in range(2):

        def body(_, row, layer=layer):
            f = [f_scr[i, layer, pl.ds(row, 8), :] for i in range(Q)]
            rho, u = moments(f)
            g = collide(f, rho, u, b_ref[layer, 1, pl.ds(row, 8), :], range(Q))
            for i in range(Q):
                g_scr[i, layer, pl.ds(row, 8), :] = g[i]

        tiles_loop(3, body)

    for i in range(Q):
        for layer in range(2):
            to = layer + VEL[i][0]
            tiles = moved(g_ref[i, layer], g_scr[i, layer], i, 1)
            for lane in range(2):
                if to in (0, 1):
                    f1_ref[i, to, lane] = tiles[lane]
                else:
                    edge_ref[i, lane] = tiles[lane]
    for layer in range(2):
        for lane in range(2):
            stay = {i: f1_ref[i, layer, lane] for i in X0}
            level_ref[0, layer, lane] = total(stay.values())
            for axis in (1, 2):
                level_ref[axis, layer, lane] = total(
                    stay[i] if VEL[i][axis] == 1 else -stay[i] for i in X0 if VEL[i][axis]
                )

    def tiles_of(forward, backward, layer):
        def pick(ref, *where):
            return (lambda: ref[where + (0,)]), (lambda: ref[where + (1,)])

        out = [pick(f1_ref, i, layer) for i in forward]
        out += [pick(level_ref, k, layer) for k in range(3)]
        out.append(pick(b_ref, layer))
        out += [pick(edge_ref, i) for i in forward]
        for i in backward:
            pair = moved(main_ref[Q + i, layer], s_ref[i, layer], i, -1)
            out.append(((lambda pair=pair: pair[0]), (lambda pair=pair: pair[1])))
        return out

    pack(up_ref, tiles_of(XP, XM, 1))
    pack(down_ref, tiles_of(XM, XP, 0))


def seed_kernel(main_ref, s_ref, b2_ref):
    for i in range(Q):
        for layer in range(2):
            to = layer - VEL[i][0]
            if to in (0, 1):
                main, rim = moved(main_ref[Q + i, layer], s_ref[i, layer], i, -1)
                b2_ref[i, to, 0] = main
                b2_ref[i, to, 1] = rim


def middle_kernel(
    f1_ref, edge_ref, level_ref, b_ref, b2_ref, left_ref, right_ref,
    mom_ref, bh_ref, grad_ref, b1_ref, edge1_ref, sums_ref, up_ref, down_ref,
    l_scr, r_scr, g_scr, f_scr, a_scr,
):
    rims(left_ref, SEND1, l_scr)
    rims(right_ref, SEND1, r_scr)
    got = ((left_ref, right_ref), (l_scr, r_scr))
    for side in range(2):
        for lane in range(2):
            bh_ref[side, lane] = got[lane][side][8]

    for layer in range(2):
        for lane in range(2):

            def body(_, row, layer=layer, lane=lane):
                rows = pl.ds(row, 8)
                missing = XP if layer == 0 else XM
                f = [None if i in missing else f1_ref[i, layer, lane, rows, :] for i in range(Q)]
                for k, i in enumerate(missing):
                    f[i] = got[lane][layer][9 + k, rows, :]
                rho, u = moments_from([level_ref[k, layer, lane, rows, :] for k in range(3)], f)
                mom_ref[3, layer + 1, lane, rows, :] = rho
                for axis in range(3):
                    mom_ref[axis, layer + 1, lane, rows, :] = u[axis]
                g = collide(f, rho, u, b_ref[layer, lane, rows, :], range(Q))
                for i in range(Q):
                    g_scr[i, layer + 1, lane, rows, :] = g[i]

            tiles_loop(3, body)

    for side in range(2):
        for lane in range(2):

            def body(_, row, side=side, lane=lane):
                rows = pl.ds(row, 8)
                theirs, ours = (XP, XM) if side == 0 else (XM, XP)
                f = [None] * Q
                for k, i in enumerate(theirs):
                    f[i] = got[lane][side][k, rows, :]
                for i in ours:
                    f[i] = edge_ref[i, lane, rows, :]
                rho, u = moments_from([got[lane][side][5 + k, rows, :] for k in range(3)], f)
                for axis in range(3):
                    mom_ref[axis, 3 * side, lane, rows, :] = u[axis]
                g = collide(f, rho, u, got[lane][side][8, rows, :], theirs)
                for i in theirs:
                    g_scr[i, 3 * side, lane, rows, :] = g[i]

            tiles_loop(3, body)

    for i in range(Q):
        for layer in range(2):
            n = layer + 1 - VEL[i][0]
            main, rim = moved(g_scr[i, n, 0], g_scr[i, n, 1], i, 1)
            f_scr[i, layer, 0] = main
            f_scr[i, layer, 1] = rim

    for layer in range(2):
        for lane in range(2):

            def body(row, layer=layer, lane=lane, own=False):
                rows = pl.ds(row, 8)
                missing = XM if layer == 0 else XP
                f = [f_scr[i, layer, lane, rows, :] for i in range(Q)]
                b = {i: b2_ref[i, layer, lane, rows, :] for i in range(Q) if i not in missing}
                for k, i in enumerate(missing):
                    b[i] = got[lane][layer][14 + k, rows, :]
                rho, u = moments(f)
                sums = flow(b, u)
                a = back(b, sums, u, b_ref[layer, lane, rows, :], range(Q))
                for i in range(Q):
                    a_scr[i, layer, lane, rows, :] = a[i]
                if own:
                    grad_ref[layer, rows, :] = gradient_of(b, f, rho, sums[0])

            if lane == 0:

                def step(n, carry, body=body):
                    body(pl.multiple_of(n * 8, 8), own=True)
                    return carry

                lax.fori_loop(0, 2, step, 0)
                body(16)
            else:
                tiles_loop(3, lambda _, row, body=body: body(row))

    for i in range(Q):
        for layer in range(2):
            to = layer - VEL[i][0]
            tiles = moved(a_scr[i, layer, 0], a_scr[i, layer, 1], i, -1)
            for lane in range(2):
                if to in (0, 1):
                    b1_ref[i, to, lane] = tiles[lane]
                else:
                    edge1_ref[i, lane] = tiles[lane]

    for layer in range(2):
        for lane in range(2):

            def body(_, row, layer=layer, lane=lane):
                rows = pl.ds(row, 8)
                missing = XM if layer == 0 else XP
                b = {i: b1_ref[i, layer, lane, rows, :] for i in range(Q) if i not in missing}
                sums = flow(b, [mom_ref[axis, layer + 1, lane, rows, :] for axis in range(3)])
                for k in range(4):
                    sums_ref[k, layer, lane, rows, :] = sums[k]

            tiles_loop(3, body)

    def tiles_of(theirs, layer):
        def pick(ref, *where):
            return (lambda: ref[where + (0,)]), (lambda: ref[where + (1,)])

        return (
            [pick(edge1_ref, i) for i in theirs]
            + [pick(b1_ref, i, layer) for i in theirs]
            + [pick(sums_ref, k, layer) for k in range(4)]
        )

    pack(up_ref, tiles_of(XM, 1))
    pack(down_ref, tiles_of(XP, 0))


def last_kernel(
    b1_ref, edge1_ref, sums_ref, mom_ref, b_ref, bh_ref, f1_ref, left1_ref, right1_ref, grad_ref, left_ref, right_ref, f_ref, solid_ref,
    out_grad_ref, out_ref,
    l_scr, r_scr, a_scr, b0_scr,
):
    rims(left_ref, SEND2, l_scr)
    rims(right_ref, SEND2, r_scr)
    got = ((left_ref, right_ref), (l_scr, r_scr))
    got1 = (left1_ref, right1_ref)

    for layer in range(2):
        for lane in range(2):

            def body(row, layer=layer, lane=lane, own=False):
                rows = pl.ds(row, 8)
                missing = XM if layer == 0 else XP
                new = {i: got[lane][layer][k, rows, :] for k, i in enumerate(missing)}
                b = {i: b1_ref[i, layer, lane, rows, :] for i in range(Q) if i not in missing}
                b.update(new)
                u = [mom_ref[axis, layer + 1, lane, rows, :] for axis in range(3)]
                sums = [sums_ref[k, layer, lane, rows, :] + part for k, part in enumerate(flow(new, u))]
                a = back(b, sums, u, b_ref[layer, lane, rows, :], range(Q))
                for i in range(Q):
                    a_scr[i, layer + 1, lane, rows, :] = a[i]
                if own:
                    f = {i: f1_ref[i, layer, lane, rows, :] for i in range(Q) if OPP[i] not in missing}
                    for k, i in enumerate(XP if layer == 0 else XM):
                        f[i] = got1[layer][9 + k, rows, :]
                    grad = gradient_of(b, f, mom_ref[3, layer + 1, lane, rows, :], sums[0])
                    out_grad_ref[layer, rows, :] = grad + grad_ref[layer, rows, :]

            if lane == 0:

                def step(n, carry, body=body):
                    body(pl.multiple_of(n * 8, 8), own=True)
                    return carry

                lax.fori_loop(0, 2, step, 0)
                body(16)
            else:
                tiles_loop(3, lambda _, row, body=body: body(row))

    for side in range(2):
        for lane in range(2):

            def body(_, row, side=side, lane=lane):
                rows = pl.ds(row, 8)
                theirs, ours = (XM, XP) if side == 0 else (XP, XM)
                new = {i: edge1_ref[i, lane, rows, :] for i in ours}
                b = dict(new)
                for k, i in enumerate(theirs):
                    b[i] = got[lane][side][5 + k, rows, :]
                u = [mom_ref[axis, 3 * side, lane, rows, :] for axis in range(3)]
                sums = [got[lane][side][10 + k, rows, :] + part for k, part in enumerate(flow(new, u))]
                a = back(b, sums, u, bh_ref[side, lane, rows, :], theirs)
                for i in theirs:
                    a_scr[i, 3 * side, lane, rows, :] = a[i]

            tiles_loop(3, body)

    for i in range(Q):
        for layer in range(2):
            n = layer + 1 + VEL[i][0]
            main, _ = moved(a_scr[i, n, 0], a_scr[i, n, 1], i, -1)
            b0_scr[i, layer] = main[0:OWN]

    for layer in range(2):

        def final(n, carry, layer=layer):
            rows = pl.ds(pl.multiple_of(n * 8, 8), 8)
            f = [f_ref[i, layer, rows, :] for i in range(Q)]
            b = {i: b0_scr[i, layer, rows, :] for i in range(Q)}
            rho, u = moments(f)
            sums = flow(b, u)
            a = back(b, sums, u, b_ref[layer, 0, rows, :], range(Q))
            for i in range(Q):
                out_ref[i, layer, rows, :] = a[i]
            grad = gradient_of(b, f, rho, sums[0]) + out_grad_ref[layer, rows, :]
            out_grad_ref[layer, rows, :] = jnp.where(solid_ref[layer, rows, :] == 1, 0.0, grad)
            return carry

        lax.fori_loop(0, 2, final, 0)


def both_ways(up, down, axis):
    count = lax.axis_size(axis)
    ring = [(i, (i + 1) % count) for i in range(count)]
    return lax.ppermute(up, axis, ring), lax.ppermute(down, axis, [(j, i) for i, j in ring])


def body(populations, porosity, solid, seed_adjoint):
    half, tile = (2, 2, ROWS, LANES), (ROWS, LANES)
    inputs = (populations, porosity, solid, seed_adjoint)
    block = populations.shape
    up, down = call(
        rows_kernel,
        [(FIELDS, 8, LANES)] * 2,
        [block, block[1:], block],
        [pltpu.VMEM(block[1:], jnp.int32), pltpu.SemaphoreType.DMA((4,))],
        space=[pltpu.HBM] * 4,
    )(*inputs)
    below, above = both_ways(up, down, "gy")
    main, up, down = call(columns_kernel, [(FIELDS, 2) + tile] + [(ZTILES,) + tile] * 2)(*inputs, below, above)
    before, beyond = both_ways(up, down, "gz")
    (g,) = call(main_kernel, [(Q, 2) + tile])(main)
    f1, edge, level, s, b, up, down = call(
        first_kernel,
        [(Q,) + half, (Q, 2) + tile, (3,) + half, (Q, 2) + tile, half] + [(packed(SEND1),) + tile] * 2,
        [(Q, 2) + tile] * 2,
    )(main, g, before, beyond)
    left1, right1 = both_ways(up, down, "gx")
    (b2,) = call(seed_kernel, [(Q,) + half])(main, s)
    wide = (4, 2) + tile
    mom, bh, grad, b1, edge1, sums, up, down = call(
        middle_kernel,
        [(4,) + wide, half, (2, OWN, LANES), (Q,) + half, (Q, 2) + tile, (4,) + half] + [(packed(SEND2),) + tile] * 2,
        [(SEND1,) + tile] * 2 + [(Q,) + wide, (Q,) + half, (Q,) + half],
    )(f1, edge, level, b, b2, left1, right1)
    left, right = both_ways(up, down, "gx")
    gradient, adjoint_out = call(
        last_kernel,
        [(2, OWN, LANES), (Q, 2, OWN, LANES)],
        [(SEND2,) + tile] * 2 + [(Q,) + wide, (Q, 2, OWN, LANES)],
    )(b1, edge1, sums, mom, b, bh, f1, left1, right1, grad, left, right, populations, solid)
    return gradient, adjoint_out


def solution(mesh):
    field, cell = P(None, "gx", "gy", "gz"), P("gx", "gy", "gz")
    return jax.shard_map(
        body, mesh=mesh, in_specs=(field, cell, cell, field), out_specs=(cell, field), check_vma=False
    )
```

time: 59.3 us -> 54.5 us (0.919)
  Pallas kernels: 10.2 us -> 7.37 us
  waiting for transfers between devices: 17.9 us -> 15.9 us
    pallas_call x5 -> x7, Pallas kernels: 10.2 us -> 7.37 us  [the longest x1 2.77 us: body(): call(middle_kernel, [(4,) + wide, half, (2, OWN, LANES), (Q,) + half, (Q,...]
    ppermute x4, waiting for transfers between devices: 8 us -> 5.99 us  [both_ways(): lax.ppermute(up, axis, ring)]
    unnamed x12 -> x10, local copies, waits for them, and re-layouts: 3.37 us -> 3.36 us
  transfers between devices with their start and end apart: 8 -> 8, of which waited for: 7 -> 7; matrix products, arithmetic and copies ran while one was open for 0% -> 0% of each run, Pallas kernels for 0% -> 1%
where the time goes in v2:
time: 54.5 us; the launch traced here: 53.8 us
  starting transfers between devices  26.5 us (49%)
  waiting for transfers between devices  15.9 us (29%)
  Pallas kernels  7.37 us (14%)
  local copies, waits for them, and re-layouts  3.36 us (6%)
  between operations  0.74 us (1%)
    ppermute x4, starting transfers between devices, both_ways(): lax.ppermute(up, axis, ring)  14.2 us
    ppermute x4, starting transfers between devices, both_ways(): lax.ppermute(down, axis, [(j, i) for i, j in ring])  12.3 us
    ppermute x4, waiting for transfers between devices, both_ways(): lax.ppermute(down, axis, [(j, i) for i, j in ring])  9.88 us
    ppermute x4, waiting for transfers between devices, both_ways(): lax.ppermute(up, axis, ring)  5.99 us
    unnamed x10, local copies, waits for them, and re-layouts  3.36 us
    pallas_call x1, Pallas kernels, body(): call(middle_kernel, [(4,) + wide, half, (2, OWN, LANES), (Q,) + half, (Q,...  2.77 us
    pallas_call x1, Pallas kernels, body(): call(last_kernel, [(2, OWN, LANES), (Q, 2, OWN, LANES)], [(SEND2,) + tile...  2.13 us
    pallas_call x1, Pallas kernels, body(): call(first_kernel, [(Q,) + half, (Q, 2) + tile, (3,) + half, (Q, 2) + til...  1.19 us
  transfers between devices with their start and end apart: 8, of which 7 were waited for; matrix products, arithmetic and copies ran while one was open for 0% of the time, Pallas kernels for 1%

profile of v2, /device:TPU:24, one launch (start us, length us, event | category | flops | bytes accessed | tf_op | source)
XLA Modules:
  0.0 53.8 jit_solution(1626258547832202563)
XLA Ops:
  0.6 0.0 copy-start
  0.6 1.0 %copy-done = f32[19,2,16,128]{3,2,1,0:T(8,128)S(1)} copy-done((f32[19,2,16,128]{3,2,1,0:T(8,128)S(1)}, f32[19,2,16,128]{3,2,1,0:T(8,128)}, u32[]{:S(2)}) %copy-start) | copy-done | bytes 311320
  1.6 0.0 copy-start.1
  1.6 1.0 %copy-done.1 = f32[19,2,16,128]{3,2,1,0:T(8,128)S(1)} copy-done((f32[19,2,16,128]{3,2,1,0:T(8,128)S(1)}, f32[19,2,16,128]{3,2,1,0:T(8,128)}, u32[]{:S(2)}) %copy-start.1) | copy-done | bytes 311320
  2.6 0.0 copy-start.2
  2.6 0.7 %copy-done.2 = s32[2,16,128]{2,1,0:T(8,128)S(1)} copy-done((s32[2,16,128]{2,1,0:T(8,128)S(1)}, s32[2,16,128]{2,1,0:T(8,128)}, u32[]{:S(2)}) %copy-start.2) | copy-done | bytes 16408
  3.3 0.0 copy-start.4
  3.3 0.7 %copy-done.4 = f32[2,16,128]{2,1,0:T(8,128)S(1)} copy-done((f32[2,16,128]{2,1,0:T(8,128)S(1)}, f32[2,16,128]{2,1,0:T(8,128)}, u32[]{:S(2)}) %copy-start.4) | copy-done | bytes 16408
  4.0 0.3 shard_map.59
  4.3 7.5 %collective-permute-start = (f32[39,8,128]{2,1,0:T(8,128)S(1)}, f32[39,8,128]{2,1,0:T(8,128)S(1)}, u32[]{:S(2)}, u32[]{:S(2)}) collective-permute-start(f32[39,8,128]{2,1,0:T(8,128)S(1)} %get-tuple-element.22), channel_id=1, source_target_pairs={{0,32},{32,64},{64,96},{96,0},{1,33},{33,65},{65,97},{97,1},{2,34}... | collective-permute-start | bytes 479240 | tf_op jit(solution)/shard_map/ppermute | solution.py:572
  11.8 1.9 %collective-permute-start.1 = (f32[39,8,128]{2,1,0:T(8,128)S(1)}, f32[39,8,128]{2,1,0:T(8,128)S(1)}, u32[]{:S(2)}, u32[]{:S(2)}) collective-permute-start(f32[39,8,128]{2,1,0:T(8,128)S(1)} %get-tuple-element.23), channel_id=1, source_target_pairs={{32,0},{64,32},{96,64},{0,96},{33,1},{65,33},{97,65},{1,97},{34,2}... | collective-permute-start | bytes 479240 | tf_op jit(solution)/shard_map/ppermute | solution.py:572
  13.7 0.8 %collective-permute-done.below_ref = f32[39,8,128]{2,1,0:T(8,128)S(1)} collective-permute-done((f32[39,8,128]{2,1,0:T(8,128)S(1)}, f32[39,8,128]{2,1,0:T(8,128)S(1)}, u32[]{:S(2)}, u32[]{:S(2)}) %collective-permute-start) | collective-permute-done | bytes 159776 | tf_op jit(solution)/shard_map/ppermute | solution.py:572
  14.6 5.6 %collective-permute-done.1.above_ref = f32[39,8,128]{2,1,0:T(8,128)S(1)} collective-permute-done((f32[39,8,128]{2,1,0:T(8,128)S(1)}, f32[39,8,128]{2,1,0:T(8,128)S(1)}, u32[]{:S(2)}, u32[]{:S(2)}) %collective-permute-start.1) | collective-permute-done | bytes 159776 | tf_op jit(solution)/shard_map/ppermute | solution.py:572
  20.2 0.6 %shard_map.60 = (f32[39,2,24,128]{3,2,1,0:T(8,128)S(1)}, f32[3,24,128]{2,1,0:T(8,128)S(1)}, f32[3,24,128]{2,1,0:T(8,128)S(1)}) custom-call(f32[19,2,16,128]{3,2,1,0:T(8,128)S(1)} %copy-done, f32[2,16,128]{2,1,0:T(8,128)S(1)} %copy-done.4, s32[2,16,128]{2,1,0:T(8,128)S(1)} %copy-done.2, f32[19,2,16,128]{3,2,1,0:T(8,128)S(1)} %copy-done.1, ...), custom_call_target="tpu_custom_call" | custom-call | flops 2000000 | bytes 1000000 | tf_op jit(solution)/shard_map/pallas_call | solution.py:587
  20.8 0.0 collective-permute-start.2
  20.8 2.9 %collective-permute-start.3 = (f32[3,24,128]{2,1,0:T(8,128)S(1)}, f32[3,24,128]{2,1,0:T(8,128)S(1)}, u32[]{:S(2)}, u32[]{:S(2)}) collective-permute-start(f32[3,24,128]{2,1,0:T(8,128)S(1)} %get-tuple-element.26), channel_id=1, source_target_pairs={{1,0},{2,1},{3,2},{4,3},{5,4},{6,5},{7,6},{8,7},{9,8},{10,9},{11,1... | collective-permute-start | bytes 110600 | tf_op jit(solution)/shard_map/ppermute | solution.py:572
  23.7 0.3 shard_map.61.g_ref
  24.0 1.4 %collective-permute-done.2.before_ref = f32[3,24,128]{2,1,0:T(8,128)S(1)} collective-permute-done((f32[3,24,128]{2,1,0:T(8,128)S(1)}, f32[3,24,128]{2,1,0:T(8,128)S(1)}, u32[]{:S(2)}, u32[]{:S(2)}) %collective-permute-start.2) | collective-permute-done | bytes 36896 | tf_op jit(solution)/shard_map/ppermute | solution.py:572
  25.4 0.0 collective-permute-done.3.beyond_ref
  25.4 1.2 %shard_map.62 = (f32[19,2,2,24,128]{4,3,2,1,0:T(8,128)S(1)}, f32[19,2,24,128]{3,2,1,0:T(8,128)S(1)}, f32[3,2,2,24,128]{4,3,2,1,0:T(8,128)S(1)}, f32[19,2,24,128]...) custom-call(f32[39,2,24,128]{3,2,1,0:T(8,128)S(1)} %get-tuple-element.2, ...), custom_call_target="tpu_custom_call" | custom-call | flops 2000000 | bytes 1000000 | tf_op jit(solution)/shard_map/pallas_call | solution.py:590
  26.6 3.3 %collective-permute-start.4 = (f32[21,24,128]{2,1,0:T(8,128)S(1)}, f32[21,24,128]{2,1,0:T(8,128)S(1)}, u32[]{:S(2)}, u32[]{:S(2)}) collective-permute-start(f32[21,24,128]{2,1,0:T(8,128)S(1)} %get-tuple-element.32), channel_id=1, source_target_pairs={{0,128},{128,256},{256,384},{384,0},{1,129},{129,257},{257,385},{3... | collective-permute-start | bytes 774152 | tf_op jit(solution)/shard_map/ppermute | solution.py:572
  29.9 3.8 %collective-permute-start.5 = (f32[21,24,128]{2,1,0:T(8,128)S(1)}, f32[21,24,128]{2,1,0:T(8,128)S(1)}, u32[]{:S(2)}, u32[]{:S(2)}) collective-permute-start(f32[21,24,128]{2,1,0:T(8,128)S(1)} %get-tuple-element.33), channel_id=1, source_target_pairs={{128,0},{256,128},{384,256},{0,384},{129,1},{257,129},{385,257},{1... | collective-permute-start | bytes 774152 | tf_op jit(solution)/shard_map/ppermute | solution.py:572
  33.6 0.2 shard_map.63.b2_ref
  33.8 2.2 %collective-permute-done.4.left_ref.left1_ref = f32[21,24,128]{2,1,0:T(8,128)S(1)} collective-permute-done((f32[21,24,128]{2,1,0:T(8,128)S(1)}, f32[21,24,128]{2,1,0:T(8,128)S(1)}, u32[]{:S(2)}, u32[]{:S(2)}) %collective-permute-start.4) | collective-permute-done | bytes 258080 | tf_op jit(solution)/shard_map/ppermute | solution.py:572
  36.0 2.1 %collective-permute-done.5.right_ref.right1_ref = f32[21,24,128]{2,1,0:T(8,128)S(1)} collective-permute-done((f32[21,24,128]{2,1,0:T(8,128)S(1)}, f32[21,24,128]{2,1,0:T(8,128)S(1)}, u32[]{:S(2)}, u32[]{:S(2)}) %collective-permute-start.5) | collective-permute-done | bytes 258080 | tf_op jit(solution)/shard_map/ppermute | solution.py:572
  38.1 2.8 %shard_map.64 = (f32[4,4,2,24,128]{4,3,2,1,0:T(8,128)S(1)}, f32[2,2,24,128]{3,2,1,0:T(8,128)S(1)}, f32[2,16,128]{2,1,0:T(8,128)S(1)}, f32[19,2,2,24,128]{4,3,2,1...) custom-call(f32[19,2,2,24,128]{4,3,2,1,0:T(8,128)S(1)} %get-tuple-el, ...), custom_call_target="tpu_custom_call" | custom-call | flops 2000000 | bytes 1000000 | tf_op jit(solution)/shard_map/pallas_call | solution.py:598
  40.8 3.4 %collective-permute-start.6 = (f32[15,24,128]{2,1,0:T(8,128)S(1)}, f32[15,24,128]{2,1,0:T(8,128)S(1)}, u32[]{:S(2)}, u32[]{:S(2)}) collective-permute-start(f32[15,24,128]{2,1,0:T(8,128)S(1)} %get-tuple-element.40), channel_id=1, source_target_pairs={{0,128},{128,256},{256,384},{384,0},{1,129},{129,257},{257,385},{3... | collective-permute-start | bytes 552968 | tf_op jit(solution)/shard_map/ppermute | solution.py:572
  44.3 3.7 %collective-permute-start.7 = (f32[15,24,128]{2,1,0:T(8,128)S(1)}, f32[15,24,128]{2,1,0:T(8,128)S(1)}, u32[]{:S(2)}, u32[]{:S(2)}) collective-permute-start(f32[15,24,128]{2,1,0:T(8,128)S(1)} %get-tuple-element.41), channel_id=1, source_target_pairs={{128,0},{256,128},{384,256},{0,384},{129,1},{257,129},{385,257},{1... | collective-permute-start | bytes 552968 | tf_op jit(solution)/shard_map/ppermute | solution.py:572
  47.9 1.6 %collective-permute-done.6.left_ref = f32[15,24,128]{2,1,0:T(8,128)S(1)} collective-permute-done((f32[15,24,128]{2,1,0:T(8,128)S(1)}, f32[15,24,128]{2,1,0:T(8,128)S(1)}, u32[]{:S(2)}, u32[]{:S(2)}) %collective-permute-start.6) | collective-permute-done | bytes 184352 | tf_op jit(solution)/shard_map/ppermute | solution.py:572
  49.5 2.2 %collective-permute-done.7.right_ref = f32[15,24,128]{2,1,0:T(8,128)S(1)} collective-permute-done((f32[15,24,128]{2,1,0:T(8,128)S(1)}, f32[15,24,128]{2,1,0:T(8,128)S(1)}, u32[]{:S(2)}, u32[]{:S(2)}) %collective-permute-start.7) | collective-permute-done | bytes 184352 | tf_op jit(solution)/shard_map/ppermute | solution.py:572
  51.7 0.0 copy-done.3
  51.7 2.1 %shard_map.65 = (f32[2,16,128]{2,1,0:T(8,128)}, f32[19,2,16,128]{3,2,1,0:T(8,128)}) custom-call(f32[19,2,2,24,128]{4,3,2,1,0:T(8,128)S(1)} %get-tuple-element.34.b1_ref, f32[19,2,24,128]{3,2,1,0:T(8,128)S(1)} %get-tuple-element.35.edge1_ref, f32[4,2,2,24,128]{4,3,2,1,0:T(8,128)S(1)} %get-tuple-element.36.sums_ref, ...), custom_call_target="tpu_custom_call" | custom-call | flops 2000000 | bytes 1000000 | tf_op jit(solution)/shard_map/pallas_call | solution.py:604
  (1 shorter events, 0.0 us)
Async XLA Ops:
  0.6 1.0 %copy-start = (f32[19,2,16,128]{3,2,1,0:T(8,128)S(1)}, f32[19,2,16,128]{3,2,1,0:T(8,128)}, u32[]{:S(2)}) copy-start(f32[19,2,16,128]{3,2,1,0:T(8,128)} %f_ref.3) | copy-start | bytes 933892
  1.6 1.0 %copy-start.1 = (f32[19,2,16,128]{3,2,1,0:T(8,128)S(1)}, f32[19,2,16,128]{3,2,1,0:T(8,128)}, u32[]{:S(2)}) copy-start(f32[19,2,16,128]{3,2,1,0:T(8,128)} %seed_ref.1) | copy-start | bytes 933892
  2.6 0.7 %copy-start.2 = (s32[2,16,128]{2,1,0:T(8,128)S(1)}, s32[2,16,128]{2,1,0:T(8,128)}, u32[]{:S(2)}) copy-start(s32[2,16,128]{2,1,0:T(8,128)} %solid_ref.3) | copy-start | bytes 49156
  3.3 0.7 %copy-start.4 = (f32[2,16,128]{2,1,0:T(8,128)S(1)}, f32[2,16,128]{2,1,0:T(8,128)}, u32[]{:S(2)}) copy-start(f32[2,16,128]{2,1,0:T(8,128)} %por_ref.1) | copy-start | bytes 49156
  4.3 10.3 %collective-permute-start = (f32[39,8,128]{2,1,0:T(8,128)S(1)}, f32[39,8,128]{2,1,0:T(8,128)S(1)}, u32[]{:S(2)}, u32[]{:S(2)}) collective-permute-start(f32[39,8,128]{2,1,0:T(8,128)S(1)} %get-tuple-element.22), channel_id=1, source_target_pairs={{0,32},{32,64},{64,96},{96,0},{1,33},{33,65},{65,97},{97,1},{2,34}... | collective-permute-start | bytes 479240 | tf_op jit(solution)/shard_map/ppermute | solution.py:572
  11.8 8.4 %collective-permute-start.1 = (f32[39,8,128]{2,1,0:T(8,128)S(1)}, f32[39,8,128]{2,1,0:T(8,128)S(1)}, u32[]{:S(2)}, u32[]{:S(2)}) collective-permute-start(f32[39,8,128]{2,1,0:T(8,128)S(1)} %get-tuple-element.23), channel_id=1, source_target_pairs={{32,0},{64,32},{96,64},{0,96},{33,1},{65,33},{97,65},{1,97},{34,2}... | collective-permute-start | bytes 479240 | tf_op jit(solution)/shard_map/ppermute | solution.py:572
  20.8 4.6 %collective-permute-start.2 = (f32[3,24,128]{2,1,0:T(8,128)S(1)}, f32[3,24,128]{2,1,0:T(8,128)S(1)}, u32[]{:S(2)}, u32[]{:S(2)}) collective-permute-start(f32[3,24,128]{2,1,0:T(8,128)S(1)} %get-tuple-element.25), channel_id=1, source_target_pairs={{0,1},{1,2},{2,3},{3,4},{4,5},{5,6},{6,7},{7,8},{8,9},{9,10},{10,1... | collective-permute-start | bytes 110600 | tf_op jit(solution)/shard_map/ppermute | solution.py:572
  20.8 4.6 %collective-permute-start.3 = (f32[3,24,128]{2,1,0:T(8,128)S(1)}, f32[3,24,128]{2,1,0:T(8,128)S(1)}, u32[]{:S(2)}, u32[]{:S(2)}) collective-permute-start(f32[3,24,128]{2,1,0:T(8,128)S(1)} %get-tuple-element.26), channel_id=1, source_target_pairs={{1,0},{2,1},{3,2},{4,3},{5,4},{6,5},{7,6},{8,7},{9,8},{10,9},{11,1... | collective-permute-start | bytes 110600 | tf_op jit(solution)/shard_map/ppermute | solution.py:572
  26.6 9.4 %collective-permute-start.4 = (f32[21,24,128]{2,1,0:T(8,128)S(1)}, f32[21,24,128]{2,1,0:T(8,128)S(1)}, u32[]{:S(2)}, u32[]{:S(2)}) collective-permute-start(f32[21,24,128]{2,1,0:T(8,128)S(1)} %get-tuple-element.32), channel_id=1, source_target_pairs={{0,128},{128,256},{256,384},{384,0},{1,129},{129,257},{257,385},{3... | collective-permute-start | bytes 774152 | tf_op jit(solution)/shard_map/ppermute | solution.py:572
  29.9 8.2 %collective-permute-start.5 = (f32[21,24,128]{2,1,0:T(8,128)S(1)}, f32[21,24,128]{2,1,0:T(8,128)S(1)}, u32[]{:S(2)}, u32[]{:S(2)}) collective-permute-start(f32[21,24,128]{2,1,0:T(8,128)S(1)} %get-tuple-element.33), channel_id=1, source_target_pairs={{128,0},{256,128},{384,256},{0,384},{129,1},{257,129},{385,257},{1... | collective-permute-start | bytes 774152 | tf_op jit(solution)/shard_map/ppermute | solution.py:572
  38.1 13.6 %copy-start.3 = (s32[2,16,128]{2,1,0:T(8,128)S(1)}, s32[2,16,128]{2,1,0:T(8,128)}, u32[]{:S(2)}) copy-start(s32[2,16,128]{2,1,0:T(8,128)} %solid_ref.3) | copy-start | bytes 49156
  40.8 8.6 %collective-permute-start.6 = (f32[15,24,128]{2,1,0:T(8,128)S(1)}, f32[15,24,128]{2,1,0:T(8,128)S(1)}, u32[]{:S(2)}, u32[]{:S(2)}) collective-permute-start(f32[15,24,128]{2,1,0:T(8,128)S(1)} %get-tuple-element.40), channel_id=1, source_target_pairs={{0,128},{128,256},{256,384},{384,0},{1,129},{129,257},{257,385},{3... | collective-permute-start | bytes 552968 | tf_op jit(solution)/shard_map/ppermute | solution.py:572
  44.3 7.4 %collective-permute-start.7 = (f32[15,24,128]{2,1,0:T(8,128)S(1)}, f32[15,24,128]{2,1,0:T(8,128)S(1)}, u32[]{:S(2)}, u32[]{:S(2)}) collective-permute-start(f32[15,24,128]{2,1,0:T(8,128)S(1)} %get-tuple-element.41), channel_id=1, source_target_pairs={{128,0},{256,128},{384,256},{0,384},{129,1},{257,129},{385,257},{1... | collective-permute-start | bytes 552968 | tf_op jit(solution)/shard_map/ppermute | solution.py:572

commit v3 on v2

--- a/solution.py
+++ b/solution.py
@@ -35,10 +35,9 @@
     return terms[0]
 
 
-def signed(values, axis):
-    plus = total(values[i] for i in range(Q) if VEL[i][axis] == 1)
-    minus = total(values[i] for i in range(Q) if VEL[i][axis] == -1)
-    return plus - minus
+ROOT = 4.5**0.5
+FACES = [i for i in PAIRS if i < 7]
+EDGES = [i for i in PAIRS if i >= 7]
 
 
 def project(vector, i):
@@ -54,96 +53,108 @@
     return out
 
 
-def moments(f):
-    rho = total(f)
+def gathered(terms, axis):
+    plus = [terms[i] for i in terms if VEL[i][axis] == 1]
+    minus = [terms[i] for i in terms if VEL[i][axis] == -1]
+    return total(plus) - total(minus) if minus else total(plus)
+
+
+def split(f, pairs=PAIRS):
+    return {i: f[i] + f[i + 1] for i in pairs}, {i: f[i] - f[i + 1] for i in pairs}
+
+
+def moments(f0, even, odd):
+    rho = f0 + total(even.values())
     inv = 1.0 / rho
-    return rho, [signed(f, axis) * inv for axis in range(3)]
-
-
-def moments_from(level, f):
-    plus, minus = total(f[i] for i in XP), total(f[i] for i in XM)
-    rho = level[0] + (plus + minus)
+    return rho, [gathered(odd, axis) * inv for axis in range(3)]
+
+
+def moments_from(level, even, odd):
+    rho = level[0] + total(even.values())
     inv = 1.0 / rho
-    along = [level[axis] + total(f[i] if VEL[i][axis] == 1 else -f[i] for i in XP + XM if VEL[i][axis]) for axis in (1, 2)]
-    return rho, [(plus - minus) * inv, along[0] * inv, along[1] * inv]
-
-
-def collide(f, rho, u, blocking, want):
+    return rho, [gathered(odd, 0) * inv] + [(level[axis] + gathered(odd, axis)) * inv for axis in (1, 2)]
+
+
+def weights(blocking):
     keep = 1.0 - blocking
     own = (1.0 - OMEGA) * keep
-    scale = OMEGA * keep * rho
-    base = 1.0 - 1.5 * (u[0] * u[0] + u[1] * u[1] + u[2] * u[2])
+    return 0.5 * (own + blocking), 0.5 * (own - blocking), OMEGA * keep
+
+
+def collide(f0, even, odd, rho, u, blocking, want):
+    k_even, k_odd, mix = weights(blocking)
+    scale = mix * rho
+    v = [ROOT * part for part in u]
+    squares = [part * part for part in v]
+    base = 1.0 - (1.0 / 3.0) * (squares[0] + squares[1] + squares[2])
     out = {}
     if 0 in want:
-        out[0] = (own + blocking) * f[0] + (WEIGHT[0] * scale) * base
-    for i in PAIRS:
-        j = i + 1
-        if i not in want and j not in want:
-            continue
-        s = WEIGHT[i] * scale
-        p = project(u, i)
-        even = s * (base + 4.5 * (p * p))
-        odd = s * (3.0 * p)
-        if i in want:
-            out[i] = own * f[i] + blocking * f[j] + (even + odd)
-        if j in want:
-            out[j] = own * f[j] + blocking * f[i] + (even - odd)
+        out[0] = (2.0 * k_even) * f0 + (WEIGHT[0] * scale) * base
+    for group in (FACES, EDGES):
+        s = WEIGHT[group[0]] * scale
+        s_odd = (2.0**0.5) * s
+        for i in group:
+            if i not in want and i + 1 not in want:
+                continue
+            p = project(v, i)
+            square = squares[VEL[i].index(1)] if i in FACES else p * p
+            p_even = k_even * even[i] + s * (base + square)
+            p_odd = k_odd * odd[i] + s_odd * p
+            if i in want:
+                out[i] = p_even + p_odd
+            if i + 1 in want:
+                out[i + 1] = p_even - p_odd
     return out
 
 
-def flow(b, u):
+def flow(b0, even, odd, u):
     base = 1.0 - 1.5 * (u[0] * u[0] + u[1] * u[1] + u[2] * u[2])
-    weighted, value, slope = [], [], [[], [], []]
-    if 0 in b:
-        weighted.append(WEIGHT[0] * b[0])
-    faces, edges = [], []
-    for i in PAIRS:
-        j = i + 1
-        if i not in b and j not in b:
-            continue
-        p = project(u, i)
-        if i in b and j in b:
-            even, odd = b[i] + b[j], b[i] - b[j]
-        elif i in b:
-            even, odd = b[i], b[i]
-        else:
-            even, odd = b[j], -b[j]
-        (faces if i < 7 else edges).append(even)
-        ps = p * even
-        d3 = 3.0 * odd
-        value.append((WEIGHT[i] * p) * (d3 + 4.5 * ps))
-        g = WEIGHT[i] * (d3 + 9.0 * ps)
+    q = [1.5 * part for part in u]
+    level = [] if b0 is None else [WEIGHT[0] * b0]
+    value, slope = [], [[], [], []]
+    for group in (FACES, EDGES):
+        group = [i for i in group if i in even]
+        w = WEIGHT[group[0]]
+        level.append(w * total(even[i] for i in group))
+        work, along = [], {}
+        for i in group:
+            p = project(q, i)
+            t = p * even[i]
+            h = odd[i] + t
+            work.append(p * h)
+            along[i] = h + t
+        value.append((2.0 * w) * total(work))
         for axis in range(3):
-            if VEL[i][axis]:
-                slope[axis].append(g if VEL[i][axis] == 1 else -g)
-    weighted = total(weighted + [WEIGHT[1] * total(faces), WEIGHT[7] * total(edges)])
-    return [base * weighted + total(value)] + [total(slope[axis]) - 3.0 * (u[axis] * weighted) for axis in range(3)]
-
-
-def back(b, sums, u, blocking, want):
+            if any(VEL[i][axis] for i in group):
+                slope[axis].append((3.0 * w) * gathered(along, axis))
+    level = total(level)
+    return [base * level + total(value)] + [total(slope[axis]) - 2.0 * (q[axis] * level) for axis in range(3)]
+
+
+def back(b0, even, odd, sums, u, blocking, want):
     energy, *v = sums
-    keep = 1.0 - blocking
-    own = (1.0 - OMEGA) * keep
-    mix = OMEGA * keep
+    k_even, k_odd, mix = weights(blocking)
     common = mix * (energy - (v[0] * u[0] + v[1] * u[1] + v[2] * u[2]))
     mv = [mix * v[axis] for axis in range(3)]
     out = {}
     if 0 in want:
-        out[0] = (own + blocking) * b[0] + common
+        out[0] = (2.0 * k_even) * b0 + common
     for i in PAIRS:
-        j = i + 1
-        if i not in want and j not in want:
+        if i not in want and i + 1 not in want:
             continue
-        p = project(mv, i)
+        p_even = k_even * even[i] + common
+        p_odd = k_odd * odd[i] + project(mv, i)
         if i in want:
-            out[i] = own * b[i] + blocking * b[j] + (common + p)
-        if j in want:
-            out[j] = own * b[j] + blocking * b[i] + (common - p)
+            out[i] = p_even + p_odd
+        if i + 1 in want:
+            out[i + 1] = p_even - p_odd
     return out
 
 
 def gradient_of(b, f, rho, energy):
-    return total(b[i] * (f[OPP[i]] - (1.0 - OMEGA) * f[i]) for i in range(Q)) - (OMEGA * rho) * energy
+    evens = total(b[1][i] * f[1][i] for i in PAIRS)
+    odds = total(b[2][i] * f[2][i] for i in PAIRS)
+    return OMEGA * (b[0] * f[0] - rho * energy) + (0.5 * OMEGA) * evens - (1.0 - 0.5 * OMEGA) * odds
 
 
 def column(shape):
@@ -167,33 +178,68 @@
     return main, rim
 
 
-def pack(ref, tiles):
-    n = len(tiles)
-    at = column((ROWS, LANES)) // 8
+def pack_rims(ref, place, tiles, width):
+    at = column((ROWS, LANES))
+    joined, first = None, 0
+    for k, (_, rim) in enumerate(tiles):
+        piece = turn(rim(), first + width[k] // 2, 1)
+        joined = piece if joined is None else jnp.where(at >= first, piece, joined)
+        first += width[k]
+    ref[place] = joined
+
+
+def unpack_rims(tile, width, out):
+    first = 0
+    for k in range(len(width)):
+        out(k, turn(tile, -(first + width[k] // 2), 1))
+        first += width[k]
+
+
+SEND1, SEND2 = 19, 14
+WIDTH1 = [6] * 14 + [4] * 5
+WIDTH2 = [2] * SEND2
+ROWTILES2 = 2 * SEND2 + -(-SEND2 // 4)
+
+
+def pack1(ref, tiles):
     for k, (main, _) in enumerate(tiles):
         ref[k] = main()
-    for first in range(0, n, 16):
-        joined = None
-        for k in range(first, min(first + 16, n)):
-            piece = turn(tiles[k][1](), 8 * (k - first) + 4, 1)
-            joined = piece if joined is None else jnp.where(at == k - first, piece, joined)
-        ref[n + first // 16] = joined
-
-
-def unpack(ref, n, k):
-    return ref[k], turn(ref[n + k // 16], -(8 * (k % 16) + 4), 1)
-
-
-def packed(n):
-    return n + -(-n // 16)
-
-
-def rims(ref, n, out_ref):
-    for k in range(n):
-        out_ref[k] = unpack(ref, n, k)[1]
-
-
-SEND1, SEND2 = 19, 14
+    pack_rims(ref, SEND1, tiles, WIDTH1)
+
+
+def unpack1(ref, rim_ref):
+    def out(k, rim):
+        rim_ref[k] = rim
+
+    unpack_rims(ref[SEND1], WIDTH1, out)
+
+
+def pack2(ref, rim_ref, tiles):
+    at = lax.broadcasted_iota(jnp.int32, (8, LANES), 0)
+    joined = None
+    for k, (main, _) in enumerate(tiles):
+        tile = main()
+        ref[2 * k], ref[2 * k + 1] = tile[0:8], tile[8:16]
+        slot = 2 * (k % 4)
+        piece = turn(tile[16:24], slot + 1, 0)
+        joined = piece if slot == 0 else jnp.where(at >= slot, piece, joined)
+        if slot == 6 or k == SEND2 - 1:
+            ref[2 * SEND2 + k // 4] = joined
+    pack_rims(rim_ref, 0, tiles, WIDTH2)
+    for k in range(3):
+        ref[ROWTILES2 + k] = rim_ref[0, 8 * k : 8 * k + 8, :]
+
+
+def unpack2(ref, out_ref):
+    for k in range(SEND2):
+        out_ref[k, 0, 0:8, :] = ref[2 * k]
+        out_ref[k, 0, 8:16, :] = ref[2 * k + 1]
+        out_ref[k, 0, 16:24, :] = turn(ref[2 * SEND2 + k // 4], -(2 * (k % 4) + 1), 0)
+
+    def out(k, rim):
+        out_ref[k, 1] = rim
+
+    unpack_rims(jnp.concatenate([ref[ROWTILES2 + k] for k in range(3)], axis=0), WIDTH2, out)
 
 
 def call(kernel, outs, scratch=(), more=(), space=None, cost=1000):
@@ -209,7 +255,7 @@
     )
 
 
-def rows_kernel(f_hbm, por_hbm, solid_hbm, seed_hbm, up_ref, down_ref, f_ref, por_ref, seed_ref, solid_ref, sems):
+def rows_kernel(f_hbm, por_hbm, solid_hbm, seed_hbm, up_ref, down_ref, f_ref, seed_ref, b_ref, por_ref, solid_ref, sems):
     copies = [
         pltpu.make_async_copy(src, dst, sems.at[k])
         for k, (src, dst) in enumerate(
@@ -219,25 +265,26 @@
     for copy in copies:
         copy.start()
 
-    def send(k, layer, tile):
-        up_ref[k, 4 * layer : 4 * layer + 4, :] = tile(12)
-        down_ref[k, 4 * layer : 4 * layer + 4, :] = tile(0)
+    def send(k, layer, ref, *where):
+        up_ref[k, 4 * layer : 4 * layer + 4, :] = ref[where + (slice(12, 16), slice(None))]
+        down_ref[k, 4 * layer : 4 * layer + 4, :] = ref[where + (slice(0, 4), slice(None))]
 
     copies[0].wait()
     for k in range(Q):
         for layer in range(2):
-            send(k, layer, lambda row: f_ref[k, layer, row : row + 4, :])
+            send(k, layer, f_ref, k, layer)
     copies[1].wait()
     for k in range(Q):
         for layer in range(2):
-            send(k + Q, layer, lambda row: seed_ref[k, layer, row : row + 4, :])
+            send(k + Q, layer, seed_ref, k, layer)
     copies[2].wait()
     copies[3].wait()
     for layer in range(2):
-        send(2 * Q, layer, lambda row: jnp.where(solid_ref[layer, row : row + 4, :] == 1, 1.0, por_ref[layer, row : row + 4, :]))
-
-
-def columns_kernel(f_ref, por_ref, solid_ref, seed_ref, below_ref, above_ref, main_ref, up_ref, down_ref):
+        b_ref[layer] = jnp.where(solid_ref[layer] == 1, 1.0, por_ref[layer])
+        send(2 * Q, layer, b_ref, layer)
+
+
+def columns_kernel(f_ref, seed_ref, b_ref, below_ref, above_ref, main_ref, up_ref, down_ref):
     at = column((ROWS, LANES)) // 4
     high = low = None
     for k in range(FIELDS):
@@ -247,7 +294,7 @@
             elif k < 2 * Q:
                 own = seed_ref[k - Q, layer]
             else:
-                own = jnp.where(solid_ref[layer] == 1, 1.0, por_ref[layer])
+                own = b_ref[layer]
             rows = slice(4 * layer, 4 * layer + 4)
             tile = jnp.concatenate([own, above_ref[k, rows, :], below_ref[k, rows, :]], axis=0)
             main_ref[k, layer] = tile
@@ -273,8 +320,9 @@
 
         def body(_, row, layer=layer):
             f = [main_ref[i, layer, pl.ds(row, 8), :] for i in range(Q)]
-            rho, u = moments(f)
-            g = collide(f, rho, u, main_ref[2 * Q, layer, pl.ds(row, 8), :], range(Q))
+            even, odd = split(f)
+            rho, u = moments(f[0], even, odd)
+            g = collide(f[0], even, odd, rho, u, main_ref[2 * Q, layer, pl.ds(row, 8), :], range(Q))
             for i in range(Q):
                 g_ref[i, layer, pl.ds(row, 8), :] = g[i]
 
@@ -306,8 +354,9 @@
 
         def body(_, row, layer=layer):
             f = [f_scr[i, layer, pl.ds(row, 8), :] for i in range(Q)]
-            rho, u = moments(f)
-            g = collide(f, rho, u, b_ref[layer, 1, pl.ds(row, 8), :], range(Q))
+            even, odd = split(f)
+            rho, u = moments(f[0], even, odd)
+            g = collide(f[0], even, odd, rho, u, b_ref[layer, 1, pl.ds(row, 8), :], range(Q))
             for i in range(Q):
                 g_scr[i, layer, pl.ds(row, 8), :] = g[i]
 
@@ -344,8 +393,8 @@
             out.append(((lambda pair=pair: pair[0]), (lambda pair=pair: pair[1])))
         return out
 
-    pack(up_ref, tiles_of(XP, XM, 1))
-    pack(down_ref, tiles_of(XM, XP, 0))
+    pack1(up_ref, tiles_of(XP, XM, 1))
+    pack1(down_ref, tiles_of(XM, XP, 0))
 
 
 def seed_kernel(main_ref, s_ref, b2_ref):
@@ -361,10 +410,10 @@
 def middle_kernel(
     f1_ref, edge_ref, level_ref, b_ref, b2_ref, left_ref, right_ref,
     mom_ref, bh_ref, grad_ref, b1_ref, edge1_ref, sums_ref, up_ref, down_ref,
-    l_scr, r_scr, g_scr, f_scr, a_scr,
+    l_scr, r_scr, g_scr, f_scr, a_scr, rim_scr,
 ):
-    rims(left_ref, SEND1, l_scr)
-    rims(right_ref, SEND1, r_scr)
+    unpack1(left_ref, l_scr)
+    unpack1(right_ref, r_scr)
     got = ((left_ref, right_ref), (l_scr, r_scr))
     for side in range(2):
         for lane in range(2):
@@ -379,11 +428,12 @@
                 f = [None if i in missing else f1_ref[i, layer, lane, rows, :] for i in range(Q)]
                 for k, i in enumerate(missing):
                     f[i] = got[lane][layer][9 + k, rows, :]
-                rho, u = moments_from([level_ref[k, layer, lane, rows, :] for k in range(3)], f)
+                even, odd = split(f)
+                rho, u = moments(f[0], even, odd)
                 mom_ref[3, layer + 1, lane, rows, :] = rho
                 for axis in range(3):
                     mom_ref[axis, layer + 1, lane, rows, :] = u[axis]
-                g = collide(f, rho, u, b_ref[layer, lane, rows, :], range(Q))
+                g = collide(f[0], even, odd, rho, u, b_ref[layer, lane, rows, :], range(Q))
                 for i in range(Q):
                     g_scr[i, layer + 1, lane, rows, :] = g[i]
 
@@ -400,10 +450,11 @@
                     f[i] = got[lane][side][k, rows, :]
                 for i in ours:
                     f[i] = edge_ref[i, lane, rows, :]
-                rho, u = moments_from([got[lane][side][5 + k, rows, :] for k in range(3)], f)
+                even, odd = split(f, XP)
+                rho, u = moments_from([got[lane][side][5 + k, rows, :] for k in range(3)], even, odd)
                 for axis in range(3):
                     mom_ref[axis, 3 * side, lane, rows, :] = u[axis]
-                g = collide(f, rho, u, got[lane][side][8, rows, :], theirs)
+                g = collide(None, even, odd, rho, u, got[lane][side][8, rows, :], theirs)
                 for i in theirs:
                     g_scr[i, 3 * side, lane, rows, :] = g[i]
 
@@ -426,13 +477,15 @@
                 b = {i: b2_ref[i, layer, lane, rows, :] for i in range(Q) if i not in missing}
                 for k, i in enumerate(missing):
                     b[i] = got[lane][layer][14 + k, rows, :]
-                rho, u = moments(f)
-                sums = flow(b, u)
-                a = back(b, sums, u, b_ref[layer, lane, rows, :], range(Q))
+                even, odd = split(f)
+                rho, u = moments(f[0], even, odd)
+                b_even, b_odd = split(b)
+                sums = flow(b[0], b_even, b_odd, u)
+                a = back(b[0], b_even, b_odd, sums, u, b_ref[layer, lane, rows, :], range(Q))
                 for i in range(Q):
                     a_scr[i, layer, lane, rows, :] = a[i]
                 if own:
-                    grad_ref[layer, rows, :] = gradient_of(b, f, rho, sums[0])
+                    grad_ref[layer, rows, :] = gradient_of((b[0], b_even, b_odd), (f[0], even, odd), rho, sums[0])
 
             if lane == 0:
 
@@ -462,7 +515,10 @@
                 rows = pl.ds(row, 8)
                 missing = XM if layer == 0 else XP
                 b = {i: b1_ref[i, layer, lane, rows, :] for i in range(Q) if i not in missing}
-                sums = flow(b, [mom_ref[axis, layer + 1, lane, rows, :] for axis in range(3)])
+                even, odd = split(b, [i for i in PAIRS if i in X0])
+                for i in XP:
+                    even[i], odd[i] = (b[i], b[i]) if layer == 0 else (b[i + 1], -b[i + 1])
+                sums = flow(b[0], even, odd, [mom_ref[axis, layer + 1, lane, rows, :] for axis in range(3)])
                 for k in range(4):
                     sums_ref[k, layer, lane, rows, :] = sums[k]
 
@@ -478,8 +534,8 @@
             + [pick(sums_ref, k, layer) for k in range(4)]
         )
 
-    pack(up_ref, tiles_of(XM, 1))
-    pack(down_ref, tiles_of(XP, 0))
+    pack2(up_ref, rim_scr, tiles_of(XM, 1))
+    pack2(down_ref, rim_scr, tiles_of(XP, 0))
 
 
 def last_kernel(
@@ -487,9 +543,9 @@
     out_grad_ref, out_ref,
     l_scr, r_scr, a_scr, b0_scr,
 ):
-    rims(left_ref, SEND2, l_scr)
-    rims(right_ref, SEND2, r_scr)
-    got = ((left_ref, right_ref), (l_scr, r_scr))
+    unpack2(left_ref, l_scr)
+    unpack2(right_ref, r_scr)
+    got = (l_scr, r_scr)
     got1 = (left1_ref, right1_ref)
 
     for layer in range(2):
@@ -498,19 +554,22 @@
             def body(row, layer=layer, lane=lane, own=False):
                 rows = pl.ds(row, 8)
                 missing = XM if layer == 0 else XP
-                new = {i: got[lane][layer][k, rows, :] for k, i in enumerate(missing)}
                 b = {i: b1_ref[i, layer, lane, rows, :] for i in range(Q) if i not in missing}
-                b.update(new)
+                for k, i in enumerate(missing):
+                    b[i] = got[layer][k, lane, rows, :]
+                new_even = {i: b[i + 1] if layer == 0 else b[i] for i in XP}
+                new_odd = {i: -b[i + 1] if layer == 0 else b[i] for i in XP}
+                even, odd = split(b)
                 u = [mom_ref[axis, layer + 1, lane, rows, :] for axis in range(3)]
-                sums = [sums_ref[k, layer, lane, rows, :] + part for k, part in enumerate(flow(new, u))]
-                a = back(b, sums, u, b_ref[layer, lane, rows, :], range(Q))
+                sums = [sums_ref[k, layer, lane, rows, :] + part for k, part in enumerate(flow(None, new_even, new_odd, u))]
+                a = back(b[0], even, odd, sums, u, b_ref[layer, lane, rows, :], range(Q))
                 for i in range(Q):
                     a_scr[i, layer + 1, lane, rows, :] = a[i]
                 if own:
                     f = {i: f1_ref[i, layer, lane, rows, :] for i in range(Q) if OPP[i] not in missing}
                     for k, i in enumerate(XP if layer == 0 else XM):
                         f[i] = got1[layer][9 + k, rows, :]
-                    grad = gradient_of(b, f, mom_ref[3, layer + 1, lane, rows, :], sums[0])
+                    grad = gradient_of((b[0], even, odd), (f[0],) + split(f), mom_ref[3, layer + 1, lane, rows, :], sums[0])
                     out_grad_ref[layer, rows, :] = grad + grad_ref[layer, rows, :]
 
             if lane == 0:
@@ -530,13 +589,15 @@
             def body(_, row, side=side, lane=lane):
                 rows = pl.ds(row, 8)
                 theirs, ours = (XM, XP) if side == 0 else (XP, XM)
-                new = {i: edge1_ref[i, lane, rows, :] for i in ours}
-                b = dict(new)
+                b = {i: edge1_ref[i, lane, rows, :] for i in ours}
                 for k, i in enumerate(theirs):
-                    b[i] = got[lane][side][5 + k, rows, :]
+                    b[i] = got[side][5 + k, lane, rows, :]
+                new_even = {i: b[i] if side == 0 else b[i + 1] for i in XP}
+                new_odd = {i: b[i] if side == 0 else -b[i + 1] for i in XP}
+                even, odd = split(b, XP)
                 u = [mom_ref[axis, 3 * side, lane, rows, :] for axis in range(3)]
-                sums = [got[lane][side][10 + k, rows, :] + part for k, part in enumerate(flow(new, u))]
-                a = back(b, sums, u, bh_ref[side, lane, rows, :], theirs)
+                sums = [got[side][10 + k, lane, rows, :] + part for k, part in enumerate(flow(None, new_even, new_odd, u))]
+                a = back(None, even, odd, sums, u, bh_ref[side, lane, rows, :], theirs)
                 for i in theirs:
                     a_scr[i, 3 * side, lane, rows, :] = a[i]
 
@@ -554,16 +615,22 @@
             rows = pl.ds(pl.multiple_of(n * 8, 8), 8)
             f = [f_ref[i, layer, rows, :] for i in range(Q)]
             b = {i: b0_scr[i, layer, rows, :] for i in range(Q)}
-            rho, u = moments(f)
-            sums = flow(b, u)
-            a = back(b, sums, u, b_ref[layer, 0, rows, :], range(Q))
+            even, odd = split(f)
+            rho, u = moments(f[0], even, odd)
+            b_even, b_odd = split(b)
+            sums = flow(b[0], b_even, b_odd, u)
+            a = back(b[0], b_even, b_odd, sums, u, b_ref[layer, 0, rows, :], range(Q))
             for i in range(Q):
                 out_ref[i, layer, rows, :] = a[i]
-            grad = gradient_of(b, f, rho, sums[0]) + out_grad_ref[layer, rows, :]
+            grad = gradient_of((b[0], b_even, b_odd), (f[0], even, odd), rho, sums[0]) + out_grad_ref[layer, rows, :]
             out_grad_ref[layer, rows, :] = jnp.where(solid_ref[layer, rows, :] == 1, 0.0, grad)
             return carry
 
         lax.fori_loop(0, 2, final, 0)
+
+
+def placed(x):
+    return x if INTERPRET else pltpu.with_memory_space_constraint(x, pltpu.HBM)
 
 
 def both_ways(up, down, axis):
@@ -574,22 +641,22 @@
 
 def body(populations, porosity, solid, seed_adjoint):
     half, tile = (2, 2, ROWS, LANES), (ROWS, LANES)
-    inputs = (populations, porosity, solid, seed_adjoint)
+    inputs = [placed(x) for x in (populations, porosity, solid, seed_adjoint)]
     block = populations.shape
-    up, down = call(
+    up, down, f, seed, b = call(
         rows_kernel,
-        [(FIELDS, 8, LANES)] * 2,
-        [block, block[1:], block],
+        [(FIELDS, 8, LANES)] * 2 + [block, block, block[1:]],
+        [block[1:]],
         [pltpu.VMEM(block[1:], jnp.int32), pltpu.SemaphoreType.DMA((4,))],
         space=[pltpu.HBM] * 4,
     )(*inputs)
     below, above = both_ways(up, down, "gy")
-    main, up, down = call(columns_kernel, [(FIELDS, 2) + tile] + [(ZTILES,) + tile] * 2)(*inputs, below, above)
+    main, up, down = call(columns_kernel, [(FIELDS, 2) + tile] + [(ZTILES,) + tile] * 2)(f, seed, b, below, above)
     before, beyond = both_ways(up, down, "gz")
     (g,) = call(main_kernel, [(Q, 2) + tile])(main)
     f1, edge, level, s, b, up, down = call(
         first_kernel,
-        [(Q,) + half, (Q, 2) + tile, (3,) + half, (Q, 2) + tile, half] + [(packed(SEND1),) + tile] * 2,
+        [(Q,) + half, (Q, 2) + tile, (3,) + half, (Q, 2) + tile, half] + [(SEND1 + 1,) + tile] * 2,
         [(Q, 2) + tile] * 2,
     )(main, g, before, beyond)
     left1, right1 = both_ways(up, down, "gx")
@@ -597,15 +664,15 @@
     wide = (4, 2) + tile
     mom, bh, grad, b1, edge1, sums, up, down = call(
         middle_kernel,
-        [(4,) + wide, half, (2, OWN, LANES), (Q,) + half, (Q, 2) + tile, (4,) + half] + [(packed(SEND2),) + tile] * 2,
-        [(SEND1,) + tile] * 2 + [(Q,) + wide, (Q,) + half, (Q,) + half],
+        [(4,) + wide, half, (2, OWN, LANES), (Q,) + half, (Q, 2) + tile, (4,) + half] + [(ROWTILES2 + 3, 8, LANES)] * 2,
+        [(SEND1,) + tile] * 2 + [(Q,) + wide, (Q,) + half, (Q,) + half, (1,) + tile],
     )(f1, edge, level, b, b2, left1, right1)
     left, right = both_ways(up, down, "gx")
     gradient, adjoint_out = call(
         last_kernel,
         [(2, OWN, LANES), (Q, 2, OWN, LANES)],
-        [(SEND2,) + tile] * 2 + [(Q,) + wide, (Q, 2, OWN, LANES)],
-    )(b1, edge1, sums, mom, b, bh, f1, left1, right1, grad, left, right, populations, solid)
+        [(SEND2, 2) + tile] * 2 + [(Q,) + wide, (Q, 2, OWN, LANES)],
+    )(b1, edge1, sums, mom, b, bh, f1, left1, right1, grad, left, right, f, solid)
     return gradient, adjoint_out
 
 

time: 54.5 us -> 50.9 us (0.934)
  local copies, waits for them, and re-layouts: 3.36 us -> 0.01 us
  waiting for transfers between devices: 15.9 us -> 15.3 us
  Pallas kernels: 7.37 us -> 7.93 us
    unnamed x10 -> x2, local copies, waits for them, and re-layouts: 3.36 us -> 0.01 us
    pallas_call x2, Pallas kernels: 2.43 us -> 3.2 us  [the longest x1 2.06 us: body(): call(last_kernel, [(2, OWN, LANES), (Q, 2, OWN, LANES)], [(SEND2, 2) + ti...]
    ppermute x4, waiting for transfers between devices: 5.99 us -> 5.44 us  [both_ways(): lax.ppermute(up, axis, ring)]
where the time goes in v3:
time: 50.9 us; the launch traced here: 50.5 us
  starting transfers between devices  26.5 us (52%)
  waiting for transfers between devices  15.3 us (30%)
  Pallas kernels  7.93 us (16%)
  between operations  0.72 us (1%)
    ppermute x4, starting transfers between devices, both_ways(): lax.ppermute(up, axis, ring)  14.2 us
    ppermute x4, starting transfers between devices, both_ways(): lax.ppermute(down, axis, [(j, i) for i, j in ring])  12.3 us
    ppermute x4, waiting for transfers between devices, both_ways(): lax.ppermute(down, axis, [(j, i) for i, j in ring])  9.88 us
    ppermute x4, waiting for transfers between devices, both_ways(): lax.ppermute(up, axis, ring)  5.44 us
    pallas_call x1, Pallas kernels, body(): call(middle_kernel, [(4,) + wide, half, (2, OWN, LANES), (Q,) + half, (Q,...  2.6 us
    pallas_call x1, Pallas kernels, body(): call(last_kernel, [(2, OWN, LANES), (Q, 2, OWN, LANES)], [(SEND2, 2) + ti...  2.06 us
    pallas_call x1, Pallas kernels, body(): call(first_kernel, [(Q,) + half, (Q, 2) + tile, (3,) + half, (Q, 2) + til...  1.16 us
    pallas_call x1, Pallas kernels, body(): call(rows_kernel, [(FIELDS, 8, LANES)] * 2 + [block, block, block[1:]], [...  1.14 us
  transfers between devices with their start and end apart: 8, of which 7 were waited for; matrix products, arithmetic and copies ran while one was open for 0% of the time, Pallas kernels for 1%

profile of v3, /device:TPU:24, one launch (start us, length us, event | category | flops | bytes accessed | tf_op | source)
XLA Modules:
  0.0 50.5 jit_solution(7130114054869438187)
XLA Ops:
  0.6 1.1 %shard_map.59 = (f32[39,8,128]{2,1,0:T(8,128)S(1)}, f32[39,8,128]{2,1,0:T(8,128)S(1)}, f32[19,2,16,128]{3,2,1,0:T(8,128)S(1)}, f32[19,2,16,128]{3,2,1,0:T(8,128)S(1)}, f32[2,16,128]{2,1,0:T(8,128)S(1)}) custom-call(f32[19,2,16,128]{3,2,1,0:T(8,128)} %f_hbm.1, f32[2,16,128]{2,1,0:T(8,128)} %por_hbm.1, s32[2,16,128]{2,1,0:T(8,128)} %solid_ref.1, ...), custom_call_target="tpu_custom_call" | custom-call | flops 2000000 | bytes 1000000 | tf_op jit(solution)/shard_map/pallas_call | solution.py:646
  1.8 7.5 %collective-permute-start = (f32[39,8,128]{2,1,0:T(8,128)S(1)}, f32[39,8,128]{2,1,0:T(8,128)S(1)}, u32[]{:S(2)}, u32[]{:S(2)}) collective-permute-start(f32[39,8,128]{2,1,0:T(8,128)S(1)} %get-tuple-element.28), channel_id=1, source_target_pairs={{0,32},{32,64},{64,96},{96,0},{1,33},{33,65},{65,97},{97,1},{2,34}... | collective-permute-start | bytes 479240 | tf_op jit(solution)/shard_map/ppermute | solution.py:639
  9.3 1.9 %collective-permute-start.1 = (f32[39,8,128]{2,1,0:T(8,128)S(1)}, f32[39,8,128]{2,1,0:T(8,128)S(1)}, u32[]{:S(2)}, u32[]{:S(2)}) collective-permute-start(f32[39,8,128]{2,1,0:T(8,128)S(1)} %get-tuple-element.29), channel_id=1, source_target_pairs={{32,0},{64,32},{96,64},{0,96},{33,1},{65,33},{97,65},{1,97},{34,2}... | collective-permute-start | bytes 479240 | tf_op jit(solution)/shard_map/ppermute | solution.py:639
  11.2 0.8 %collective-permute-done.below_ref = f32[39,8,128]{2,1,0:T(8,128)S(1)} collective-permute-done((f32[39,8,128]{2,1,0:T(8,128)S(1)}, f32[39,8,128]{2,1,0:T(8,128)S(1)}, u32[]{:S(2)}, u32[]{:S(2)}) %collective-permute-start) | collective-permute-done | bytes 159776 | tf_op jit(solution)/shard_map/ppermute | solution.py:639
  12.1 5.6 %collective-permute-done.1.above_ref = f32[39,8,128]{2,1,0:T(8,128)S(1)} collective-permute-done((f32[39,8,128]{2,1,0:T(8,128)S(1)}, f32[39,8,128]{2,1,0:T(8,128)S(1)}, u32[]{:S(2)}, u32[]{:S(2)}) %collective-permute-start.1) | collective-permute-done | bytes 159776 | tf_op jit(solution)/shard_map/ppermute | solution.py:639
  17.7 0.6 %shard_map.60 = (f32[39,2,24,128]{3,2,1,0:T(8,128)S(1)}, f32[3,24,128]{2,1,0:T(8,128)S(1)}, f32[3,24,128]{2,1,0:T(8,128)S(1)}) custom-call(f32[19,2,16,128]{3,2,1,0:T(8,128)S(1)} %get-tuple-element.25.f_ref, f32[19,2,16,128]{3,2,1,0:T(8,128)S(1)} %get-tuple-element.26.seed_ref, f32[2,16,128]{2,1,0:T(8,128)S(1)} %get-tuple-element.27.b_ref, ...), custom_call_target="tpu_custom_call" | custom-call | flops 2000000 | bytes 1000000 | tf_op jit(solution)/shard_map/pallas_call | solution.py:654
  18.2 0.0 collective-permute-start.2
  18.3 2.9 %collective-permute-start.3 = (f32[3,24,128]{2,1,0:T(8,128)S(1)}, f32[3,24,128]{2,1,0:T(8,128)S(1)}, u32[]{:S(2)}, u32[]{:S(2)}) collective-permute-start(f32[3,24,128]{2,1,0:T(8,128)S(1)} %get-tuple-element.32), channel_id=1, source_target_pairs={{1,0},{2,1},{3,2},{4,3},{5,4},{6,5},{7,6},{8,7},{9,8},{10,9},{11,1... | collective-permute-start | bytes 110600 | tf_op jit(solution)/shard_map/ppermute | solution.py:639
  21.2 0.2 shard_map.61.g_ref
  21.4 1.4 %collective-permute-done.2.before_ref = f32[3,24,128]{2,1,0:T(8,128)S(1)} collective-permute-done((f32[3,24,128]{2,1,0:T(8,128)S(1)}, f32[3,24,128]{2,1,0:T(8,128)S(1)}, u32[]{:S(2)}, u32[]{:S(2)}) %collective-permute-start.2) | collective-permute-done | bytes 36896 | tf_op jit(solution)/shard_map/ppermute | solution.py:639
  22.9 0.0 collective-permute-done.3.beyond_ref
  22.9 1.2 %shard_map.62 = (f32[19,2,2,24,128]{4,3,2,1,0:T(8,128)S(1)}, f32[19,2,24,128]{3,2,1,0:T(8,128)S(1)}, f32[3,2,2,24,128]{4,3,2,1,0:T(8,128)S(1)}, f32[19,2,24,128]...) custom-call(f32[39,2,24,128]{3,2,1,0:T(8,128)S(1)} %get-tuple-element.3, ...), custom_call_target="tpu_custom_call" | custom-call | flops 2000000 | bytes 1000000 | tf_op jit(solution)/shard_map/pallas_call | solution.py:657
  24.0 3.3 %collective-permute-start.4 = (f32[20,24,128]{2,1,0:T(8,128)S(1)}, f32[20,24,128]{2,1,0:T(8,128)S(1)}, u32[]{:S(2)}, u32[]{:S(2)}) collective-permute-start(f32[20,24,128]{2,1,0:T(8,128)S(1)} %get-tuple-element.38), channel_id=1, source_target_pairs={{0,128},{128,256},{256,384},{384,0},{1,129},{129,257},{257,385},{3... | collective-permute-start | bytes 737288 | tf_op jit(solution)/shard_map/ppermute | solution.py:639
  27.3 3.8 %collective-permute-start.5 = (f32[20,24,128]{2,1,0:T(8,128)S(1)}, f32[20,24,128]{2,1,0:T(8,128)S(1)}, u32[]{:S(2)}, u32[]{:S(2)}) collective-permute-start(f32[20,24,128]{2,1,0:T(8,128)S(1)} %get-tuple-element.39), channel_id=1, source_target_pairs={{128,0},{256,128},{384,256},{0,384},{129,1},{257,129},{385,257},{1... | collective-permute-start | bytes 737288 | tf_op jit(solution)/shard_map/ppermute | solution.py:639
  31.1 0.2 shard_map.63.b2_ref
  31.3 2.1 %collective-permute-done.4.left_ref.left1_ref = f32[20,24,128]{2,1,0:T(8,128)S(1)} collective-permute-done((f32[20,24,128]{2,1,0:T(8,128)S(1)}, f32[20,24,128]{2,1,0:T(8,128)S(1)}, u32[]{:S(2)}, u32[]{:S(2)}) %collective-permute-start.4) | collective-permute-done | bytes 245792 | tf_op jit(solution)/shard_map/ppermute | solution.py:639
  33.3 2.1 %collective-permute-done.5.right_ref.right1_ref = f32[20,24,128]{2,1,0:T(8,128)S(1)} collective-permute-done((f32[20,24,128]{2,1,0:T(8,128)S(1)}, f32[20,24,128]{2,1,0:T(8,128)S(1)}, u32[]{:S(2)}, u32[]{:S(2)}) %collective-permute-start.5) | collective-permute-done | bytes 245792 | tf_op jit(solution)/shard_map/ppermute | solution.py:639
  35.4 0.0 copy-start
  35.4 2.6 %shard_map.64 = (f32[4,4,2,24,128]{4,3,2,1,0:T(8,128)S(1)}, f32[2,2,24,128]{3,2,1,0:T(8,128)S(1)}, f32[2,16,128]{2,1,0:T(8,128)S(1)}, f32[19,2,2,24,128]{4,3,2,1...) custom-call(f32[19,2,2,24,128]{4,3,2,1,0:T(8,128)S(1)} %get-tuple-el, ...), custom_call_target="tpu_custom_call" | custom-call | flops 2000000 | bytes 1000000 | tf_op jit(solution)/shard_map/pallas_call | solution.py:665
  38.0 3.4 %collective-permute-start.6 = (f32[35,8,128]{2,1,0:T(8,128)S(1)}, f32[35,8,128]{2,1,0:T(8,128)S(1)}, u32[]{:S(2)}, u32[]{:S(2)}) collective-permute-start(f32[35,8,128]{2,1,0:T(8,128)S(1)} %get-tuple-element.46), channel_id=1, source_target_pairs={{0,128},{128,256},{256,384},{384,0},{1,129},{129,257},{257,385},{3... | collective-permute-start | bytes 430088 | tf_op jit(solution)/shard_map/ppermute | solution.py:639
  41.4 3.7 %collective-permute-start.7 = (f32[35,8,128]{2,1,0:T(8,128)S(1)}, f32[35,8,128]{2,1,0:T(8,128)S(1)}, u32[]{:S(2)}, u32[]{:S(2)}) collective-permute-start(f32[35,8,128]{2,1,0:T(8,128)S(1)} %get-tuple-element.47), channel_id=1, source_target_pairs={{128,0},{256,128},{384,256},{0,384},{129,1},{257,129},{385,257},{1... | collective-permute-start | bytes 430088 | tf_op jit(solution)/shard_map/ppermute | solution.py:639
  45.1 1.1 %collective-permute-done.6.left_ref = f32[35,8,128]{2,1,0:T(8,128)S(1)} collective-permute-done((f32[35,8,128]{2,1,0:T(8,128)S(1)}, f32[35,8,128]{2,1,0:T(8,128)S(1)}, u32[]{:S(2)}, u32[]{:S(2)}) %collective-permute-start.6) | collective-permute-done | bytes 143392 | tf_op jit(solution)/shard_map/ppermute | solution.py:639
  46.2 2.2 %collective-permute-done.7.right_ref = f32[35,8,128]{2,1,0:T(8,128)S(1)} collective-permute-done((f32[35,8,128]{2,1,0:T(8,128)S(1)}, f32[35,8,128]{2,1,0:T(8,128)S(1)}, u32[]{:S(2)}, u32[]{:S(2)}) %collective-permute-start.7) | collective-permute-done | bytes 143392 | tf_op jit(solution)/shard_map/ppermute | solution.py:639
  48.4 0.0 copy-done
  48.4 2.1 %shard_map.65 = (f32[2,16,128]{2,1,0:T(8,128)}, f32[19,2,16,128]{3,2,1,0:T(8,128)}) custom-call(f32[19,2,2,24,128]{4,3,2,1,0:T(8,128)S(1)} %get-tuple-element.40.b1_ref, f32[19,2,24,128]{3,2,1,0:T(8,128)S(1)} %get-tuple-element.41.edge1_ref, f32[4,2,2,24,128]{4,3,2,1,0:T(8,128)S(1)} %get-tuple-element.42.sums_ref, ...), custom_call_target="tpu_custom_call" | custom-call | flops 2000000 | bytes 1000000 | tf_op jit(solution)/shard_map/pallas_call | solution.py:671
Async XLA Ops:
  1.8 10.3 %collective-permute-start = (f32[39,8,128]{2,1,0:T(8,128)S(1)}, f32[39,8,128]{2,1,0:T(8,128)S(1)}, u32[]{:S(2)}, u32[]{:S(2)}) collective-permute-start(f32[39,8,128]{2,1,0:T(8,128)S(1)} %get-tuple-element.28), channel_id=1, source_target_pairs={{0,32},{32,64},{64,96},{96,0},{1,33},{33,65},{65,97},{97,1},{2,34}... | collective-permute-start | bytes 479240 | tf_op jit(solution)/shard_map/ppermute | solution.py:639
  9.3 8.4 %collective-permute-start.1 = (f32[39,8,128]{2,1,0:T(8,128)S(1)}, f32[39,8,128]{2,1,0:T(8,128)S(1)}, u32[]{:S(2)}, u32[]{:S(2)}) collective-permute-start(f32[39,8,128]{2,1,0:T(8,128)S(1)} %get-tuple-element.29), channel_id=1, source_target_pairs={{32,0},{64,32},{96,64},{0,96},{33,1},{65,33},{97,65},{1,97},{34,2}... | collective-permute-start | bytes 479240 | tf_op jit(solution)/shard_map/ppermute | solution.py:639
  18.2 4.6 %collective-permute-start.2 = (f32[3,24,128]{2,1,0:T(8,128)S(1)}, f32[3,24,128]{2,1,0:T(8,128)S(1)}, u32[]{:S(2)}, u32[]{:S(2)}) collective-permute-start(f32[3,24,128]{2,1,0:T(8,128)S(1)} %get-tuple-element.31), channel_id=1, source_target_pairs={{0,1},{1,2},{2,3},{3,4},{4,5},{5,6},{6,7},{7,8},{8,9},{9,10},{10,1... | collective-permute-start | bytes 110600 | tf_op jit(solution)/shard_map/ppermute | solution.py:639
  18.3 4.6 %collective-permute-start.3 = (f32[3,24,128]{2,1,0:T(8,128)S(1)}, f32[3,24,128]{2,1,0:T(8,128)S(1)}, u32[]{:S(2)}, u32[]{:S(2)}) collective-permute-start(f32[3,24,128]{2,1,0:T(8,128)S(1)} %get-tuple-element.32), channel_id=1, source_target_pairs={{1,0},{2,1},{3,2},{4,3},{5,4},{6,5},{7,6},{8,7},{9,8},{10,9},{11,1... | collective-permute-start | bytes 110600 | tf_op jit(solution)/shard_map/ppermute | solution.py:639
  24.0 9.3 %collective-permute-start.4 = (f32[20,24,128]{2,1,0:T(8,128)S(1)}, f32[20,24,128]{2,1,0:T(8,128)S(1)}, u32[]{:S(2)}, u32[]{:S(2)}) collective-permute-start(f32[20,24,128]{2,1,0:T(8,128)S(1)} %get-tuple-element.38), channel_id=1, source_target_pairs={{0,128},{128,256},{256,384},{384,0},{1,129},{129,257},{257,385},{3... | collective-permute-start | bytes 737288 | tf_op jit(solution)/shard_map/ppermute | solution.py:639
  27.3 8.1 %collective-permute-start.5 = (f32[20,24,128]{2,1,0:T(8,128)S(1)}, f32[20,24,128]{2,1,0:T(8,128)S(1)}, u32[]{:S(2)}, u32[]{:S(2)}) collective-permute-start(f32[20,24,128]{2,1,0:T(8,128)S(1)} %get-tuple-element.39), channel_id=1, source_target_pairs={{128,0},{256,128},{384,256},{0,384},{129,1},{257,129},{385,257},{1... | collective-permute-start | bytes 737288 | tf_op jit(solution)/shard_map/ppermute | solution.py:639
  35.4 13.0 %copy-start = (s32[2,16,128]{2,1,0:T(8,128)S(1)}, s32[2,16,128]{2,1,0:T(8,128)}, u32[]{:S(2)}) copy-start(s32[2,16,128]{2,1,0:T(8,128)} %solid_ref.1) | copy-start | bytes 49156
  38.0 8.2 %collective-permute-start.6 = (f32[35,8,128]{2,1,0:T(8,128)S(1)}, f32[35,8,128]{2,1,0:T(8,128)S(1)}, u32[]{:S(2)}, u32[]{:S(2)}) collective-permute-start(f32[35,8,128]{2,1,0:T(8,128)S(1)} %get-tuple-element.46), channel_id=1, source_target_pairs={{0,128},{128,256},{256,384},{384,0},{1,129},{129,257},{257,385},{3... | collective-permute-start | bytes 430088 | tf_op jit(solution)/shard_map/ppermute | solution.py:639
  41.4 7.0 %collective-permute-start.7 = (f32[35,8,128]{2,1,0:T(8,128)S(1)}, f32[35,8,128]{2,1,0:T(8,128)S(1)}, u32[]{:S(2)}, u32[]{:S(2)}) collective-permute-start(f32[35,8,128]{2,1,0:T(8,128)S(1)} %get-tuple-element.47), channel_id=1, source_target_pairs={{128,0},{256,128},{384,256},{0,384},{129,1},{257,129},{385,257},{1... | collective-permute-start | bytes 430088 | tf_op jit(solution)/shard_map/ppermute | solution.py:639

commit v4 on v3

--- a/solution.py
+++ b/solution.py
@@ -1,3 +1,5 @@
+import functools
+
 import jax
 import jax.numpy as jnp
 from jax import lax
@@ -255,7 +257,7 @@
     )
 
 
-def rows_kernel(f_hbm, por_hbm, solid_hbm, seed_hbm, up_ref, down_ref, f_ref, seed_ref, b_ref, por_ref, solid_ref, sems):
+def rows_kernel(f_hbm, por_hbm, solid_hbm, seed_hbm, up_ref, down_ref, f_ref, seed_ref, b_ref, fluid_ref, por_ref, solid_ref, sems):
     copies = [
         pltpu.make_async_copy(src, dst, sems.at[k])
         for k, (src, dst) in enumerate(
@@ -281,6 +283,7 @@
     copies[3].wait()
     for layer in range(2):
         b_ref[layer] = jnp.where(solid_ref[layer] == 1, 1.0, por_ref[layer])
+        fluid_ref[layer] = jnp.where(solid_ref[layer] == 1, 0.0, 1.0)
         send(2 * Q, layer, b_ref, layer)
 
 
@@ -308,31 +311,28 @@
 
 
 def tiles_loop(count, body):
-    def step(n, carry):
-        body(n // 3, pl.multiple_of((n % 3) * 8, 8))
-        return carry
-
-    lax.fori_loop(0, count, step, 0)
+    for n in range(count):
+        body(8 * n)
 
 
 def main_kernel(main_ref, g_ref):
     for layer in range(2):
 
-        def body(_, row, layer=layer):
-            f = [main_ref[i, layer, pl.ds(row, 8), :] for i in range(Q)]
+        def body(row, layer=layer):
+            f = [main_ref[i, layer, slice(row, row + 8), :] for i in range(Q)]
             even, odd = split(f)
             rho, u = moments(f[0], even, odd)
-            g = collide(f[0], even, odd, rho, u, main_ref[2 * Q, layer, pl.ds(row, 8), :], range(Q))
+            g = collide(f[0], even, odd, rho, u, main_ref[2 * Q, layer, slice(row, row + 8), :], range(Q))
             for i in range(Q):
-                g_ref[i, layer, pl.ds(row, 8), :] = g[i]
+                g_ref[i, layer, slice(row, row + 8), :] = g[i]
 
         tiles_loop(3, body)
 
 
 def first_kernel(
     main_ref, g_ref, before_ref, beyond_ref,
-    f1_ref, edge_ref, level_ref, s_ref, b_ref, up_ref, down_ref,
-    f_scr, g_scr,
+    f1_ref, edge_ref, s_ref, b_ref, up_ref, down_ref,
+    f_scr, g_scr, level_ref,
 ):
     at = column((ROWS, LANES))
     for k in range(FIELDS):
@@ -352,13 +352,13 @@
 
     for layer in range(2):
 
-        def body(_, row, layer=layer):
-            f = [f_scr[i, layer, pl.ds(row, 8), :] for i in range(Q)]
+        def body(row, layer=layer):
+            f = [f_scr[i, layer, slice(row, row + 8), :] for i in range(Q)]
             even, odd = split(f)
             rho, u = moments(f[0], even, odd)
-            g = collide(f[0], even, odd, rho, u, b_ref[layer, 1, pl.ds(row, 8), :], range(Q))
+            g = collide(f[0], even, odd, rho, u, b_ref[layer, 1, slice(row, row + 8), :], range(Q))
             for i in range(Q):
-                g_scr[i, layer, pl.ds(row, 8), :] = g[i]
+                g_scr[i, layer, slice(row, row + 8), :] = g[i]
 
         tiles_loop(3, body)
 
@@ -407,71 +407,76 @@
                 b2_ref[i, to, 1] = rim
 
 
+def side_kernel(side, f1_ref, edge_ref, b_ref, got_ref, mom_ref, far_ref, bh_ref, g_ref, far_g_ref, rim_scr):
+    unpack1(got_ref, rim_scr)
+    got = (got_ref, rim_scr)
+    theirs, ours = (XP, XM) if side == 0 else (XM, XP)
+    for lane in range(2):
+        bh_ref[lane] = got[lane][8]
+
+        def near(row, lane=lane):
+            rows = slice(row, row + 8)
+            f = [None if i in theirs else f1_ref[i, side, lane, rows, :] for i in range(Q)]
+            for k, i in enumerate(theirs):
+                f[i] = got[lane][9 + k, rows, :]
+            even, odd = split(f)
+            rho, u = moments(f[0], even, odd)
+            mom_ref[3, lane, rows, :] = rho
+            for axis in range(3):
+                mom_ref[axis, lane, rows, :] = u[axis]
+            g = collide(f[0], even, odd, rho, u, b_ref[side, lane, rows, :], range(Q))
+            for i in range(Q):
+                g_ref[i, lane, rows, :] = g[i]
+
+        def far(row, lane=lane):
+            rows = slice(row, row + 8)
+            f = [None] * Q
+            for k, i in enumerate(theirs):
+                f[i] = got[lane][k, rows, :]
+            for i in ours:
+                f[i] = edge_ref[i, lane, rows, :]
+            even, odd = split(f, XP)
+            rho, u = moments_from([got[lane][5 + k, rows, :] for k in range(3)], even, odd)
+            for axis in range(3):
+                far_ref[axis, lane, rows, :] = u[axis]
+            g = collide(None, even, odd, rho, u, got[lane][8, rows, :], theirs)
+            for i in theirs:
+                far_g_ref[i, lane, rows, :] = g[i]
+
+        tiles_loop(3, near)
+        tiles_loop(3, far)
+
+
 def middle_kernel(
-    f1_ref, edge_ref, level_ref, b_ref, b2_ref, left_ref, right_ref,
-    mom_ref, bh_ref, grad_ref, b1_ref, edge1_ref, sums_ref, up_ref, down_ref,
-    l_scr, r_scr, g_scr, f_scr, a_scr, rim_scr,
+    b_ref, b2_ref, left_ref, right_ref, mom0_ref, mom1_ref, g0_ref, g1_ref, g_left_ref, g_right_ref,
+    grad_ref, b1_ref, edge1_ref, sums_ref, up_ref, down_ref,
+    l_scr, r_scr, f_scr, a_scr, rim_scr,
 ):
-    unpack1(left_ref, l_scr)
-    unpack1(right_ref, r_scr)
+    def out(scr):
+        def put(k, rim):
+            if k >= 14:
+                scr[k] = rim
+
+        return put
+
+    unpack_rims(left_ref[SEND1], WIDTH1, out(l_scr))
+    unpack_rims(right_ref[SEND1], WIDTH1, out(r_scr))
     got = ((left_ref, right_ref), (l_scr, r_scr))
-    for side in range(2):
-        for lane in range(2):
-            bh_ref[side, lane] = got[lane][side][8]
+    g_refs = (g_left_ref, g0_ref, g1_ref, g_right_ref)
+    mom = (mom0_ref, mom1_ref)
+
+    for i in range(Q):
+        for layer in range(2):
+            ref = g_refs[layer + 1 - VEL[i][0]]
+            main, rim = moved(ref[i, 0], ref[i, 1], i, 1)
+            f_scr[i, layer, 0] = main
+            f_scr[i, layer, 1] = rim
 
     for layer in range(2):
         for lane in range(2):
 
-            def body(_, row, layer=layer, lane=lane):
-                rows = pl.ds(row, 8)
-                missing = XP if layer == 0 else XM
-                f = [None if i in missing else f1_ref[i, layer, lane, rows, :] for i in range(Q)]
-                for k, i in enumerate(missing):
-                    f[i] = got[lane][layer][9 + k, rows, :]
-                even, odd = split(f)
-                rho, u = moments(f[0], even, odd)
-                mom_ref[3, layer + 1, lane, rows, :] = rho
-                for axis in range(3):
-                    mom_ref[axis, layer + 1, lane, rows, :] = u[axis]
-                g = collide(f[0], even, odd, rho, u, b_ref[layer, lane, rows, :], range(Q))
-                for i in range(Q):
-                    g_scr[i, layer + 1, lane, rows, :] = g[i]
-
-            tiles_loop(3, body)
-
-    for side in range(2):
-        for lane in range(2):
-
-            def body(_, row, side=side, lane=lane):
-                rows = pl.ds(row, 8)
-                theirs, ours = (XP, XM) if side == 0 else (XM, XP)
-                f = [None] * Q
-                for k, i in enumerate(theirs):
-                    f[i] = got[lane][side][k, rows, :]
-                for i in ours:
-                    f[i] = edge_ref[i, lane, rows, :]
-                even, odd = split(f, XP)
-                rho, u = moments_from([got[lane][side][5 + k, rows, :] for k in range(3)], even, odd)
-                for axis in range(3):
-                    mom_ref[axis, 3 * side, lane, rows, :] = u[axis]
-                g = collide(None, even, odd, rho, u, got[lane][side][8, rows, :], theirs)
-                for i in theirs:
-                    g_scr[i, 3 * side, lane, rows, :] = g[i]
-
-            tiles_loop(3, body)
-
-    for i in range(Q):
-        for layer in range(2):
-            n = layer + 1 - VEL[i][0]
-            main, rim = moved(g_scr[i, n, 0], g_scr[i, n, 1], i, 1)
-            f_scr[i, layer, 0] = main
-            f_scr[i, layer, 1] = rim
-
-    for layer in range(2):
-        for lane in range(2):
-
-            def body(row, layer=layer, lane=lane, own=False):
-                rows = pl.ds(row, 8)
+            def body(row, layer=layer, lane=lane):
+                rows = slice(row, row + 8)
                 missing = XM if layer == 0 else XP
                 f = [f_scr[i, layer, lane, rows, :] for i in range(Q)]
                 b = {i: b2_ref[i, layer, lane, rows, :] for i in range(Q) if i not in missing}
@@ -484,19 +489,10 @@
                 a = back(b[0], b_even, b_odd, sums, u, b_ref[layer, lane, rows, :], range(Q))
                 for i in range(Q):
                     a_scr[i, layer, lane, rows, :] = a[i]
-                if own:
+                if lane == 0 and row < OWN:
                     grad_ref[layer, rows, :] = gradient_of((b[0], b_even, b_odd), (f[0], even, odd), rho, sums[0])
 
-            if lane == 0:
-
-                def step(n, carry, body=body):
-                    body(pl.multiple_of(n * 8, 8), own=True)
-                    return carry
-
-                lax.fori_loop(0, 2, step, 0)
-                body(16)
-            else:
-                tiles_loop(3, lambda _, row, body=body: body(row))
+            tiles_loop(3, body)
 
     for i in range(Q):
         for layer in range(2):
@@ -511,14 +507,14 @@
     for layer in range(2):
         for lane in range(2):
 
-            def body(_, row, layer=layer, lane=lane):
-                rows = pl.ds(row, 8)
+            def body(row, layer=layer, lane=lane):
+                rows = slice(row, row + 8)
                 missing = XM if layer == 0 else XP
                 b = {i: b1_ref[i, layer, lane, rows, :] for i in range(Q) if i not in missing}
                 even, odd = split(b, [i for i in PAIRS if i in X0])
                 for i in XP:
                     even[i], odd[i] = (b[i], b[i]) if layer == 0 else (b[i + 1], -b[i + 1])
-                sums = flow(b[0], even, odd, [mom_ref[axis, layer + 1, lane, rows, :] for axis in range(3)])
+                sums = flow(b[0], even, odd, [mom[layer][axis, lane, rows, :] for axis in range(3)])
                 for k in range(4):
                     sums_ref[k, layer, lane, rows, :] = sums[k]
 
@@ -538,83 +534,74 @@
     pack2(down_ref, rim_scr, tiles_of(XP, 0))
 
 
+def side_back_kernel(
+    side, b1_ref, edge1_ref, sums_ref, mom_ref, far_ref, b_ref, bh_ref, f1_ref, got1_ref, grad_ref, got_ref,
+    out_grad_ref, a_ref, far_a_ref,
+    got,
+):
+    unpack2(got_ref, got)
+    near_pops, far_pops = (XM, XP) if side == 0 else (XP, XM)
+
+    def halves(b, plus):
+        return {i: b[i] if plus else b[i + 1] for i in XP}, {i: b[i] if plus else -b[i + 1] for i in XP}
+
+    for lane in range(2):
+
+        def near(row, lane=lane):
+            rows = slice(row, row + 8)
+            b = {i: b1_ref[i, side, lane, rows, :] for i in range(Q) if i not in near_pops}
+            for k, i in enumerate(near_pops):
+                b[i] = got[k, lane, rows, :]
+            even, odd = split(b)
+            u = [mom_ref[axis, lane, rows, :] for axis in range(3)]
+            parts = flow(None, *halves(b, side == 1), u)
+            sums = [sums_ref[k, side, lane, rows, :] + part for k, part in enumerate(parts)]
+            a = back(b[0], even, odd, sums, u, b_ref[side, lane, rows, :], range(Q))
+            for i in range(Q):
+                a_ref[i, lane, rows, :] = a[i]
+            if lane == 0 and row < OWN:
+                f = {i: f1_ref[i, side, lane, rows, :] for i in range(Q) if i not in far_pops}
+                for k, i in enumerate(far_pops):
+                    f[i] = got1_ref[9 + k, rows, :]
+                grad = gradient_of((b[0], even, odd), (f[0],) + split(f), mom_ref[3, lane, rows, :], sums[0])
+                out_grad_ref[rows, :] = grad + grad_ref[side, rows, :]
+
+        def far(row, lane=lane):
+            rows = slice(row, row + 8)
+            b = {i: edge1_ref[i, lane, rows, :] for i in far_pops}
+            for k, i in enumerate(near_pops):
+                b[i] = got[5 + k, lane, rows, :]
+            even, odd = split(b, XP)
+            u = [far_ref[axis, lane, rows, :] for axis in range(3)]
+            parts = flow(None, *halves(b, side == 0), u)
+            sums = [got[10 + k, lane, rows, :] + part for k, part in enumerate(parts)]
+            a = back(None, even, odd, sums, u, bh_ref[lane, rows, :], near_pops)
+            for i in near_pops:
+                far_a_ref[i, lane, rows, :] = a[i]
+
+        tiles_loop(3, near)
+        tiles_loop(3, far)
+
+
 def last_kernel(
-    b1_ref, edge1_ref, sums_ref, mom_ref, b_ref, bh_ref, f1_ref, left1_ref, right1_ref, grad_ref, left_ref, right_ref, f_ref, solid_ref,
+    b_ref, grad0_ref, grad1_ref, a_left_ref, a0_ref, a1_ref, a_right_ref, f_ref, fluid_ref,
     out_grad_ref, out_ref,
-    l_scr, r_scr, a_scr, b0_scr,
+    b_scr,
 ):
-    unpack2(left_ref, l_scr)
-    unpack2(right_ref, r_scr)
-    got = (l_scr, r_scr)
-    got1 = (left1_ref, right1_ref)
+    a_refs = (a_left_ref, a0_ref, a1_ref, a_right_ref)
+    grads = (grad0_ref, grad1_ref)
+    for i in range(Q):
+        for layer in range(2):
+            ref = a_refs[layer + 1 + VEL[i][0]]
+            main, _ = moved(ref[i, 0], ref[i, 1], i, -1)
+            b_scr[i, layer] = main[0:OWN]
 
     for layer in range(2):
-        for lane in range(2):
-
-            def body(row, layer=layer, lane=lane, own=False):
-                rows = pl.ds(row, 8)
-                missing = XM if layer == 0 else XP
-                b = {i: b1_ref[i, layer, lane, rows, :] for i in range(Q) if i not in missing}
-                for k, i in enumerate(missing):
-                    b[i] = got[layer][k, lane, rows, :]
-                new_even = {i: b[i + 1] if layer == 0 else b[i] for i in XP}
-                new_odd = {i: -b[i + 1] if layer == 0 else b[i] for i in XP}
-                even, odd = split(b)
-                u = [mom_ref[axis, layer + 1, lane, rows, :] for axis in range(3)]
-                sums = [sums_ref[k, layer, lane, rows, :] + part for k, part in enumerate(flow(None, new_even, new_odd, u))]
-                a = back(b[0], even, odd, sums, u, b_ref[layer, lane, rows, :], range(Q))
-                for i in range(Q):
-                    a_scr[i, layer + 1, lane, rows, :] = a[i]
-                if own:
-                    f = {i: f1_ref[i, layer, lane, rows, :] for i in range(Q) if OPP[i] not in missing}
-                    for k, i in enumerate(XP if layer == 0 else XM):
-                        f[i] = got1[layer][9 + k, rows, :]
-                    grad = gradient_of((b[0], even, odd), (f[0],) + split(f), mom_ref[3, layer + 1, lane, rows, :], sums[0])
-                    out_grad_ref[layer, rows, :] = grad + grad_ref[layer, rows, :]
-
-            if lane == 0:
-
-                def step(n, carry, body=body):
-                    body(pl.multiple_of(n * 8, 8), own=True)
-                    return carry
-
-                lax.fori_loop(0, 2, step, 0)
-                body(16)
-            else:
-                tiles_loop(3, lambda _, row, body=body: body(row))
-
-    for side in range(2):
-        for lane in range(2):
-
-            def body(_, row, side=side, lane=lane):
-                rows = pl.ds(row, 8)
-                theirs, ours = (XM, XP) if side == 0 else (XP, XM)
-                b = {i: edge1_ref[i, lane, rows, :] for i in ours}
-                for k, i in enumerate(theirs):
-                    b[i] = got[side][5 + k, lane, rows, :]
-                new_even = {i: b[i] if side == 0 else b[i + 1] for i in XP}
-                new_odd = {i: b[i] if side == 0 else -b[i + 1] for i in XP}
-                even, odd = split(b, XP)
-                u = [mom_ref[axis, 3 * side, lane, rows, :] for axis in range(3)]
-                sums = [got[side][10 + k, lane, rows, :] + part for k, part in enumerate(flow(None, new_even, new_odd, u))]
-                a = back(None, even, odd, sums, u, bh_ref[side, lane, rows, :], theirs)
-                for i in theirs:
-                    a_scr[i, 3 * side, lane, rows, :] = a[i]
-
-            tiles_loop(3, body)
-
-    for i in range(Q):
-        for layer in range(2):
-            n = layer + 1 + VEL[i][0]
-            main, _ = moved(a_scr[i, n, 0], a_scr[i, n, 1], i, -1)
-            b0_scr[i, layer] = main[0:OWN]
-
-    for layer in range(2):
-
-        def final(n, carry, layer=layer):
-            rows = pl.ds(pl.multiple_of(n * 8, 8), 8)
+
+        def body(row, layer=layer):
+            rows = slice(row, row + 8)
             f = [f_ref[i, layer, rows, :] for i in range(Q)]
-            b = {i: b0_scr[i, layer, rows, :] for i in range(Q)}
+            b = {i: b_scr[i, layer, rows, :] for i in range(Q)}
             even, odd = split(f)
             rho, u = moments(f[0], even, odd)
             b_even, b_odd = split(b)
@@ -622,11 +609,10 @@
             a = back(b[0], b_even, b_odd, sums, u, b_ref[layer, 0, rows, :], range(Q))
             for i in range(Q):
                 out_ref[i, layer, rows, :] = a[i]
-            grad = gradient_of((b[0], b_even, b_odd), (f[0], even, odd), rho, sums[0]) + out_grad_ref[layer, rows, :]
-            out_grad_ref[layer, rows, :] = jnp.where(solid_ref[layer, rows, :] == 1, 0.0, grad)
-            return carry
-
-        lax.fori_loop(0, 2, final, 0)
+            grad = gradient_of((b[0], b_even, b_odd), (f[0], even, odd), rho, sums[0]) + grads[layer][rows, :]
+            out_grad_ref[layer, rows, :] = jnp.where(fluid_ref[layer, rows, :] == 0.0, 0.0, grad)
+
+        tiles_loop(2, body)
 
 
 def placed(x):
@@ -643,9 +629,9 @@
     half, tile = (2, 2, ROWS, LANES), (ROWS, LANES)
     inputs = [placed(x) for x in (populations, porosity, solid, seed_adjoint)]
     block = populations.shape
-    up, down, f, seed, b = call(
+    up, down, f, seed, b, fluid = call(
         rows_kernel,
-        [(FIELDS, 8, LANES)] * 2 + [block, block, block[1:]],
+        [(FIELDS, 8, LANES)] * 2 + [block, block, block[1:], block[1:]],
         [block[1:]],
         [pltpu.VMEM(block[1:], jnp.int32), pltpu.SemaphoreType.DMA((4,))],
         space=[pltpu.HBM] * 4,
@@ -654,25 +640,42 @@
     main, up, down = call(columns_kernel, [(FIELDS, 2) + tile] + [(ZTILES,) + tile] * 2)(f, seed, b, below, above)
     before, beyond = both_ways(up, down, "gz")
     (g,) = call(main_kernel, [(Q, 2) + tile])(main)
-    f1, edge, level, s, b, up, down = call(
+    f1, edge, s, b, up, down = call(
         first_kernel,
-        [(Q,) + half, (Q, 2) + tile, (3,) + half, (Q, 2) + tile, half] + [(SEND1 + 1,) + tile] * 2,
-        [(Q, 2) + tile] * 2,
+        [(Q,) + half, (Q, 2) + tile, (Q, 2) + tile, half] + [(SEND1 + 1,) + tile] * 2,
+        [(Q, 2) + tile] * 2 + [(3,) + half],
     )(main, g, before, beyond)
     left1, right1 = both_ways(up, down, "gx")
     (b2,) = call(seed_kernel, [(Q,) + half])(main, s)
-    wide = (4, 2) + tile
-    mom, bh, grad, b1, edge1, sums, up, down = call(
+    sides = []
+    for side, got in enumerate((left1, right1)):
+        sides.append(
+            call(
+                functools.partial(side_kernel, side),
+                [(4, 2) + tile, (3, 2) + tile, (2,) + tile, (Q, 2) + tile, (Q, 2) + tile],
+                [(SEND1,) + tile],
+            )(f1, edge, b, got)
+        )
+    (mom0, far0, bh0, g0, g_left), (mom1, far1, bh1, g1, g_right) = sides
+    grad, b1, edge1, sums, up, down = call(
         middle_kernel,
-        [(4,) + wide, half, (2, OWN, LANES), (Q,) + half, (Q, 2) + tile, (4,) + half] + [(ROWTILES2 + 3, 8, LANES)] * 2,
-        [(SEND1,) + tile] * 2 + [(Q,) + wide, (Q,) + half, (Q,) + half, (1,) + tile],
-    )(f1, edge, level, b, b2, left1, right1)
+        [(2, OWN, LANES), (Q,) + half, (Q, 2) + tile, (4,) + half] + [(ROWTILES2 + 3, 8, LANES)] * 2,
+        [(SEND1,) + tile] * 2 + [(Q,) + half, (Q,) + half, (1,) + tile],
+    )(b, b2, left1, right1, mom0, mom1, g0, g1, g_left, g_right)
     left, right = both_ways(up, down, "gx")
-    gradient, adjoint_out = call(
-        last_kernel,
-        [(2, OWN, LANES), (Q, 2, OWN, LANES)],
-        [(SEND2, 2) + tile] * 2 + [(Q,) + wide, (Q, 2, OWN, LANES)],
-    )(b1, edge1, sums, mom, b, bh, f1, left1, right1, grad, left, right, f, solid)
+    sides = []
+    for side, (mom, far, bh, got1, got) in enumerate(((mom0, far0, bh0, left1, left), (mom1, far1, bh1, right1, right))):
+        sides.append(
+            call(
+                functools.partial(side_back_kernel, side),
+                [(OWN, LANES), (Q, 2) + tile, (Q, 2) + tile],
+                [(SEND2, 2) + tile],
+            )(b1, edge1, sums, mom, far, b, bh, f1, got1, grad, got)
+        )
+    (grad0, a0, a_left), (grad1, a1, a_right) = sides
+    gradient, adjoint_out = call(last_kernel, [(2, OWN, LANES), (Q, 2, OWN, LANES)], [(Q, 2, OWN, LANES)])(
+        b, grad0, grad1, a_left, a0, a1, a_right, f, fluid
+    )
     return gradient, adjoint_out
 
 

time: 50.9 us -> 50.6 us (level)
  waiting for transfers between devices: 15.3 us -> 18.9 us
  Pallas kernels: 7.93 us -> 6.08 us
  starting transfers between devices: 26.5 us -> 24.7 us
    ppermute x4, waiting for transfers between devices: 5.44 us -> 10.5 us  [both_ways(): lax.ppermute(up, axis, ring)]
    pallas_call x4 -> x8, Pallas kernels: 6.96 us -> 5.18 us  [the longest x1 1.14 us: body(): call(rows_kernel, [(FIELDS, 8, LANES)] * 2 + [block, block, block[1:], bl...]
    ppermute x4, waiting for transfers between devices: 9.88 us -> 8.33 us  [both_ways(): lax.ppermute(down, axis, [(j, i) for i, j in ring])]
    ppermute x4, starting transfers between devices: 12.3 us -> 11.3 us  [both_ways(): lax.ppermute(down, axis, [(j, i) for i, j in ring])]
    ppermute x4, starting transfers between devices: 14.2 us -> 13.4 us  [both_ways(): lax.ppermute(up, axis, ring)]
  transfers between devices with their start and end apart: 8 -> 8, of which waited for: 7 -> 7; matrix products, arithmetic and copies ran while one was open for 0% -> 0% of each run, Pallas kernels for 1% -> 2%
where the time goes in v4:
time: 50.6 us; the launch traced here: 50.4 us
  starting transfers between devices  24.7 us (49%)
  waiting for transfers between devices  18.9 us (37%)
  Pallas kernels  6.08 us (12%)
  between operations  0.74 us (1%)
    ppermute x4, starting transfers between devices, both_ways(): lax.ppermute(up, axis, ring)  13.4 us
    ppermute x4, starting transfers between devices, both_ways(): lax.ppermute(down, axis, [(j, i) for i, j in ring])  11.3 us
    ppermute x4, waiting for transfers between devices, both_ways(): lax.ppermute(up, axis, ring)  10.5 us
    ppermute x4, waiting for transfers between devices, both_ways(): lax.ppermute(down, axis, [(j, i) for i, j in ring])  8.33 us
    pallas_call x1, Pallas kernels, body(): call(rows_kernel, [(FIELDS, 8, LANES)] * 2 + [block, block, block[1:], bl...  1.14 us
  transfers between devices with their start and end apart: 8, of which 7 were waited for; matrix products, arithmetic and copies ran while one was open for 0% of the time, Pallas kernels for 2%

profile of v4, /device:TPU:24, one launch (start us, length us, event | category | flops | bytes accessed | tf_op | source)
XLA Modules:
  0.0 50.4 jit_solution(16256920969490262161)
XLA Ops:
  0.6 1.1 %shard_map.59 = (f32[39,8,128]{2,1,0:T(8,128)S(1)}, f32[39,8,128]{2,1,0:T(8,128)S(1)}, f32[19,2,16,128]{3,2,1,0:T(8,128)S(1)}, f32[19,2,16,128]{3,2,1,0:T(8,128)...) custom-call(f32[19,2,16,128]{3,2,1,0:T(8,128)} %f_hbm.1, f32[2,16,128]{2,1,0:T(8,128)} %por_hbm.1, ...), custom_call_target="tpu_custom_call" | custom-call | flops 2000000 | bytes 1000000 | tf_op jit(solution)/shard_map/pallas_call | solution.py:632
  1.8 7.5 %collective-permute-start = (f32[39,8,128]{2,1,0:T(8,128)S(1)}, f32[39,8,128]{2,1,0:T(8,128)S(1)}, u32[]{:S(2)}, u32[]{:S(2)}) collective-permute-start(f32[39,8,128]{2,1,0:T(8,128)S(1)} %get-tuple-element.42), channel_id=1, source_target_pairs={{0,32},{32,64},{64,96},{96,0},{1,33},{33,65},{65,97},{97,1},{2,34}... | collective-permute-start | bytes 479240 | tf_op jit(solution)/shard_map/ppermute | solution.py:625
  9.3 1.9 %collective-permute-start.1 = (f32[39,8,128]{2,1,0:T(8,128)S(1)}, f32[39,8,128]{2,1,0:T(8,128)S(1)}, u32[]{:S(2)}, u32[]{:S(2)}) collective-permute-start(f32[39,8,128]{2,1,0:T(8,128)S(1)} %get-tuple-element.43), channel_id=1, source_target_pairs={{32,0},{64,32},{96,64},{0,96},{33,1},{65,33},{97,65},{1,97},{34,2}... | collective-permute-start | bytes 479240 | tf_op jit(solution)/shard_map/ppermute | solution.py:625
  11.2 0.8 %collective-permute-done.below_ref = f32[39,8,128]{2,1,0:T(8,128)S(1)} collective-permute-done((f32[39,8,128]{2,1,0:T(8,128)S(1)}, f32[39,8,128]{2,1,0:T(8,128)S(1)}, u32[]{:S(2)}, u32[]{:S(2)}) %collective-permute-start) | collective-permute-done | bytes 159776 | tf_op jit(solution)/shard_map/ppermute | solution.py:625
  12.1 5.6 %collective-permute-done.1.above_ref = f32[39,8,128]{2,1,0:T(8,128)S(1)} collective-permute-done((f32[39,8,128]{2,1,0:T(8,128)S(1)}, f32[39,8,128]{2,1,0:T(8,128)S(1)}, u32[]{:S(2)}, u32[]{:S(2)}) %collective-permute-start.1) | collective-permute-done | bytes 159776 | tf_op jit(solution)/shard_map/ppermute | solution.py:625
  17.7 0.6 %shard_map.60 = (f32[39,2,24,128]{3,2,1,0:T(8,128)S(1)}, f32[3,24,128]{2,1,0:T(8,128)S(1)}, f32[3,24,128]{2,1,0:T(8,128)S(1)}) custom-call(f32[19,2,16,128]{3,2,1,0:T(8,128)S(1)} %get-tuple-element.39.f_ref, f32[19,2,16,128]{3,2,1,0:T(8,128)S(1)} %get-tuple-element.40.seed_ref, f32[2,16,128]{2,1,0:T(8,128)S(1)} %get-tuple-element.41.b_ref, ...), custom_call_target="tpu_custom_call" | custom-call | flops 2000000 | bytes 1000000 | tf_op jit(solution)/shard_map/pallas_call | solution.py:640
  18.2 0.0 collective-permute-start.2
  18.3 2.9 %collective-permute-start.3 = (f32[3,24,128]{2,1,0:T(8,128)S(1)}, f32[3,24,128]{2,1,0:T(8,128)S(1)}, u32[]{:S(2)}, u32[]{:S(2)}) collective-permute-start(f32[3,24,128]{2,1,0:T(8,128)S(1)} %get-tuple-element.46), channel_id=1, source_target_pairs={{1,0},{2,1},{3,2},{4,3},{5,4},{6,5},{7,6},{8,7},{9,8},{10,9},{11,1... | collective-permute-start | bytes 110600 | tf_op jit(solution)/shard_map/ppermute | solution.py:625
  21.2 0.1 shard_map.61.g_ref
  21.4 1.5 %collective-permute-done.2.before_ref = f32[3,24,128]{2,1,0:T(8,128)S(1)} collective-permute-done((f32[3,24,128]{2,1,0:T(8,128)S(1)}, f32[3,24,128]{2,1,0:T(8,128)S(1)}, u32[]{:S(2)}, u32[]{:S(2)}) %collective-permute-start.2) | collective-permute-done | bytes 36896 | tf_op jit(solution)/shard_map/ppermute | solution.py:625
  22.9 0.0 collective-permute-done.3.beyond_ref
  22.9 1.0 %shard_map.62 = (f32[19,2,2,24,128]{4,3,2,1,0:T(8,128)S(1)}, f32[19,2,24,128]{3,2,1,0:T(8,128)S(1)}, f32[19,2,24,128]{3,2,1,0:T(8,128)S(1)}, f32[2,2,24,128]{3,2...) custom-call(f32[39,2,24,128]{3,2,1,0:T(8,128)S(1)} %get-tuple-element.44.main_ref, ...), custom_call_target="tpu_custom_call" | custom-call | flops 2000000 | bytes 1000000 | tf_op jit(solution)/shard_map/pallas_call | solution.py:643
  23.8 4.5 %collective-permute-start.5 = (f32[20,24,128]{2,1,0:T(8,128)S(1)}, f32[20,24,128]{2,1,0:T(8,128)S(1)}, u32[]{:S(2)}, u32[]{:S(2)}) collective-permute-start(f32[20,24,128]{2,1,0:T(8,128)S(1)} %get-tuple-element.50), channel_id=1, source_target_pairs={{128,0},{256,128},{384,256},{0,384},{129,1},{257,129},{385,257},{1... | collective-permute-start | bytes 737288 | tf_op jit(solution)/shard_map/ppermute | solution.py:625
  28.4 1.9 %collective-permute-start.4 = (f32[20,24,128]{2,1,0:T(8,128)S(1)}, f32[20,24,128]{2,1,0:T(8,128)S(1)}, u32[]{:S(2)}, u32[]{:S(2)}) collective-permute-start(f32[20,24,128]{2,1,0:T(8,128)S(1)} %get-tuple-element.49), channel_id=1, source_target_pairs={{0,128},{128,256},{256,384},{384,0},{1,129},{129,257},{257,385},{3... | collective-permute-start | bytes 737288 | tf_op jit(solution)/shard_map/ppermute | solution.py:625
  30.3 0.2 shard_map.63.b2_ref
  30.5 1.6 %collective-permute-done.5.got_ref.right_ref.got1_ref = f32[20,24,128]{2,1,0:T(8,128)S(1)} collective-permute-done((f32[20,24,128]{2,1,0:T(8,128)S(1)}, f32[20,24,128]{2,1,0:T(8,128)S(1)}, u32[]{:S(2)}, u32[]{:S(2)}) %collective-permute-start.5) | collective-permute-done | bytes 245792 | tf_op jit(solution)/shard_map/ppermute | solution.py:625
  32.1 0.2 shard_map.65
  32.3 5.4 %collective-permute-done.4.got_ref.left_ref.got1_ref = f32[20,24,128]{2,1,0:T(8,128)S(1)} collective-permute-done((f32[20,24,128]{2,1,0:T(8,128)S(1)}, f32[20,24,128]{2,1,0:T(8,128)S(1)}, u32[]{:S(2)}, u32[]{:S(2)}) %collective-permute-start.4) | collective-permute-done | bytes 245792 | tf_op jit(solution)/shard_map/ppermute | solution.py:625
  37.7 0.2 shard_map.64
  37.9 1.0 %shard_map.66 = (f32[2,16,128]{2,1,0:T(8,128)S(1)}, f32[19,2,2,24,128]{4,3,2,1,0:T(8,128)S(1)}, f32[19,2,24,128]{3,2,1,0:T(8,128)S(1)}, f32[4,2,2,24,128]{4,3,2,...) custom-call(f32[2,2,24,128]{3,2,1,0:T(8,128)S(1)} %get-tuple-element.47.b_ref, ...), custom_call_target="tpu_custom_call" | custom-call | flops 2000000 | bytes 1000000 | tf_op jit(solution)/shard_map/pallas_call | solution.py:660
  39.0 1.9 %collective-permute-start.7 = (f32[35,8,128]{2,1,0:T(8,128)S(1)}, f32[35,8,128]{2,1,0:T(8,128)S(1)}, u32[]{:S(2)}, u32[]{:S(2)}) collective-permute-start(f32[35,8,128]{2,1,0:T(8,128)S(1)} %get-tuple-element.69), channel_id=1, source_target_pairs={{128,0},{256,128},{384,256},{0,384},{129,1},{257,129},{385,257},{1... | collective-permute-start | bytes 430088 | tf_op jit(solution)/shard_map/ppermute | solution.py:625
  40.9 3.9 %collective-permute-start.6 = (f32[35,8,128]{2,1,0:T(8,128)S(1)}, f32[35,8,128]{2,1,0:T(8,128)S(1)}, u32[]{:S(2)}, u32[]{:S(2)}) collective-permute-start(f32[35,8,128]{2,1,0:T(8,128)S(1)} %get-tuple-element.65), channel_id=1, source_target_pairs={{0,128},{128,256},{256,384},{384,0},{1,129},{129,257},{257,385},{3... | collective-permute-start | bytes 430088 | tf_op jit(solution)/shard_map/ppermute | solution.py:625
  44.8 1.1 %collective-permute-done.7.got_ref = f32[35,8,128]{2,1,0:T(8,128)S(1)} collective-permute-done((f32[35,8,128]{2,1,0:T(8,128)S(1)}, f32[35,8,128]{2,1,0:T(8,128)S(1)}, u32[]{:S(2)}, u32[]{:S(2)}) %collective-permute-start.7) | collective-permute-done | bytes 143392 | tf_op jit(solution)/shard_map/ppermute | solution.py:625
  45.9 0.3 shard_map.68
  46.2 2.8 %collective-permute-done.6.got_ref = f32[35,8,128]{2,1,0:T(8,128)S(1)} collective-permute-done((f32[35,8,128]{2,1,0:T(8,128)S(1)}, f32[35,8,128]{2,1,0:T(8,128)S(1)}, u32[]{:S(2)}, u32[]{:S(2)}) %collective-permute-start.6) | collective-permute-done | bytes 143392 | tf_op jit(solution)/shard_map/ppermute | solution.py:625
  49.1 0.3 shard_map.67
  49.4 1.0 %shard_map.69 = (f32[2,16,128]{2,1,0:T(8,128)}, f32[19,2,16,128]{3,2,1,0:T(8,128)}) custom-call(f32[2,2,24,128]{3,2,1,0:T(8,128)S(1)} %get-tuple-element.47.b_ref, f32[16,128]{1,0:T(8,128)S(1)} %get-tuple-element.66.grad0_ref, f32[16,128]{1,0:T(8,128)S(1)} %get-tuple-element.70.grad1_ref, f32[19,2,24,128]{3,2,1,0:T(8,128)S(1)} %get-tuple-element.71.a_left_ref, ...), custom_call_target="tpu_custom_call" | custom-call | flops 2000000 | bytes 1000000 | tf_op jit(solution)/shard_map/pallas_call | solution.py:676
Async XLA Ops:
  1.8 10.3 %collective-permute-start = (f32[39,8,128]{2,1,0:T(8,128)S(1)}, f32[39,8,128]{2,1,0:T(8,128)S(1)}, u32[]{:S(2)}, u32[]{:S(2)}) collective-permute-start(f32[39,8,128]{2,1,0:T(8,128)S(1)} %get-tuple-element.42), channel_id=1, source_target_pairs={{0,32},{32,64},{64,96},{96,0},{1,33},{33,65},{65,97},{97,1},{2,34}... | collective-permute-start | bytes 479240 | tf_op jit(solution)/shard_map/ppermute | solution.py:625
  9.3 8.4 %collective-permute-start.1 = (f32[39,8,128]{2,1,0:T(8,128)S(1)}, f32[39,8,128]{2,1,0:T(8,128)S(1)}, u32[]{:S(2)}, u32[]{:S(2)}) collective-permute-start(f32[39,8,128]{2,1,0:T(8,128)S(1)} %get-tuple-element.43), channel_id=1, source_target_pairs={{32,0},{64,32},{96,64},{0,96},{33,1},{65,33},{97,65},{1,97},{34,2}... | collective-permute-start | bytes 479240 | tf_op jit(solution)/shard_map/ppermute | solution.py:625
  18.2 4.6 %collective-permute-start.2 = (f32[3,24,128]{2,1,0:T(8,128)S(1)}, f32[3,24,128]{2,1,0:T(8,128)S(1)}, u32[]{:S(2)}, u32[]{:S(2)}) collective-permute-start(f32[3,24,128]{2,1,0:T(8,128)S(1)} %get-tuple-element.45), channel_id=1, source_target_pairs={{0,1},{1,2},{2,3},{3,4},{4,5},{5,6},{6,7},{7,8},{8,9},{9,10},{10,1... | collective-permute-start | bytes 110600 | tf_op jit(solution)/shard_map/ppermute | solution.py:625
  18.3 4.6 %collective-permute-start.3 = (f32[3,24,128]{2,1,0:T(8,128)S(1)}, f32[3,24,128]{2,1,0:T(8,128)S(1)}, u32[]{:S(2)}, u32[]{:S(2)}) collective-permute-start(f32[3,24,128]{2,1,0:T(8,128)S(1)} %get-tuple-element.46), channel_id=1, source_target_pairs={{1,0},{2,1},{3,2},{4,3},{5,4},{6,5},{7,6},{8,7},{9,8},{10,9},{11,1... | collective-permute-start | bytes 110600 | tf_op jit(solution)/shard_map/ppermute | solution.py:625
  23.8 8.2 %collective-permute-start.5 = (f32[20,24,128]{2,1,0:T(8,128)S(1)}, f32[20,24,128]{2,1,0:T(8,128)S(1)}, u32[]{:S(2)}, u32[]{:S(2)}) collective-permute-start(f32[20,24,128]{2,1,0:T(8,128)S(1)} %get-tuple-element.50), channel_id=1, source_target_pairs={{128,0},{256,128},{384,256},{0,384},{129,1},{257,129},{385,257},{1... | collective-permute-start | bytes 737288 | tf_op jit(solution)/shard_map/ppermute | solution.py:625
  28.4 9.3 %collective-permute-start.4 = (f32[20,24,128]{2,1,0:T(8,128)S(1)}, f32[20,24,128]{2,1,0:T(8,128)S(1)}, u32[]{:S(2)}, u32[]{:S(2)}) collective-permute-start(f32[20,24,128]{2,1,0:T(8,128)S(1)} %get-tuple-element.49), channel_id=1, source_target_pairs={{0,128},{128,256},{256,384},{384,0},{1,129},{129,257},{257,385},{3... | collective-permute-start | bytes 737288 | tf_op jit(solution)/shard_map/ppermute | solution.py:625
  39.0 7.0 %collective-permute-start.7 = (f32[35,8,128]{2,1,0:T(8,128)S(1)}, f32[35,8,128]{2,1,0:T(8,128)S(1)}, u32[]{:S(2)}, u32[]{:S(2)}) collective-permute-start(f32[35,8,128]{2,1,0:T(8,128)S(1)} %get-tuple-element.69), channel_id=1, source_target_pairs={{128,0},{256,128},{384,256},{0,384},{129,1},{257,129},{385,257},{1... | collective-permute-start | bytes 430088 | tf_op jit(solution)/shard_map/ppermute | solution.py:625
  40.9 8.2 %collective-permute-start.6 = (f32[35,8,128]{2,1,0:T(8,128)S(1)}, f32[35,8,128]{2,1,0:T(8,128)S(1)}, u32[]{:S(2)}, u32[]{:S(2)}) collective-permute-start(f32[35,8,128]{2,1,0:T(8,128)S(1)} %get-tuple-element.65), channel_id=1, source_target_pairs={{0,128},{128,256},{256,384},{384,0},{1,129},{129,257},{257,385},{3... | collective-permute-start | bytes 430088 | tf_op jit(solution)/shard_map/ppermute | solution.py:625

commit v5 on v4

--- a/solution.py
+++ b/solution.py
@@ -257,57 +257,89 @@
     )
 
 
-def rows_kernel(f_hbm, por_hbm, solid_hbm, seed_hbm, up_ref, down_ref, f_ref, seed_ref, b_ref, fluid_ref, por_ref, solid_ref, sems):
+LEVEL_Y = [i for i in range(Q) if VEL[i][1] == 0][:3]
+YTILES = Q + (Q + 1) // 2
+
+
+def rows_moves(up):
+    inwards = 1 if up else -1
+    first = lambda count: OWN - count if up else 0
+    fourth, third = (OWN - 4, OWN - 3) if up else (3, 2)
+    out = []
+    for i in range(Q):
+        for layer in range(2):
+            out.append((0, i, layer, first(3), 3, i, 3 * layer))
+            out.append((1, i, layer, first(2), 2, Q + i // 2, 4 * (i % 2) + 2 * layer))
+            if VEL[i][1] == inwards:
+                out.append((0, i, layer, fourth, 1, i, 6 + layer))
+            elif VEL[i][1] == -inwards:
+                out.append((1, i, layer, third, 1, i, 6 + layer))
+            elif i in LEVEL_Y:
+                out.append((2, 0, layer, first(3) + LEVEL_Y.index(i), 1, i, 6 + layer))
+    return out
+
+
+def collided(f, blocking):
+    even, odd = split(f)
+    rho, u = moments(f[0], even, odd)
+    return collide(f[0], even, odd, rho, u, blocking, range(Q))
+
+
+def rows_kernel(
+    f_hbm, por_hbm, solid_hbm, seed_hbm,
+    up_ref, down_ref, f_ref, seed_ref, g_ref, b_ref, fluid_ref,
+    por_ref, solid_ref, sems,
+):
     copies = [
         pltpu.make_async_copy(src, dst, sems.at[k])
         for k, (src, dst) in enumerate(
-            [(f_hbm, f_ref), (seed_hbm, seed_ref), (por_hbm, por_ref), (solid_hbm, solid_ref)]
+            [(f_hbm, f_ref), (por_hbm, por_ref), (solid_hbm, solid_ref), (seed_hbm, seed_ref)]
         )
     ]
     for copy in copies:
         copy.start()
-
-    def send(k, layer, ref, *where):
-        up_ref[k, 4 * layer : 4 * layer + 4, :] = ref[where + (slice(12, 16), slice(None))]
-        down_ref[k, 4 * layer : 4 * layer + 4, :] = ref[where + (slice(0, 4), slice(None))]
-
-    copies[0].wait()
-    for k in range(Q):
-        for layer in range(2):
-            send(k, layer, f_ref, k, layer)
-    copies[1].wait()
-    for k in range(Q):
-        for layer in range(2):
-            send(k + Q, layer, seed_ref, k, layer)
-    copies[2].wait()
+    for copy in copies[:3]:
+        copy.wait()
+    for layer in range(2):
+        solid = solid_ref[layer] == 1
+        b_ref[0, layer] = jnp.where(solid, 1.0, por_ref[layer])
+        fluid_ref[layer] = jnp.where(solid, 0.0, 1.0)
+
+        def body(row, layer=layer):
+            rows = slice(row, row + 8)
+            g = collided([f_ref[i, layer, rows, :] for i in range(Q)], b_ref[0, layer, rows, :])
+            for i in range(Q):
+                g_ref[i, layer, rows, :] = g[i]
+
+        tiles_loop(2, body)
     copies[3].wait()
-    for layer in range(2):
-        b_ref[layer] = jnp.where(solid_ref[layer] == 1, 1.0, por_ref[layer])
-        fluid_ref[layer] = jnp.where(solid_ref[layer] == 1, 0.0, 1.0)
-        send(2 * Q, layer, b_ref, layer)
-
-
-def columns_kernel(f_ref, seed_ref, b_ref, below_ref, above_ref, main_ref, up_ref, down_ref):
-    at = column((ROWS, LANES)) // 4
+    arrays = (g_ref, seed_ref, b_ref)
+    for ref, up in ((up_ref, True), (down_ref, False)):
+        for which, i, layer, row, count, tile, at in rows_moves(up):
+            ref[tile, at : at + count, :] = arrays[which][i, layer, row : row + count, :]
+
+
+def columns_kernel(g_ref, seed_ref, b_ref, below_ref, above_ref, main_ref, up_ref, down_ref):
+    for k in range(FIELDS):
+        for layer in range(2):
+            own = g_ref[k, layer] if k < Q else seed_ref[k - Q, layer] if k < 2 * Q else b_ref[0, layer]
+            main_ref[k, layer, 0:OWN, :] = own
+    for ref, up, shift in ((below_ref, True, ROWS - OWN), (above_ref, False, OWN)):
+        for which, i, layer, row, count, tile, at in rows_moves(up):
+            main_ref[which * Q + i, layer, row + shift : row + shift + count, :] = ref[tile, at : at + count, :]
+    at = column((ROWS, LANES))
     high = low = None
     for k in range(FIELDS):
         for layer in range(2):
-            if k < Q:
-                own = f_ref[k, layer]
-            elif k < 2 * Q:
-                own = seed_ref[k - Q, layer]
-            else:
-                own = b_ref[layer]
-            rows = slice(4 * layer, 4 * layer + 4)
-            tile = jnp.concatenate([own, above_ref[k, rows, :], below_ref[k, rows, :]], axis=0)
-            main_ref[k, layer] = tile
-            slot = (2 * k + layer) % 32
+            tile = main_ref[k, layer]
+            n = 2 * k + layer
+            slot = n % 32
             piece_up, piece_down = turn(tile, 4 * slot + 4, 1), turn(tile, 4 * slot, 1)
-            high = piece_up if slot == 0 else jnp.where(at == slot, piece_up, high)
-            low = piece_down if slot == 0 else jnp.where(at == slot, piece_down, low)
-            if slot == 31 or 2 * k + layer == 2 * FIELDS - 1:
-                up_ref[(2 * k + layer) // 32] = high
-                down_ref[(2 * k + layer) // 32] = low
+            high = piece_up if slot == 0 else jnp.where(at >= 4 * slot, piece_up, high)
+            low = piece_down if slot == 0 else jnp.where(at >= 4 * slot, piece_down, low)
+            if slot == 31 or n == 2 * FIELDS - 1:
+                up_ref[n // 32] = high
+                down_ref[n // 32] = low
 
 
 def tiles_loop(count, body):
@@ -315,57 +347,32 @@
         body(8 * n)
 
 
-def main_kernel(main_ref, g_ref):
+def rim_of(before_ref, beyond_ref, k, layer):
+    n = 2 * k + layer
+    slot, tile = n % 32, n // 32
+    before = turn(before_ref[tile], -(4 * slot + 4), 1)
+    beyond = turn(beyond_ref[tile], -4 * slot, 1)
+    return jnp.where(column((ROWS, LANES)) < RIM, beyond, before)
+
+
+def first_kernel(
+    main_ref, before_ref, beyond_ref,
+    f1_ref, edge_ref, b_ref, up_ref, down_ref,
+    level_ref, rim_ref, seed_ref,
+):
+    for i in range(Q):
+        for layer in range(2):
+            rim_ref[i, layer] = rim_of(before_ref, beyond_ref, i, layer)
+    for layer, pops in ((1, XM), (0, XP)):
+        for i in pops:
+            seed_ref[i, 0] = rim_of(before_ref, beyond_ref, Q + i, layer)
     for layer in range(2):
-
-        def body(row, layer=layer):
-            f = [main_ref[i, layer, slice(row, row + 8), :] for i in range(Q)]
-            even, odd = split(f)
-            rho, u = moments(f[0], even, odd)
-            g = collide(f[0], even, odd, rho, u, main_ref[2 * Q, layer, slice(row, row + 8), :], range(Q))
-            for i in range(Q):
-                g_ref[i, layer, slice(row, row + 8), :] = g[i]
-
-        tiles_loop(3, body)
-
-
-def first_kernel(
-    main_ref, g_ref, before_ref, beyond_ref,
-    f1_ref, edge_ref, s_ref, b_ref, up_ref, down_ref,
-    f_scr, g_scr, level_ref,
-):
-    at = column((ROWS, LANES))
-    for k in range(FIELDS):
-        for layer in range(2):
-            n = 2 * k + layer
-            slot, tile = n % 32, n // 32
-            before = turn(before_ref[tile], -(4 * slot + 4), 1)
-            beyond = turn(beyond_ref[tile], -4 * slot, 1)
-            rim = jnp.where(at < RIM, beyond, before)
-            if k < Q:
-                f_scr[k, layer] = rim
-            elif k < 2 * Q:
-                s_ref[k - Q, layer] = rim
-            else:
-                b_ref[layer, 0] = main_ref[k, layer]
-                b_ref[layer, 1] = rim
-
-    for layer in range(2):
-
-        def body(row, layer=layer):
-            f = [f_scr[i, layer, slice(row, row + 8), :] for i in range(Q)]
-            even, odd = split(f)
-            rho, u = moments(f[0], even, odd)
-            g = collide(f[0], even, odd, rho, u, b_ref[layer, 1, slice(row, row + 8), :], range(Q))
-            for i in range(Q):
-                g_scr[i, layer, slice(row, row + 8), :] = g[i]
-
-        tiles_loop(3, body)
-
+        b_ref[layer, 0] = main_ref[2 * Q, layer]
+        b_ref[layer, 1] = rim_of(before_ref, beyond_ref, 2 * Q, layer)
     for i in range(Q):
         for layer in range(2):
             to = layer + VEL[i][0]
-            tiles = moved(g_ref[i, layer], g_scr[i, layer], i, 1)
+            tiles = moved(main_ref[i, layer], rim_ref[i, layer], i, 1)
             for lane in range(2):
                 if to in (0, 1):
                     f1_ref[i, to, lane] = tiles[lane]
@@ -389,20 +396,24 @@
         out.append(pick(b_ref, layer))
         out += [pick(edge_ref, i) for i in forward]
         for i in backward:
-            pair = moved(main_ref[Q + i, layer], s_ref[i, layer], i, -1)
-            out.append(((lambda pair=pair: pair[0]), (lambda pair=pair: pair[1])))
+            seed_ref[i, 0], seed_ref[i, 1] = moved(main_ref[Q + i, layer], seed_ref[i, 0], i, -1)
+            out.append(pick(seed_ref, i))
         return out
 
     pack1(up_ref, tiles_of(XP, XM, 1))
     pack1(down_ref, tiles_of(XM, XP, 0))
 
 
-def seed_kernel(main_ref, s_ref, b2_ref):
+def seed_kernel(main_ref, before_ref, beyond_ref, b2_ref, rim_ref):
+    for i in range(Q):
+        for layer in range(2):
+            if layer - VEL[i][0] in (0, 1):
+                rim_ref[i, layer] = rim_of(before_ref, beyond_ref, Q + i, layer)
     for i in range(Q):
         for layer in range(2):
             to = layer - VEL[i][0]
             if to in (0, 1):
-                main, rim = moved(main_ref[Q + i, layer], s_ref[i, layer], i, -1)
+                main, rim = moved(main_ref[Q + i, layer], rim_ref[i, layer], i, -1)
                 b2_ref[i, to, 0] = main
                 b2_ref[i, to, 1] = rim
 
@@ -629,24 +640,24 @@
     half, tile = (2, 2, ROWS, LANES), (ROWS, LANES)
     inputs = [placed(x) for x in (populations, porosity, solid, seed_adjoint)]
     block = populations.shape
-    up, down, f, seed, b, fluid = call(
+    cells = block[1:]
+    up, down, f, seed, g, own_b, fluid = call(
         rows_kernel,
-        [(FIELDS, 8, LANES)] * 2 + [block, block, block[1:], block[1:]],
-        [block[1:]],
-        [pltpu.VMEM(block[1:], jnp.int32), pltpu.SemaphoreType.DMA((4,))],
+        [(YTILES, 8, LANES)] * 2 + [block, block, block, (1,) + cells, cells],
+        [cells],
+        [pltpu.VMEM(cells, jnp.int32), pltpu.SemaphoreType.DMA((4,))],
         space=[pltpu.HBM] * 4,
     )(*inputs)
     below, above = both_ways(up, down, "gy")
-    main, up, down = call(columns_kernel, [(FIELDS, 2) + tile] + [(ZTILES,) + tile] * 2)(f, seed, b, below, above)
+    main, up, down = call(columns_kernel, [(FIELDS, 2) + tile] + [(ZTILES,) + tile] * 2)(g, seed, own_b, below, above)
     before, beyond = both_ways(up, down, "gz")
-    (g,) = call(main_kernel, [(Q, 2) + tile])(main)
-    f1, edge, s, b, up, down = call(
+    f1, edge, b, up, down = call(
         first_kernel,
-        [(Q,) + half, (Q, 2) + tile, (Q, 2) + tile, half] + [(SEND1 + 1,) + tile] * 2,
-        [(Q, 2) + tile] * 2 + [(3,) + half],
-    )(main, g, before, beyond)
+        [(Q,) + half, (Q, 2) + tile, half] + [(SEND1 + 1,) + tile] * 2,
+        [(3,) + half, (Q, 2) + tile, (Q, 2) + tile],
+    )(main, before, beyond)
     left1, right1 = both_ways(up, down, "gx")
-    (b2,) = call(seed_kernel, [(Q,) + half])(main, s)
+    (b2,) = call(seed_kernel, [(Q,) + half], [(Q, 2) + tile])(main, before, beyond)
     sides = []
     for side, got in enumerate((left1, right1)):
         sides.append(

time: 50.6 us -> 49.5 us (0.978)
  starting transfers between devices: 24.7 us -> 24.1 us
    ppermute x4, waiting for transfers between devices: 10.5 us -> 9.84 us  [both_ways(): lax.ppermute(up, axis, ring)]
    ppermute x4, starting transfers between devices: 11.3 us -> 10.7 us  [both_ways(): lax.ppermute(down, axis, [(j, i) for i, j in ring])]
    pallas_call x4 -> x3, Pallas kernels: 2.45 us -> 2.24 us  [the longest x1 1.2 us: body(): call(rows_kernel, [(YTILES, 8, LANES)] * 2 + [block, block, block, (1,) +...]
where the time goes in v5:
time: 49.5 us; the launch traced here: 49.1 us
  starting transfers between devices  24.1 us (49%)
  waiting for transfers between devices  18.4 us (37%)
  Pallas kernels  5.88 us (12%)
  between operations  0.74 us (1%)
    ppermute x4, starting transfers between devices, both_ways(): lax.ppermute(up, axis, ring)  13.4 us
    ppermute x4, starting transfers between devices, both_ways(): lax.ppermute(down, axis, [(j, i) for i, j in ring])  10.7 us
    ppermute x4, waiting for transfers between devices, both_ways(): lax.ppermute(up, axis, ring)  9.84 us
    ppermute x4, waiting for transfers between devices, both_ways(): lax.ppermute(down, axis, [(j, i) for i, j in ring])  8.57 us
    pallas_call x1, Pallas kernels, body(): call(rows_kernel, [(YTILES, 8, LANES)] * 2 + [block, block, block, (1,) +...  1.2 us
    pallas_call x1, Pallas kernels, body(): call(middle_kernel, [(2, OWN, LANES), (Q,) + half, (Q, 2) + tile, (4,) +...  1.01 us
  transfers between devices with their start and end apart: 8, of which 7 were waited for; matrix products, arithmetic and copies ran while one was open for 0% of the time, Pallas kernels for 2%

profile of v5, /device:TPU:24, one launch (start us, length us, event | category | flops | bytes accessed | tf_op | source)
XLA Modules:
  0.0 49.1 jit_solution(16248624559500085496)
XLA Ops:
  0.6 1.2 %shard_map.59 = (f32[29,8,128]{2,1,0:T(8,128)S(1)}, f32[29,8,128]{2,1,0:T(8,128)S(1)}, f32[19,2,16,128]{3,2,1,0:T(8,128)S(1)}, f32[19,2,16,128]{3,2,1,0:T(8,128)...) custom-call(f32[19,2,16,128]{3,2,1,0:T(8,128)} %f_hbm.1, ...), custom_call_target="tpu_custom_call" | custom-call | flops 2000000 | bytes 1000000 | tf_op jit(solution)/shard_map/pallas_call | solution.py:644
  1.8 7.5 %collective-permute-start = (f32[29,8,128]{2,1,0:T(8,128)S(1)}, f32[29,8,128]{2,1,0:T(8,128)S(1)}, u32[]{:S(2)}, u32[]{:S(2)}) collective-permute-start(f32[29,8,128]{2,1,0:T(8,128)S(1)} %get-tuple-element.42), channel_id=1, source_target_pairs={{0,32},{32,64},{64,96},{96,0},{1,33},{33,65},{65,97},{97,1},{2,34}... | collective-permute-start | bytes 356360 | tf_op jit(solution)/shard_map/ppermute | solution.py:636
  9.4 1.9 %collective-permute-start.1 = (f32[29,8,128]{2,1,0:T(8,128)S(1)}, f32[29,8,128]{2,1,0:T(8,128)S(1)}, u32[]{:S(2)}, u32[]{:S(2)}) collective-permute-start(f32[29,8,128]{2,1,0:T(8,128)S(1)} %get-tuple-element.43), channel_id=1, source_target_pairs={{32,0},{64,32},{96,64},{0,96},{33,1},{65,33},{97,65},{1,97},{34,2}... | collective-permute-start | bytes 356360 | tf_op jit(solution)/shard_map/ppermute | solution.py:636
  11.3 0.5 collective-permute-done.below_ref
  11.7 5.6 %collective-permute-done.1.above_ref = f32[29,8,128]{2,1,0:T(8,128)S(1)} collective-permute-done((f32[29,8,128]{2,1,0:T(8,128)S(1)}, f32[29,8,128]{2,1,0:T(8,128)S(1)}, u32[]{:S(2)}, u32[]{:S(2)}) %collective-permute-start.1) | collective-permute-done | bytes 118816 | tf_op jit(solution)/shard_map/ppermute | solution.py:636
  17.3 0.6 %shard_map.60 = (f32[39,2,24,128]{3,2,1,0:T(8,128)S(1)}, f32[3,24,128]{2,1,0:T(8,128)S(1)}, f32[3,24,128]{2,1,0:T(8,128)S(1)}) custom-call(f32[19,2,16,128]{3,2,1,0:T(8,128)S(1)} %get-tuple-element.39.g_ref, f32[19,2,16,128]{3,2,1,0:T(8,128)S(1)} %get-tuple-element.40.seed_ref, f32[1,2,16,128]{3,2,1,0:T(8,128)S(1)} %get-tuple-element.41.b_ref, ...), custom_call_target="tpu_custom_call" | custom-call | flops 2000000 | bytes 1000000 | tf_op jit(solution)/shard_map/pallas_call | solution.py:652
  17.9 0.0 collective-permute-start.2
  17.9 2.9 %collective-permute-start.3 = (f32[3,24,128]{2,1,0:T(8,128)S(1)}, f32[3,24,128]{2,1,0:T(8,128)S(1)}, u32[]{:S(2)}, u32[]{:S(2)}) collective-permute-start(f32[3,24,128]{2,1,0:T(8,128)S(1)} %get-tuple-element.46), channel_id=1, source_target_pairs={{1,0},{2,1},{3,2},{4,3},{5,4},{6,5},{7,6},{8,7},{9,8},{10,9},{11,1... | collective-permute-start | bytes 110600 | tf_op jit(solution)/shard_map/ppermute | solution.py:636
  20.8 1.6 %collective-permute-done.2.before_ref = f32[3,24,128]{2,1,0:T(8,128)S(1)} collective-permute-done((f32[3,24,128]{2,1,0:T(8,128)S(1)}, f32[3,24,128]{2,1,0:T(8,128)S(1)}, u32[]{:S(2)}, u32[]{:S(2)}) %collective-permute-start.2) | collective-permute-done | bytes 36896 | tf_op jit(solution)/shard_map/ppermute | solution.py:636
  22.5 0.0 collective-permute-done.3.beyond_ref
  22.5 0.7 %shard_map.61 = (f32[19,2,2,24,128]{4,3,2,1,0:T(8,128)S(1)}, f32[19,2,24,128]{3,2,1,0:T(8,128)S(1)}, f32[2,2,24,128]{3,2,1,0:T(8,128)S(1)}, f32[20,24,128]{2,1,0:T(8,128)S(1)}, f32[20,24,128]{2,1,0:T(8,128)S(1)}) custom-call(f32[39,2,24,128]{3,2,1,0:T(8,128)S(1)} %get-tuple-element.44.main_ref, f32[3,24,128]{2,1,0:T(8,128)S(1)} %collective-permute-done.2.before_ref, ...), custom_call_target="tpu_custom_call" | custom-call | flops 2000000 | bytes 1000000 | tf_op jit(solution)/shard_map/pallas_call | solution.py:654
  23.2 3.9 %collective-permute-start.5 = (f32[20,24,128]{2,1,0:T(8,128)S(1)}, f32[20,24,128]{2,1,0:T(8,128)S(1)}, u32[]{:S(2)}, u32[]{:S(2)}) collective-permute-start(f32[20,24,128]{2,1,0:T(8,128)S(1)} %get-tuple-element.49), channel_id=1, source_target_pairs={{128,0},{256,128},{384,256},{0,384},{129,1},{257,129},{385,257},{1... | collective-permute-start | bytes 737288 | tf_op jit(solution)/shard_map/ppermute | solution.py:636
  27.1 1.9 %collective-permute-start.4 = (f32[20,24,128]{2,1,0:T(8,128)S(1)}, f32[20,24,128]{2,1,0:T(8,128)S(1)}, u32[]{:S(2)}, u32[]{:S(2)}) collective-permute-start(f32[20,24,128]{2,1,0:T(8,128)S(1)} %get-tuple-element.48), channel_id=1, source_target_pairs={{0,128},{128,256},{256,384},{384,0},{1,129},{129,257},{257,385},{3... | collective-permute-start | bytes 737288 | tf_op jit(solution)/shard_map/ppermute | solution.py:636
  29.0 0.3 shard_map.62.b2_ref
  29.4 1.9 %collective-permute-done.5.got_ref.right_ref.got1_ref = f32[20,24,128]{2,1,0:T(8,128)S(1)} collective-permute-done((f32[20,24,128]{2,1,0:T(8,128)S(1)}, f32[20,24,128]{2,1,0:T(8,128)S(1)}, u32[]{:S(2)}, u32[]{:S(2)}) %collective-permute-start.5) | collective-permute-done | bytes 245792 | tf_op jit(solution)/shard_map/ppermute | solution.py:636
  31.3 0.2 shard_map.64
  31.5 4.9 %collective-permute-done.4.got_ref.left_ref.got1_ref = f32[20,24,128]{2,1,0:T(8,128)S(1)} collective-permute-done((f32[20,24,128]{2,1,0:T(8,128)S(1)}, f32[20,24,128]{2,1,0:T(8,128)S(1)}, u32[]{:S(2)}, u32[]{:S(2)}) %collective-permute-start.4) | collective-permute-done | bytes 245792 | tf_op jit(solution)/shard_map/ppermute | solution.py:636
  36.4 0.2 shard_map.63
  36.7 1.0 %shard_map.65 = (f32[2,16,128]{2,1,0:T(8,128)S(1)}, f32[19,2,2,24,128]{4,3,2,1,0:T(8,128)S(1)}, f32[19,2,24,128]{3,2,1,0:T(8,128)S(1)}, f32[4,2,2,24,128]{4,3,2,...) custom-call(f32[2,2,24,128]{3,2,1,0:T(8,128)S(1)} %get-tuple-element.47.b_ref, ...), custom_call_target="tpu_custom_call" | custom-call | flops 2000000 | bytes 1000000 | tf_op jit(solution)/shard_map/pallas_call | solution.py:671
  37.7 1.9 %collective-permute-start.7 = (f32[35,8,128]{2,1,0:T(8,128)S(1)}, f32[35,8,128]{2,1,0:T(8,128)S(1)}, u32[]{:S(2)}, u32[]{:S(2)}) collective-permute-start(f32[35,8,128]{2,1,0:T(8,128)S(1)} %get-tuple-element.68), channel_id=1, source_target_pairs={{128,0},{256,128},{384,256},{0,384},{129,1},{257,129},{385,257},{1... | collective-permute-start | bytes 430088 | tf_op jit(solution)/shard_map/ppermute | solution.py:636
  39.6 3.9 %collective-permute-start.6 = (f32[35,8,128]{2,1,0:T(8,128)S(1)}, f32[35,8,128]{2,1,0:T(8,128)S(1)}, u32[]{:S(2)}, u32[]{:S(2)}) collective-permute-start(f32[35,8,128]{2,1,0:T(8,128)S(1)} %get-tuple-element.64), channel_id=1, source_target_pairs={{0,128},{128,256},{256,384},{384,0},{1,129},{129,257},{257,385},{3... | collective-permute-start | bytes 430088 | tf_op jit(solution)/shard_map/ppermute | solution.py:636
  43.5 1.1 %collective-permute-done.7.got_ref = f32[35,8,128]{2,1,0:T(8,128)S(1)} collective-permute-done((f32[35,8,128]{2,1,0:T(8,128)S(1)}, f32[35,8,128]{2,1,0:T(8,128)S(1)}, u32[]{:S(2)}, u32[]{:S(2)}) %collective-permute-start.7) | collective-permute-done | bytes 143392 | tf_op jit(solution)/shard_map/ppermute | solution.py:636
  44.7 0.3 shard_map.67
  45.0 2.8 %collective-permute-done.6.got_ref = f32[35,8,128]{2,1,0:T(8,128)S(1)} collective-permute-done((f32[35,8,128]{2,1,0:T(8,128)S(1)}, f32[35,8,128]{2,1,0:T(8,128)S(1)}, u32[]{:S(2)}, u32[]{:S(2)}) %collective-permute-start.6) | collective-permute-done | bytes 143392 | tf_op jit(solution)/shard_map/ppermute | solution.py:636
  47.8 0.3 shard_map.66
  48.1 1.0 %shard_map.68 = (f32[2,16,128]{2,1,0:T(8,128)}, f32[19,2,16,128]{3,2,1,0:T(8,128)}) custom-call(f32[2,2,24,128]{3,2,1,0:T(8,128)S(1)} %get-tuple-element.47.b_ref, f32[16,128]{1,0:T(8,128)S(1)} %get-tuple-element.65.grad0_ref, f32[16,128]{1,0:T(8,128)S(1)} %get-tuple-element.69.grad1_ref, f32[19,2,24,128]{3,2,1,0:T(8,128)S(1)} %get-tuple-element.70.a_left_ref, ...), custom_call_target="tpu_custom_call" | custom-call | flops 2000000 | bytes 1000000 | tf_op jit(solution)/shard_map/pallas_call | solution.py:687
Async XLA Ops:
  1.8 9.9 %collective-permute-start = (f32[29,8,128]{2,1,0:T(8,128)S(1)}, f32[29,8,128]{2,1,0:T(8,128)S(1)}, u32[]{:S(2)}, u32[]{:S(2)}) collective-permute-start(f32[29,8,128]{2,1,0:T(8,128)S(1)} %get-tuple-element.42), channel_id=1, source_target_pairs={{0,32},{32,64},{64,96},{96,0},{1,33},{33,65},{65,97},{97,1},{2,34}... | collective-permute-start | bytes 356360 | tf_op jit(solution)/shard_map/ppermute | solution.py:636
  9.4 7.9 %collective-permute-start.1 = (f32[29,8,128]{2,1,0:T(8,128)S(1)}, f32[29,8,128]{2,1,0:T(8,128)S(1)}, u32[]{:S(2)}, u32[]{:S(2)}) collective-permute-start(f32[29,8,128]{2,1,0:T(8,128)S(1)} %get-tuple-element.43), channel_id=1, source_target_pairs={{32,0},{64,32},{96,64},{0,96},{33,1},{65,33},{97,65},{1,97},{34,2}... | collective-permute-start | bytes 356360 | tf_op jit(solution)/shard_map/ppermute | solution.py:636
  17.9 4.6 %collective-permute-start.2 = (f32[3,24,128]{2,1,0:T(8,128)S(1)}, f32[3,24,128]{2,1,0:T(8,128)S(1)}, u32[]{:S(2)}, u32[]{:S(2)}) collective-permute-start(f32[3,24,128]{2,1,0:T(8,128)S(1)} %get-tuple-element.45), channel_id=1, source_target_pairs={{0,1},{1,2},{2,3},{3,4},{4,5},{5,6},{6,7},{7,8},{8,9},{9,10},{10,1... | collective-permute-start | bytes 110600 | tf_op jit(solution)/shard_map/ppermute | solution.py:636
  17.9 4.6 %collective-permute-start.3 = (f32[3,24,128]{2,1,0:T(8,128)S(1)}, f32[3,24,128]{2,1,0:T(8,128)S(1)}, u32[]{:S(2)}, u32[]{:S(2)}) collective-permute-start(f32[3,24,128]{2,1,0:T(8,128)S(1)} %get-tuple-element.46), channel_id=1, source_target_pairs={{1,0},{2,1},{3,2},{4,3},{5,4},{6,5},{7,6},{8,7},{9,8},{10,9},{11,1... | collective-permute-start | bytes 110600 | tf_op jit(solution)/shard_map/ppermute | solution.py:636
  23.2 8.1 %collective-permute-start.5 = (f32[20,24,128]{2,1,0:T(8,128)S(1)}, f32[20,24,128]{2,1,0:T(8,128)S(1)}, u32[]{:S(2)}, u32[]{:S(2)}) collective-permute-start(f32[20,24,128]{2,1,0:T(8,128)S(1)} %get-tuple-element.49), channel_id=1, source_target_pairs={{128,0},{256,128},{384,256},{0,384},{129,1},{257,129},{385,257},{1... | collective-permute-start | bytes 737288 | tf_op jit(solution)/shard_map/ppermute | solution.py:636
  27.1 9.3 %collective-permute-start.4 = (f32[20,24,128]{2,1,0:T(8,128)S(1)}, f32[20,24,128]{2,1,0:T(8,128)S(1)}, u32[]{:S(2)}, u32[]{:S(2)}) collective-permute-start(f32[20,24,128]{2,1,0:T(8,128)S(1)} %get-tuple-element.48), channel_id=1, source_target_pairs={{0,128},{128,256},{256,384},{384,0},{1,129},{129,257},{257,385},{3... | collective-permute-start | bytes 737288 | tf_op jit(solution)/shard_map/ppermute | solution.py:636
  37.7 7.0 %collective-permute-start.7 = (f32[35,8,128]{2,1,0:T(8,128)S(1)}, f32[35,8,128]{2,1,0:T(8,128)S(1)}, u32[]{:S(2)}, u32[]{:S(2)}) collective-permute-start(f32[35,8,128]{2,1,0:T(8,128)S(1)} %get-tuple-element.68), channel_id=1, source_target_pairs={{128,0},{256,128},{384,256},{0,384},{129,1},{257,129},{385,257},{1... | collective-permute-start | bytes 430088 | tf_op jit(solution)/shard_map/ppermute | solution.py:636
  39.6 8.2 %collective-permute-start.6 = (f32[35,8,128]{2,1,0:T(8,128)S(1)}, f32[35,8,128]{2,1,0:T(8,128)S(1)}, u32[]{:S(2)}, u32[]{:S(2)}) collective-permute-start(f32[35,8,128]{2,1,0:T(8,128)S(1)} %get-tuple-element.64), channel_id=1, source_target_pairs={{0,128},{128,256},{256,384},{384,0},{1,129},{129,257},{257,385},{3... | collective-permute-start | bytes 430088 | tf_op jit(solution)/shard_map/ppermute | solution.py:636

commit v6 on v5

--- a/solution.py
+++ b/solution.py
@@ -180,14 +180,14 @@
     return main, rim
 
 
-def pack_rims(ref, place, tiles, width):
+def packed_rims(tiles, width):
     at = column((ROWS, LANES))
     joined, first = None, 0
     for k, (_, rim) in enumerate(tiles):
         piece = turn(rim(), first + width[k] // 2, 1)
         joined = piece if joined is None else jnp.where(at >= first, piece, joined)
         first += width[k]
-    ref[place] = joined
+    return joined
 
 
 def unpack_rims(tile, width, out):
@@ -203,17 +203,36 @@
 ROWTILES2 = 2 * SEND2 + -(-SEND2 // 4)
 
 
+STRIPS1 = [sum(WIDTH1[:k]) + OWN * SEND1 for k in range(SEND1 + 1)]
+
+
 def pack1(ref, tiles):
     for k, (main, _) in enumerate(tiles):
-        ref[k] = main()
-    pack_rims(ref, SEND1, tiles, WIDTH1)
-
-
-def unpack1(ref, rim_ref):
+        tile, half, at = main(), WIDTH1[k] // 2, STRIPS1[k]
+        ref[OWN * k : OWN * k + OWN, :] = tile[0:OWN]
+        ref[at : at + half, :] = tile[ROWS - half : ROWS]
+        ref[at + half : at + 2 * half, :] = tile[OWN : OWN + half]
+    ref[STRIPS1[-1] : STRIPS1[-1] + ROWS, :] = packed_rims(tiles, WIDTH1)
+
+
+def unpack1(ref, beyond_ref, rim_ref, first=0):
+    for k in range(first, SEND1):
+        half, at = WIDTH1[k] // 2, STRIPS1[k]
+        beyond_ref[k, 8 - half : 8, :] = ref[at : at + half, :]
+        beyond_ref[k, 0:half, :] = ref[at + half : at + 2 * half, :]
+
     def out(k, rim):
-        rim_ref[k] = rim
-
-    unpack_rims(ref[SEND1], WIDTH1, out)
+        if k >= first:
+            rim_ref[k] = rim
+
+    unpack_rims(ref[STRIPS1[-1] : STRIPS1[-1] + ROWS, :], WIDTH1, out)
+
+    def tile(k, lane, row):
+        if lane:
+            return rim_ref[k, row : row + 8, :]
+        return ref[OWN * k + row : OWN * k + row + 8, :] if row < OWN else beyond_ref[k]
+
+    return tile
 
 
 def pack2(ref, rim_ref, tiles):
@@ -227,7 +246,7 @@
         joined = piece if slot == 0 else jnp.where(at >= slot, piece, joined)
         if slot == 6 or k == SEND2 - 1:
             ref[2 * SEND2 + k // 4] = joined
-    pack_rims(rim_ref, 0, tiles, WIDTH2)
+    rim_ref[0] = packed_rims(tiles, WIDTH2)
     for k in range(3):
         ref[ROWTILES2 + k] = rim_ref[0, 8 * k : 8 * k + 8, :]
 
@@ -418,18 +437,15 @@
                 b2_ref[i, to, 1] = rim
 
 
-def side_kernel(side, f1_ref, edge_ref, b_ref, got_ref, mom_ref, far_ref, bh_ref, g_ref, far_g_ref, rim_scr):
-    unpack1(got_ref, rim_scr)
-    got = (got_ref, rim_scr)
+def side_kernel(side, f1_ref, edge_ref, b_ref, got_ref, mom_ref, far_ref, bh_ref, g_ref, far_g_ref, beyond_scr, rim_scr):
+    got = unpack1(got_ref, beyond_scr, rim_scr)
     theirs, ours = (XP, XM) if side == 0 else (XM, XP)
     for lane in range(2):
-        bh_ref[lane] = got[lane][8]
-
         def near(row, lane=lane):
             rows = slice(row, row + 8)
             f = [None if i in theirs else f1_ref[i, side, lane, rows, :] for i in range(Q)]
             for k, i in enumerate(theirs):
-                f[i] = got[lane][9 + k, rows, :]
+                f[i] = got(9 + k, lane, row)
             even, odd = split(f)
             rho, u = moments(f[0], even, odd)
             mom_ref[3, lane, rows, :] = rho
@@ -443,14 +459,16 @@
             rows = slice(row, row + 8)
             f = [None] * Q
             for k, i in enumerate(theirs):
-                f[i] = got[lane][k, rows, :]
+                f[i] = got(k, lane, row)
             for i in ours:
                 f[i] = edge_ref[i, lane, rows, :]
             even, odd = split(f, XP)
-            rho, u = moments_from([got[lane][5 + k, rows, :] for k in range(3)], even, odd)
+            rho, u = moments_from([got(5 + k, lane, row) for k in range(3)], even, odd)
             for axis in range(3):
                 far_ref[axis, lane, rows, :] = u[axis]
-            g = collide(None, even, odd, rho, u, got[lane][8, rows, :], theirs)
+            blocking = got(8, lane, row)
+            bh_ref[lane, rows, :] = blocking
+            g = collide(None, even, odd, rho, u, blocking, theirs)
             for i in theirs:
                 far_g_ref[i, lane, rows, :] = g[i]
 
@@ -461,18 +479,9 @@
 def middle_kernel(
     b_ref, b2_ref, left_ref, right_ref, mom0_ref, mom1_ref, g0_ref, g1_ref, g_left_ref, g_right_ref,
     grad_ref, b1_ref, edge1_ref, sums_ref, up_ref, down_ref,
-    l_scr, r_scr, f_scr, a_scr, rim_scr,
+    l_beyond, l_scr, r_beyond, r_scr, f_scr, a_scr, rim_scr,
 ):
-    def out(scr):
-        def put(k, rim):
-            if k >= 14:
-                scr[k] = rim
-
-        return put
-
-    unpack_rims(left_ref[SEND1], WIDTH1, out(l_scr))
-    unpack_rims(right_ref[SEND1], WIDTH1, out(r_scr))
-    got = ((left_ref, right_ref), (l_scr, r_scr))
+    got = (unpack1(left_ref, l_beyond, l_scr, 14), unpack1(right_ref, r_beyond, r_scr, 14))
     g_refs = (g_left_ref, g0_ref, g1_ref, g_right_ref)
     mom = (mom0_ref, mom1_ref)
 
@@ -492,7 +501,7 @@
                 f = [f_scr[i, layer, lane, rows, :] for i in range(Q)]
                 b = {i: b2_ref[i, layer, lane, rows, :] for i in range(Q) if i not in missing}
                 for k, i in enumerate(missing):
-                    b[i] = got[lane][layer][14 + k, rows, :]
+                    b[i] = got[layer](14 + k, lane, row)
                 even, odd = split(f)
                 rho, u = moments(f[0], even, odd)
                 b_even, b_odd = split(b)
@@ -573,7 +582,7 @@
             if lane == 0 and row < OWN:
                 f = {i: f1_ref[i, side, lane, rows, :] for i in range(Q) if i not in far_pops}
                 for k, i in enumerate(far_pops):
-                    f[i] = got1_ref[9 + k, rows, :]
+                    f[i] = got1_ref[OWN * (9 + k) + row : OWN * (9 + k) + row + 8, :]
                 grad = gradient_of((b[0], even, odd), (f[0],) + split(f), mom_ref[3, lane, rows, :], sums[0])
                 out_grad_ref[rows, :] = grad + grad_ref[side, rows, :]
 
@@ -653,7 +662,7 @@
     before, beyond = both_ways(up, down, "gz")
     f1, edge, b, up, down = call(
         first_kernel,
-        [(Q,) + half, (Q, 2) + tile, half] + [(SEND1 + 1,) + tile] * 2,
+        [(Q,) + half, (Q, 2) + tile, half] + [(STRIPS1[-1] + ROWS, LANES)] * 2,
         [(3,) + half, (Q, 2) + tile, (Q, 2) + tile],
     )(main, before, beyond)
     left1, right1 = both_ways(up, down, "gx")
@@ -664,14 +673,14 @@
             call(
                 functools.partial(side_kernel, side),
                 [(4, 2) + tile, (3, 2) + tile, (2,) + tile, (Q, 2) + tile, (Q, 2) + tile],
-                [(SEND1,) + tile],
+                [(SEND1, 8, LANES), (SEND1,) + tile],
             )(f1, edge, b, got)
         )
     (mom0, far0, bh0, g0, g_left), (mom1, far1, bh1, g1, g_right) = sides
     grad, b1, edge1, sums, up, down = call(
         middle_kernel,
         [(2, OWN, LANES), (Q,) + half, (Q, 2) + tile, (4,) + half] + [(ROWTILES2 + 3, 8, LANES)] * 2,
-        [(SEND1,) + tile] * 2 + [(Q,) + half, (Q,) + half, (1,) + tile],
+        [(SEND1, 8, LANES), (SEND1,) + tile] * 2 + [(Q,) + half, (Q,) + half, (1,) + tile],
     )(b, b2, left1, right1, mom0, mom1, g0, g1, g_left, g_right)
     left, right = both_ways(up, down, "gx")
     sides = []

time: 49.5 us -> 49.2 us (level)
  no operation moved by 1% of the time
where the time goes in v6:
time: 49.2 us; the launch traced here: 48.8 us
  starting transfers between devices  24.1 us (49%)
  waiting for transfers between devices  18.1 us (37%)
  Pallas kernels  5.89 us (12%)
  between operations  0.73 us (1%)
    ppermute x4, starting transfers between devices, both_ways(): lax.ppermute(up, axis, ring)  13.4 us
    ppermute x4, starting transfers between devices, both_ways(): lax.ppermute(down, axis, [(j, i) for i, j in ring])  10.7 us
    ppermute x4, waiting for transfers between devices, both_ways(): lax.ppermute(up, axis, ring)  9.83 us
    ppermute x4, waiting for transfers between devices, both_ways(): lax.ppermute(down, axis, [(j, i) for i, j in ring])  8.3 us
    pallas_call x1, Pallas kernels, body(): call(rows_kernel, [(YTILES, 8, LANES)] * 2 + [block, block, block, (1,) +...  1.2 us
    pallas_call x1, Pallas kernels, body(): call(middle_kernel, [(2, OWN, LANES), (Q,) + half, (Q, 2) + tile, (4,) +...  1 us
    pallas_call x1, Pallas kernels, body(): call(last_kernel, [(2, OWN, LANES), (Q, 2, OWN, LANES)], [(Q, 2, OWN, LAN...  0.99 us
  transfers between devices with their start and end apart: 8, of which 7 were waited for; matrix products, arithmetic and copies ran while one was open for 0% of the time, Pallas kernels for 2%

profile of v6, /device:TPU:24, one launch (start us, length us, event | category | flops | bytes accessed | tf_op | source)
XLA Modules:
  0.0 48.8 jit_solution(5385411502728825377)
XLA Ops:
  0.6 1.2 %shard_map.59 = (f32[29,8,128]{2,1,0:T(8,128)S(1)}, f32[29,8,128]{2,1,0:T(8,128)S(1)}, f32[19,2,16,128]{3,2,1,0:T(8,128)S(1)}, f32[19,2,16,128]{3,2,1,0:T(8,128)...) custom-call(f32[19,2,16,128]{3,2,1,0:T(8,128)} %f_hbm.1, ...), custom_call_target="tpu_custom_call" | custom-call | flops 2000000 | bytes 1000000 | tf_op jit(solution)/shard_map/pallas_call | solution.py:653
  1.8 7.5 %collective-permute-start = (f32[29,8,128]{2,1,0:T(8,128)S(1)}, f32[29,8,128]{2,1,0:T(8,128)S(1)}, u32[]{:S(2)}, u32[]{:S(2)}) collective-permute-start(f32[29,8,128]{2,1,0:T(8,128)S(1)} %get-tuple-element.42), channel_id=1, source_target_pairs={{0,32},{32,64},{64,96},{96,0},{1,33},{33,65},{65,97},{97,1},{2,34}... | collective-permute-start | bytes 356360 | tf_op jit(solution)/shard_map/ppermute | solution.py:645
  9.4 1.9 %collective-permute-start.1 = (f32[29,8,128]{2,1,0:T(8,128)S(1)}, f32[29,8,128]{2,1,0:T(8,128)S(1)}, u32[]{:S(2)}, u32[]{:S(2)}) collective-permute-start(f32[29,8,128]{2,1,0:T(8,128)S(1)} %get-tuple-element.43), channel_id=1, source_target_pairs={{32,0},{64,32},{96,64},{0,96},{33,1},{65,33},{97,65},{1,97},{34,2}... | collective-permute-start | bytes 356360 | tf_op jit(solution)/shard_map/ppermute | solution.py:645
  11.3 0.5 collective-permute-done.below_ref
  11.7 5.6 %collective-permute-done.1.above_ref = f32[29,8,128]{2,1,0:T(8,128)S(1)} collective-permute-done((f32[29,8,128]{2,1,0:T(8,128)S(1)}, f32[29,8,128]{2,1,0:T(8,128)S(1)}, u32[]{:S(2)}, u32[]{:S(2)}) %collective-permute-start.1) | collective-permute-done | bytes 118816 | tf_op jit(solution)/shard_map/ppermute | solution.py:645
  17.3 0.6 %shard_map.60 = (f32[39,2,24,128]{3,2,1,0:T(8,128)S(1)}, f32[3,24,128]{2,1,0:T(8,128)S(1)}, f32[3,24,128]{2,1,0:T(8,128)S(1)}) custom-call(f32[19,2,16,128]{3,2,1,0:T(8,128)S(1)} %get-tuple-element.39.g_ref, f32[19,2,16,128]{3,2,1,0:T(8,128)S(1)} %get-tuple-element.40.seed_ref, f32[1,2,16,128]{3,2,1,0:T(8,128)S(1)} %get-tuple-element.41.b_ref, ...), custom_call_target="tpu_custom_call" | custom-call | flops 2000000 | bytes 1000000 | tf_op jit(solution)/shard_map/pallas_call | solution.py:661
  17.9 0.0 collective-permute-start.2
  17.9 2.9 %collective-permute-start.3 = (f32[3,24,128]{2,1,0:T(8,128)S(1)}, f32[3,24,128]{2,1,0:T(8,128)S(1)}, u32[]{:S(2)}, u32[]{:S(2)}) collective-permute-start(f32[3,24,128]{2,1,0:T(8,128)S(1)} %get-tuple-element.46), channel_id=1, source_target_pairs={{1,0},{2,1},{3,2},{4,3},{5,4},{6,5},{7,6},{8,7},{9,8},{10,9},{11,1... | collective-permute-start | bytes 110600 | tf_op jit(solution)/shard_map/ppermute | solution.py:645
  20.8 1.6 %collective-permute-done.2.before_ref = f32[3,24,128]{2,1,0:T(8,128)S(1)} collective-permute-done((f32[3,24,128]{2,1,0:T(8,128)S(1)}, f32[3,24,128]{2,1,0:T(8,128)S(1)}, u32[]{:S(2)}, u32[]{:S(2)}) %collective-permute-start.2) | collective-permute-done | bytes 36896 | tf_op jit(solution)/shard_map/ppermute | solution.py:645
  22.5 0.0 collective-permute-done.3.beyond_ref
  22.5 0.7 %shard_map.61 = (f32[19,2,2,24,128]{4,3,2,1,0:T(8,128)S(1)}, f32[19,2,24,128]{3,2,1,0:T(8,128)S(1)}, f32[2,2,24,128]{3,2,1,0:T(8,128)S(1)}, f32[432,128]{1,0:T(8,128)S(1)}, f32[432,128]{1,0:T(8,128)S(1)}) custom-call(f32[39,2,24,128]{3,2,1,0:T(8,128)S(1)} %get-tuple-element.44.main_ref, f32[3,24,128]{2,1,0:T(8,128)S(1)} %collective-permute-done.2.before_ref, ...), custom_call_target="tpu_custom_call" | custom-call | flops 2000000 | bytes 1000000 | tf_op jit(solution)/shard_map/pallas_call | solution.py:663
  23.2 3.9 %collective-permute-start.5 = (f32[432,128]{1,0:T(8,128)S(1)}, f32[432,128]{1,0:T(8,128)S(1)}, u32[]{:S(2)}, u32[]{:S(2)}) collective-permute-start(f32[432,128]{1,0:T(8,128)S(1)} %get-tuple-element.49), channel_id=1, source_target_pairs={{128,0},{256,128},{384,256},{0,384},{129,1},{257,129},{385,257},{1... | collective-permute-start | bytes 663560 | tf_op jit(solution)/shard_map/ppermute | solution.py:645
  27.1 1.9 %collective-permute-start.4 = (f32[432,128]{1,0:T(8,128)S(1)}, f32[432,128]{1,0:T(8,128)S(1)}, u32[]{:S(2)}, u32[]{:S(2)}) collective-permute-start(f32[432,128]{1,0:T(8,128)S(1)} %get-tuple-element.48), channel_id=1, source_target_pairs={{0,128},{128,256},{256,384},{384,0},{1,129},{129,257},{257,385},{3... | collective-permute-start | bytes 663560 | tf_op jit(solution)/shard_map/ppermute | solution.py:645
  29.0 0.3 shard_map.62.b2_ref
  29.4 1.6 %collective-permute-done.5.got_ref.right_ref.got1_ref = f32[432,128]{1,0:T(8,128)S(1)} collective-permute-done((f32[432,128]{1,0:T(8,128)S(1)}, f32[432,128]{1,0:T(8,128)S(1)}, u32[]{:S(2)}, u32[]{:S(2)}) %collective-permute-start.5) | collective-permute-done | bytes 221216 | tf_op jit(solution)/shard_map/ppermute | solution.py:645
  31.0 0.3 shard_map.64
  31.3 4.9 %collective-permute-done.4.got_ref.left_ref.got1_ref = f32[432,128]{1,0:T(8,128)S(1)} collective-permute-done((f32[432,128]{1,0:T(8,128)S(1)}, f32[432,128]{1,0:T(8,128)S(1)}, u32[]{:S(2)}, u32[]{:S(2)}) %collective-permute-start.4) | collective-permute-done | bytes 221216 | tf_op jit(solution)/shard_map/ppermute | solution.py:645
  36.2 0.3 shard_map.63
  36.4 1.0 %shard_map.65 = (f32[2,16,128]{2,1,0:T(8,128)S(1)}, f32[19,2,2,24,128]{4,3,2,1,0:T(8,128)S(1)}, f32[19,2,24,128]{3,2,1,0:T(8,128)S(1)}, f32[4,2,2,24,128]{4,3,2,...) custom-call(f32[2,2,24,128]{3,2,1,0:T(8,128)S(1)} %get-tuple-element.47.b_ref, ...), custom_call_target="tpu_custom_call" | custom-call | flops 2000000 | bytes 1000000 | tf_op jit(solution)/shard_map/pallas_call | solution.py:680
  37.4 1.9 %collective-permute-start.7 = (f32[35,8,128]{2,1,0:T(8,128)S(1)}, f32[35,8,128]{2,1,0:T(8,128)S(1)}, u32[]{:S(2)}, u32[]{:S(2)}) collective-permute-start(f32[35,8,128]{2,1,0:T(8,128)S(1)} %get-tuple-element.68), channel_id=1, source_target_pairs={{128,0},{256,128},{384,256},{0,384},{129,1},{257,129},{385,257},{1... | collective-permute-start | bytes 430088 | tf_op jit(solution)/shard_map/ppermute | solution.py:645
  39.4 3.9 %collective-permute-start.6 = (f32[35,8,128]{2,1,0:T(8,128)S(1)}, f32[35,8,128]{2,1,0:T(8,128)S(1)}, u32[]{:S(2)}, u32[]{:S(2)}) collective-permute-start(f32[35,8,128]{2,1,0:T(8,128)S(1)} %get-tuple-element.64), channel_id=1, source_target_pairs={{0,128},{128,256},{256,384},{384,0},{1,129},{129,257},{257,385},{3... | collective-permute-start | bytes 430088 | tf_op jit(solution)/shard_map/ppermute | solution.py:645
  43.3 1.1 %collective-permute-done.7.got_ref = f32[35,8,128]{2,1,0:T(8,128)S(1)} collective-permute-done((f32[35,8,128]{2,1,0:T(8,128)S(1)}, f32[35,8,128]{2,1,0:T(8,128)S(1)}, u32[]{:S(2)}, u32[]{:S(2)}) %collective-permute-start.7) | collective-permute-done | bytes 143392 | tf_op jit(solution)/shard_map/ppermute | solution.py:645
  44.4 0.3 shard_map.67
  44.7 2.8 %collective-permute-done.6.got_ref = f32[35,8,128]{2,1,0:T(8,128)S(1)} collective-permute-done((f32[35,8,128]{2,1,0:T(8,128)S(1)}, f32[35,8,128]{2,1,0:T(8,128)S(1)}, u32[]{:S(2)}, u32[]{:S(2)}) %collective-permute-start.6) | collective-permute-done | bytes 143392 | tf_op jit(solution)/shard_map/ppermute | solution.py:645
  47.6 0.3 shard_map.66
  47.9 1.0 %shard_map.68 = (f32[2,16,128]{2,1,0:T(8,128)}, f32[19,2,16,128]{3,2,1,0:T(8,128)}) custom-call(f32[2,2,24,128]{3,2,1,0:T(8,128)S(1)} %get-tuple-element.47.b_ref, f32[16,128]{1,0:T(8,128)S(1)} %get-tuple-element.65.grad0_ref, f32[16,128]{1,0:T(8,128)S(1)} %get-tuple-element.69.grad1_ref, f32[19,2,24,128]{3,2,1,0:T(8,128)S(1)} %get-tuple-element.70.a_left_ref, ...), custom_call_target="tpu_custom_call" | custom-call | flops 2000000 | bytes 1000000 | tf_op jit(solution)/shard_map/pallas_call | solution.py:696
Async XLA Ops:
  1.8 9.9 %collective-permute-start = (f32[29,8,128]{2,1,0:T(8,128)S(1)}, f32[29,8,128]{2,1,0:T(8,128)S(1)}, u32[]{:S(2)}, u32[]{:S(2)}) collective-permute-start(f32[29,8,128]{2,1,0:T(8,128)S(1)} %get-tuple-element.42), channel_id=1, source_target_pairs={{0,32},{32,64},{64,96},{96,0},{1,33},{33,65},{65,97},{97,1},{2,34}... | collective-permute-start | bytes 356360 | tf_op jit(solution)/shard_map/ppermute | solution.py:645
  9.4 7.9 %collective-permute-start.1 = (f32[29,8,128]{2,1,0:T(8,128)S(1)}, f32[29,8,128]{2,1,0:T(8,128)S(1)}, u32[]{:S(2)}, u32[]{:S(2)}) collective-permute-start(f32[29,8,128]{2,1,0:T(8,128)S(1)} %get-tuple-element.43), channel_id=1, source_target_pairs={{32,0},{64,32},{96,64},{0,96},{33,1},{65,33},{97,65},{1,97},{34,2}... | collective-permute-start | bytes 356360 | tf_op jit(solution)/shard_map/ppermute | solution.py:645
  17.9 4.6 %collective-permute-start.2 = (f32[3,24,128]{2,1,0:T(8,128)S(1)}, f32[3,24,128]{2,1,0:T(8,128)S(1)}, u32[]{:S(2)}, u32[]{:S(2)}) collective-permute-start(f32[3,24,128]{2,1,0:T(8,128)S(1)} %get-tuple-element.45), channel_id=1, source_target_pairs={{0,1},{1,2},{2,3},{3,4},{4,5},{5,6},{6,7},{7,8},{8,9},{9,10},{10,1... | collective-permute-start | bytes 110600 | tf_op jit(solution)/shard_map/ppermute | solution.py:645
  17.9 4.6 %collective-permute-start.3 = (f32[3,24,128]{2,1,0:T(8,128)S(1)}, f32[3,24,128]{2,1,0:T(8,128)S(1)}, u32[]{:S(2)}, u32[]{:S(2)}) collective-permute-start(f32[3,24,128]{2,1,0:T(8,128)S(1)} %get-tuple-element.46), channel_id=1, source_target_pairs={{1,0},{2,1},{3,2},{4,3},{5,4},{6,5},{7,6},{8,7},{9,8},{10,9},{11,1... | collective-permute-start | bytes 110600 | tf_op jit(solution)/shard_map/ppermute | solution.py:645
  23.2 7.8 %collective-permute-start.5 = (f32[432,128]{1,0:T(8,128)S(1)}, f32[432,128]{1,0:T(8,128)S(1)}, u32[]{:S(2)}, u32[]{:S(2)}) collective-permute-start(f32[432,128]{1,0:T(8,128)S(1)} %get-tuple-element.49), channel_id=1, source_target_pairs={{128,0},{256,128},{384,256},{0,384},{129,1},{257,129},{385,257},{1... | collective-permute-start | bytes 663560 | tf_op jit(solution)/shard_map/ppermute | solution.py:645
  27.1 9.0 %collective-permute-start.4 = (f32[432,128]{1,0:T(8,128)S(1)}, f32[432,128]{1,0:T(8,128)S(1)}, u32[]{:S(2)}, u32[]{:S(2)}) collective-permute-start(f32[432,128]{1,0:T(8,128)S(1)} %get-tuple-element.48), channel_id=1, source_target_pairs={{0,128},{128,256},{256,384},{384,0},{1,129},{129,257},{257,385},{3... | collective-permute-start | bytes 663560 | tf_op jit(solution)/shard_map/ppermute | solution.py:645
  37.4 7.0 %collective-permute-start.7 = (f32[35,8,128]{2,1,0:T(8,128)S(1)}, f32[35,8,128]{2,1,0:T(8,128)S(1)}, u32[]{:S(2)}, u32[]{:S(2)}) collective-permute-start(f32[35,8,128]{2,1,0:T(8,128)S(1)} %get-tuple-element.68), channel_id=1, source_target_pairs={{128,0},{256,128},{384,256},{0,384},{129,1},{257,129},{385,257},{1... | collective-permute-start | bytes 430088 | tf_op jit(solution)/shard_map/ppermute | solution.py:645
  39.4 8.2 %collective-permute-start.6 = (f32[35,8,128]{2,1,0:T(8,128)S(1)}, f32[35,8,128]{2,1,0:T(8,128)S(1)}, u32[]{:S(2)}, u32[]{:S(2)}) collective-permute-start(f32[35,8,128]{2,1,0:T(8,128)S(1)} %get-tuple-element.64), channel_id=1, source_target_pairs={{0,128},{128,256},{256,384},{384,0},{1,129},{129,257},{257,385},{3... | collective-permute-start | bytes 430088 | tf_op jit(solution)/shard_map/ppermute | solution.py:645

commit v7 on v6

--- a/solution.py
+++ b/solution.py
@@ -353,9 +353,9 @@
             tile = main_ref[k, layer]
             n = 2 * k + layer
             slot = n % 32
-            piece_up, piece_down = turn(tile, 4 * slot + 4, 1), turn(tile, 4 * slot, 1)
-            high = piece_up if slot == 0 else jnp.where(at >= 4 * slot, piece_up, high)
-            low = piece_down if slot == 0 else jnp.where(at >= 4 * slot, piece_down, low)
+            piece = turn(tile, 4 * slot + 4, 1)
+            high = piece if slot == 0 else jnp.where(at >= 4 * slot, piece, high)
+            low = piece if slot == 0 else jnp.where((at >= 4 * slot + 4) if slot < 31 else (at < 4), piece, low)
             if slot == 31 or n == 2 * FIELDS - 1:
                 up_ref[n // 32] = high
                 down_ref[n // 32] = low
@@ -366,28 +366,33 @@
         body(8 * n)
 
 
-def rim_of(before_ref, beyond_ref, k, layer):
-    n = 2 * k + layer
-    slot, tile = n % 32, n // 32
-    before = turn(before_ref[tile], -(4 * slot + 4), 1)
-    beyond = turn(beyond_ref[tile], -4 * slot, 1)
-    return jnp.where(column((ROWS, LANES)) < RIM, beyond, before)
+def joined_columns(before_ref, beyond_ref, out_ref):
+    odd = (column((ROWS, LANES)) // 4) % 2
+    for tile in range(ZTILES):
+        for part in range(2):
+            out_ref[2 * tile + part] = jnp.where(odd == part, before_ref[tile], beyond_ref[tile])
+
+
+def rim_of(columns_ref, k, layer):
+    slot = (2 * k + layer) % 32
+    return turn(columns_ref[2 * ((2 * k + layer) // 32) + slot % 2], -(4 * slot + 4), 1)
 
 
 def first_kernel(
     main_ref, before_ref, beyond_ref,
     f1_ref, edge_ref, b_ref, up_ref, down_ref,
-    level_ref, rim_ref, seed_ref,
+    level_ref, rim_ref, seed_ref, columns_ref,
 ):
+    joined_columns(before_ref, beyond_ref, columns_ref)
     for i in range(Q):
         for layer in range(2):
-            rim_ref[i, layer] = rim_of(before_ref, beyond_ref, i, layer)
+            rim_ref[i, layer] = rim_of(columns_ref, i, layer)
     for layer, pops in ((1, XM), (0, XP)):
         for i in pops:
-            seed_ref[i, 0] = rim_of(before_ref, beyond_ref, Q + i, layer)
+            seed_ref[i, 0] = rim_of(columns_ref, Q + i, layer)
     for layer in range(2):
         b_ref[layer, 0] = main_ref[2 * Q, layer]
-        b_ref[layer, 1] = rim_of(before_ref, beyond_ref, 2 * Q, layer)
+        b_ref[layer, 1] = rim_of(columns_ref, 2 * Q, layer)
     for i in range(Q):
         for layer in range(2):
             to = layer + VEL[i][0]
@@ -423,11 +428,12 @@
     pack1(down_ref, tiles_of(XM, XP, 0))
 
 
-def seed_kernel(main_ref, before_ref, beyond_ref, b2_ref, rim_ref):
+def seed_kernel(main_ref, before_ref, beyond_ref, b2_ref, rim_ref, columns_ref):
+    joined_columns(before_ref, beyond_ref, columns_ref)
     for i in range(Q):
         for layer in range(2):
             if layer - VEL[i][0] in (0, 1):
-                rim_ref[i, layer] = rim_of(before_ref, beyond_ref, Q + i, layer)
+                rim_ref[i, layer] = rim_of(columns_ref, Q + i, layer)
     for i in range(Q):
         for layer in range(2):
             to = layer - VEL[i][0]
@@ -663,10 +669,10 @@
     f1, edge, b, up, down = call(
         first_kernel,
         [(Q,) + half, (Q, 2) + tile, half] + [(STRIPS1[-1] + ROWS, LANES)] * 2,
-        [(3,) + half, (Q, 2) + tile, (Q, 2) + tile],
+        [(3,) + half, (Q, 2) + tile, (Q, 2) + tile, (2 * ZTILES,) + tile],
     )(main, before, beyond)
     left1, right1 = both_ways(up, down, "gx")
-    (b2,) = call(seed_kernel, [(Q,) + half], [(Q, 2) + tile])(main, before, beyond)
+    (b2,) = call(seed_kernel, [(Q,) + half], [(Q, 2) + tile, (2 * ZTILES,) + tile])(main, before, beyond)
     sides = []
     for side, got in enumerate((left1, right1)):
         sides.append(

time: 49.2 us -> 48.8 us (level)
  no operation moved by 1% of the time
where the time goes in v7:
time: 48.8 us; the launch traced here: 48.4 us
  starting transfers between devices  24.1 us (49%)
  waiting for transfers between devices  18.2 us (37%)
  Pallas kernels  5.42 us (11%)
  between operations  0.74 us (2%)
    ppermute x4, starting transfers between devices, both_ways(): lax.ppermute(up, axis, ring)  13.4 us
    ppermute x4, starting transfers between devices, both_ways(): lax.ppermute(down, axis, [(j, i) for i, j in ring])  10.7 us
    ppermute x4, waiting for transfers between devices, both_ways(): lax.ppermute(up, axis, ring)  9.83 us
    ppermute x4, waiting for transfers between devices, both_ways(): lax.ppermute(down, axis, [(j, i) for i, j in ring])  8.38 us
    pallas_call x1, Pallas kernels, body(): call(rows_kernel, [(YTILES, 8, LANES)] * 2 + [block, block, block, (1,) +...  1.2 us
    pallas_call x1, Pallas kernels, body(): call(middle_kernel, [(2, OWN, LANES), (Q,) + half, (Q, 2) + tile, (4,) +...  1 us
    pallas_call x1, Pallas kernels, body(): call(last_kernel, [(2, OWN, LANES), (Q, 2, OWN, LANES)], [(Q, 2, OWN, LAN...  0.99 us
  transfers between devices with their start and end apart: 8, of which 7 were waited for; matrix products, arithmetic and copies ran while one was open for 0% of the time, Pallas kernels for 2%

profile of v7, /device:TPU:24, one launch (start us, length us, event | category | flops | bytes accessed | tf_op | source)
XLA Modules:
  0.0 48.4 jit_solution(4812689532725768552)
XLA Ops:
  0.6 1.2 %shard_map.59 = (f32[29,8,128]{2,1,0:T(8,128)S(1)}, f32[29,8,128]{2,1,0:T(8,128)S(1)}, f32[19,2,16,128]{3,2,1,0:T(8,128)S(1)}, f32[19,2,16,128]{3,2,1,0:T(8,128)...) custom-call(f32[19,2,16,128]{3,2,1,0:T(8,128)} %f_hbm.1, ...), custom_call_target="tpu_custom_call" | custom-call | flops 2000000 | bytes 1000000 | tf_op jit(solution)/shard_map/pallas_call | solution.py:659
  1.8 7.5 %collective-permute-start = (f32[29,8,128]{2,1,0:T(8,128)S(1)}, f32[29,8,128]{2,1,0:T(8,128)S(1)}, u32[]{:S(2)}, u32[]{:S(2)}) collective-permute-start(f32[29,8,128]{2,1,0:T(8,128)S(1)} %get-tuple-element.42), channel_id=1, source_target_pairs={{0,32},{32,64},{64,96},{96,0},{1,33},{33,65},{65,97},{97,1},{2,34}... | collective-permute-start | bytes 356360 | tf_op jit(solution)/shard_map/ppermute | solution.py:651
  9.4 1.9 %collective-permute-start.1 = (f32[29,8,128]{2,1,0:T(8,128)S(1)}, f32[29,8,128]{2,1,0:T(8,128)S(1)}, u32[]{:S(2)}, u32[]{:S(2)}) collective-permute-start(f32[29,8,128]{2,1,0:T(8,128)S(1)} %get-tuple-element.43), channel_id=1, source_target_pairs={{32,0},{64,32},{96,64},{0,96},{33,1},{65,33},{97,65},{1,97},{34,2}... | collective-permute-start | bytes 356360 | tf_op jit(solution)/shard_map/ppermute | solution.py:651
  11.3 0.5 collective-permute-done.below_ref
  11.7 5.6 %collective-permute-done.1.above_ref = f32[29,8,128]{2,1,0:T(8,128)S(1)} collective-permute-done((f32[29,8,128]{2,1,0:T(8,128)S(1)}, f32[29,8,128]{2,1,0:T(8,128)S(1)}, u32[]{:S(2)}, u32[]{:S(2)}) %collective-permute-start.1) | collective-permute-done | bytes 118816 | tf_op jit(solution)/shard_map/ppermute | solution.py:651
  17.3 0.3 shard_map.60
  17.6 0.0 collective-permute-start.2
  17.7 2.9 %collective-permute-start.3 = (f32[3,24,128]{2,1,0:T(8,128)S(1)}, f32[3,24,128]{2,1,0:T(8,128)S(1)}, u32[]{:S(2)}, u32[]{:S(2)}) collective-permute-start(f32[3,24,128]{2,1,0:T(8,128)S(1)} %get-tuple-element.46), channel_id=1, source_target_pairs={{1,0},{2,1},{3,2},{4,3},{5,4},{6,5},{7,6},{8,7},{9,8},{10,9},{11,1... | collective-permute-start | bytes 110600 | tf_op jit(solution)/shard_map/ppermute | solution.py:651
  20.6 1.6 %collective-permute-done.2.before_ref = f32[3,24,128]{2,1,0:T(8,128)S(1)} collective-permute-done((f32[3,24,128]{2,1,0:T(8,128)S(1)}, f32[3,24,128]{2,1,0:T(8,128)S(1)}, u32[]{:S(2)}, u32[]{:S(2)}) %collective-permute-start.2) | collective-permute-done | bytes 36896 | tf_op jit(solution)/shard_map/ppermute | solution.py:651
  22.2 0.0 collective-permute-done.3.beyond_ref
  22.2 0.6 %shard_map.61 = (f32[19,2,2,24,128]{4,3,2,1,0:T(8,128)S(1)}, f32[19,2,24,128]{3,2,1,0:T(8,128)S(1)}, f32[2,2,24,128]{3,2,1,0:T(8,128)S(1)}, f32[432,128]{1,0:T(8,128)S(1)}, f32[432,128]{1,0:T(8,128)S(1)}) custom-call(f32[39,2,24,128]{3,2,1,0:T(8,128)S(1)} %get-tuple-element.44.main_ref, f32[3,24,128]{2,1,0:T(8,128)S(1)} %collective-permute-done.2.before_ref, ...), custom_call_target="tpu_custom_call" | custom-call | flops 2000000 | bytes 1000000 | tf_op jit(solution)/shard_map/pallas_call | solution.py:669
  22.8 3.9 %collective-permute-start.5 = (f32[432,128]{1,0:T(8,128)S(1)}, f32[432,128]{1,0:T(8,128)S(1)}, u32[]{:S(2)}, u32[]{:S(2)}) collective-permute-start(f32[432,128]{1,0:T(8,128)S(1)} %get-tuple-element.49), channel_id=1, source_target_pairs={{128,0},{256,128},{384,256},{0,384},{129,1},{257,129},{385,257},{1... | collective-permute-start | bytes 663560 | tf_op jit(solution)/shard_map/ppermute | solution.py:651
  26.7 1.9 %collective-permute-start.4 = (f32[432,128]{1,0:T(8,128)S(1)}, f32[432,128]{1,0:T(8,128)S(1)}, u32[]{:S(2)}, u32[]{:S(2)}) collective-permute-start(f32[432,128]{1,0:T(8,128)S(1)} %get-tuple-element.48), channel_id=1, source_target_pairs={{0,128},{128,256},{256,384},{384,0},{1,129},{129,257},{257,385},{3... | collective-permute-start | bytes 663560 | tf_op jit(solution)/shard_map/ppermute | solution.py:651
  28.7 0.3 shard_map.62.b2_ref
  28.9 1.7 %collective-permute-done.5.got_ref.right_ref.got1_ref = f32[432,128]{1,0:T(8,128)S(1)} collective-permute-done((f32[432,128]{1,0:T(8,128)S(1)}, f32[432,128]{1,0:T(8,128)S(1)}, u32[]{:S(2)}, u32[]{:S(2)}) %collective-permute-start.5) | collective-permute-done | bytes 221216 | tf_op jit(solution)/shard_map/ppermute | solution.py:651
  30.6 0.3 shard_map.64
  30.9 4.9 %collective-permute-done.4.got_ref.left_ref.got1_ref = f32[432,128]{1,0:T(8,128)S(1)} collective-permute-done((f32[432,128]{1,0:T(8,128)S(1)}, f32[432,128]{1,0:T(8,128)S(1)}, u32[]{:S(2)}, u32[]{:S(2)}) %collective-permute-start.4) | collective-permute-done | bytes 221216 | tf_op jit(solution)/shard_map/ppermute | solution.py:651
  35.8 0.3 shard_map.63
  36.0 1.0 %shard_map.65 = (f32[2,16,128]{2,1,0:T(8,128)S(1)}, f32[19,2,2,24,128]{4,3,2,1,0:T(8,128)S(1)}, f32[19,2,24,128]{3,2,1,0:T(8,128)S(1)}, f32[4,2,2,24,128]{4,3,2,...) custom-call(f32[2,2,24,128]{3,2,1,0:T(8,128)S(1)} %get-tuple-element.47.b_ref, ...), custom_call_target="tpu_custom_call" | custom-call | flops 2000000 | bytes 1000000 | tf_op jit(solution)/shard_map/pallas_call | solution.py:686
  37.0 1.9 %collective-permute-start.7 = (f32[35,8,128]{2,1,0:T(8,128)S(1)}, f32[35,8,128]{2,1,0:T(8,128)S(1)}, u32[]{:S(2)}, u32[]{:S(2)}) collective-permute-start(f32[35,8,128]{2,1,0:T(8,128)S(1)} %get-tuple-element.68), channel_id=1, source_target_pairs={{128,0},{256,128},{384,256},{0,384},{129,1},{257,129},{385,257},{1... | collective-permute-start | bytes 430088 | tf_op jit(solution)/shard_map/ppermute | solution.py:651
  39.0 3.9 %collective-permute-start.6 = (f32[35,8,128]{2,1,0:T(8,128)S(1)}, f32[35,8,128]{2,1,0:T(8,128)S(1)}, u32[]{:S(2)}, u32[]{:S(2)}) collective-permute-start(f32[35,8,128]{2,1,0:T(8,128)S(1)} %get-tuple-element.64), channel_id=1, source_target_pairs={{0,128},{128,256},{256,384},{384,0},{1,129},{129,257},{257,385},{3... | collective-permute-start | bytes 430088 | tf_op jit(solution)/shard_map/ppermute | solution.py:651
  42.9 1.1 %collective-permute-done.7.got_ref = f32[35,8,128]{2,1,0:T(8,128)S(1)} collective-permute-done((f32[35,8,128]{2,1,0:T(8,128)S(1)}, f32[35,8,128]{2,1,0:T(8,128)S(1)}, u32[]{:S(2)}, u32[]{:S(2)}) %collective-permute-start.7) | collective-permute-done | bytes 143392 | tf_op jit(solution)/shard_map/ppermute | solution.py:651
  44.0 0.3 shard_map.67
  44.3 2.8 %collective-permute-done.6.got_ref = f32[35,8,128]{2,1,0:T(8,128)S(1)} collective-permute-done((f32[35,8,128]{2,1,0:T(8,128)S(1)}, f32[35,8,128]{2,1,0:T(8,128)S(1)}, u32[]{:S(2)}, u32[]{:S(2)}) %collective-permute-start.6) | collective-permute-done | bytes 143392 | tf_op jit(solution)/shard_map/ppermute | solution.py:651
  47.2 0.3 shard_map.66
  47.5 1.0 %shard_map.68 = (f32[2,16,128]{2,1,0:T(8,128)}, f32[19,2,16,128]{3,2,1,0:T(8,128)}) custom-call(f32[2,2,24,128]{3,2,1,0:T(8,128)S(1)} %get-tuple-element.47.b_ref, f32[16,128]{1,0:T(8,128)S(1)} %get-tuple-element.65.grad0_ref, f32[16,128]{1,0:T(8,128)S(1)} %get-tuple-element.69.grad1_ref, f32[19,2,24,128]{3,2,1,0:T(8,128)S(1)} %get-tuple-element.70.a_left_ref, ...), custom_call_target="tpu_custom_call" | custom-call | flops 2000000 | bytes 1000000 | tf_op jit(solution)/shard_map/pallas_call | solution.py:702
Async XLA Ops:
  1.8 9.9 %collective-permute-start = (f32[29,8,128]{2,1,0:T(8,128)S(1)}, f32[29,8,128]{2,1,0:T(8,128)S(1)}, u32[]{:S(2)}, u32[]{:S(2)}) collective-permute-start(f32[29,8,128]{2,1,0:T(8,128)S(1)} %get-tuple-element.42), channel_id=1, source_target_pairs={{0,32},{32,64},{64,96},{96,0},{1,33},{33,65},{65,97},{97,1},{2,34}... | collective-permute-start | bytes 356360 | tf_op jit(solution)/shard_map/ppermute | solution.py:651
  9.4 7.9 %collective-permute-start.1 = (f32[29,8,128]{2,1,0:T(8,128)S(1)}, f32[29,8,128]{2,1,0:T(8,128)S(1)}, u32[]{:S(2)}, u32[]{:S(2)}) collective-permute-start(f32[29,8,128]{2,1,0:T(8,128)S(1)} %get-tuple-element.43), channel_id=1, source_target_pairs={{32,0},{64,32},{96,64},{0,96},{33,1},{65,33},{97,65},{1,97},{34,2}... | collective-permute-start | bytes 356360 | tf_op jit(solution)/shard_map/ppermute | solution.py:651
  17.6 4.6 %collective-permute-start.2 = (f32[3,24,128]{2,1,0:T(8,128)S(1)}, f32[3,24,128]{2,1,0:T(8,128)S(1)}, u32[]{:S(2)}, u32[]{:S(2)}) collective-permute-start(f32[3,24,128]{2,1,0:T(8,128)S(1)} %get-tuple-element.45), channel_id=1, source_target_pairs={{0,1},{1,2},{2,3},{3,4},{4,5},{5,6},{6,7},{7,8},{8,9},{9,10},{10,1... | collective-permute-start | bytes 110600 | tf_op jit(solution)/shard_map/ppermute | solution.py:651
  17.7 4.6 %collective-permute-start.3 = (f32[3,24,128]{2,1,0:T(8,128)S(1)}, f32[3,24,128]{2,1,0:T(8,128)S(1)}, u32[]{:S(2)}, u32[]{:S(2)}) collective-permute-start(f32[3,24,128]{2,1,0:T(8,128)S(1)} %get-tuple-element.46), channel_id=1, source_target_pairs={{1,0},{2,1},{3,2},{4,3},{5,4},{6,5},{7,6},{8,7},{9,8},{10,9},{11,1... | collective-permute-start | bytes 110600 | tf_op jit(solution)/shard_map/ppermute | solution.py:651
  22.8 7.8 %collective-permute-start.5 = (f32[432,128]{1,0:T(8,128)S(1)}, f32[432,128]{1,0:T(8,128)S(1)}, u32[]{:S(2)}, u32[]{:S(2)}) collective-permute-start(f32[432,128]{1,0:T(8,128)S(1)} %get-tuple-element.49), channel_id=1, source_target_pairs={{128,0},{256,128},{384,256},{0,384},{129,1},{257,129},{385,257},{1... | collective-permute-start | bytes 663560 | tf_op jit(solution)/shard_map/ppermute | solution.py:651
  26.7 9.0 %collective-permute-start.4 = (f32[432,128]{1,0:T(8,128)S(1)}, f32[432,128]{1,0:T(8,128)S(1)}, u32[]{:S(2)}, u32[]{:S(2)}) collective-permute-start(f32[432,128]{1,0:T(8,128)S(1)} %get-tuple-element.48), channel_id=1, source_target_pairs={{0,128},{128,256},{256,384},{384,0},{1,129},{129,257},{257,385},{3... | collective-permute-start | bytes 663560 | tf_op jit(solution)/shard_map/ppermute | solution.py:651
  37.0 7.0 %collective-permute-start.7 = (f32[35,8,128]{2,1,0:T(8,128)S(1)}, f32[35,8,128]{2,1,0:T(8,128)S(1)}, u32[]{:S(2)}, u32[]{:S(2)}) collective-permute-start(f32[35,8,128]{2,1,0:T(8,128)S(1)} %get-tuple-element.68), channel_id=1, source_target_pairs={{128,0},{256,128},{384,256},{0,384},{129,1},{257,129},{385,257},{1... | collective-permute-start | bytes 430088 | tf_op jit(solution)/shard_map/ppermute | solution.py:651
  39.0 8.2 %collective-permute-start.6 = (f32[35,8,128]{2,1,0:T(8,128)S(1)}, f32[35,8,128]{2,1,0:T(8,128)S(1)}, u32[]{:S(2)}, u32[]{:S(2)}) collective-permute-start(f32[35,8,128]{2,1,0:T(8,128)S(1)} %get-tuple-element.64), channel_id=1, source_target_pairs={{0,128},{128,256},{256,384},{384,0},{1,129},{129,257},{257,385},{3... | collective-permute-start | bytes 430088 | tf_op jit(solution)/shard_map/ppermute | solution.py:651

commit v8 on v7

--- a/solution.py
+++ b/solution.py
@@ -276,8 +276,8 @@
     )
 
 
-LEVEL_Y = [i for i in range(Q) if VEL[i][1] == 0][:3]
-YTILES = Q + (Q + 1) // 2
+LEVEL_Y = [i for i in range(Q) if VEL[i][1] == 0]
+YTILES = Q + 8
 
 
 def rows_moves(up):
@@ -288,12 +288,15 @@
     for i in range(Q):
         for layer in range(2):
             out.append((0, i, layer, first(3), 3, i, 3 * layer))
-            out.append((1, i, layer, first(2), 2, Q + i // 2, 4 * (i % 2) + 2 * layer))
+            if i < 16:
+                out.append((1, i, layer, first(2), 2, Q + i // 2, 4 * (i % 2) + 2 * layer))
+            else:
+                out.append((1, i, layer, first(2), 2, LEVEL_Y[3 + 2 * (i - 16) + layer], 6))
             if VEL[i][1] == inwards:
                 out.append((0, i, layer, fourth, 1, i, 6 + layer))
             elif VEL[i][1] == -inwards:
                 out.append((1, i, layer, third, 1, i, 6 + layer))
-            elif i in LEVEL_Y:
+            elif i in LEVEL_Y[:3]:
                 out.append((2, 0, layer, first(3) + LEVEL_Y.index(i), 1, i, 6 + layer))
     return out
 
@@ -378,8 +381,29 @@
     return turn(columns_ref[2 * ((2 * k + layer) // 32) + slot % 2], -(4 * slot + 4), 1)
 
 
+def turned(tile, i, sign):
+    return turn(turn(tile, sign * VEL[i][1], 0), sign * VEL[i][2], 1)
+
+
+def edged(main, rim, i, sign):
+    z = sign * VEL[i][2]
+    if z == 0:
+        return main, rim
+    edge = column(main.shape) == (0 if z == 1 else LANES - 1)
+    return jnp.where(edge, rim, main), jnp.where(edge, main, rim)
+
+
+def turn_kernel(main_ref, g_ref, seed_ref):
+    for i in range(Q):
+        for layer in range(2):
+            g_ref[i, layer] = turned(main_ref[i, layer], i, 1)
+    for layer, pops in ((1, XM), (0, XP)):
+        for i in pops:
+            seed_ref[i] = turned(main_ref[Q + i, layer], i, -1)
+
+
 def first_kernel(
-    main_ref, before_ref, beyond_ref,
+    main_ref, g_ref, turned_seed_ref, before_ref, beyond_ref,
     f1_ref, edge_ref, b_ref, up_ref, down_ref,
     level_ref, rim_ref, seed_ref, columns_ref,
 ):
@@ -396,7 +420,7 @@
     for i in range(Q):
         for layer in range(2):
             to = layer + VEL[i][0]
-            tiles = moved(main_ref[i, layer], rim_ref[i, layer], i, 1)
+            tiles = edged(g_ref[i, layer], turned(rim_ref[i, layer], i, 1), i, 1)
             for lane in range(2):
                 if to in (0, 1):
                     f1_ref[i, to, lane] = tiles[lane]
@@ -420,7 +444,7 @@
         out.append(pick(b_ref, layer))
         out += [pick(edge_ref, i) for i in forward]
         for i in backward:
-            seed_ref[i, 0], seed_ref[i, 1] = moved(main_ref[Q + i, layer], seed_ref[i, 0], i, -1)
+            seed_ref[i, 0], seed_ref[i, 1] = edged(turned_seed_ref[i], turned(seed_ref[i, 0], i, -1), i, -1)
             out.append(pick(seed_ref, i))
         return out
 
@@ -666,11 +690,12 @@
     below, above = both_ways(up, down, "gy")
     main, up, down = call(columns_kernel, [(FIELDS, 2) + tile] + [(ZTILES,) + tile] * 2)(g, seed, own_b, below, above)
     before, beyond = both_ways(up, down, "gz")
+    g_turned, seed_turned = call(turn_kernel, [(Q, 2) + tile, (Q,) + tile])(main)
     f1, edge, b, up, down = call(
         first_kernel,
         [(Q,) + half, (Q, 2) + tile, half] + [(STRIPS1[-1] + ROWS, LANES)] * 2,
         [(3,) + half, (Q, 2) + tile, (Q, 2) + tile, (2 * ZTILES,) + tile],
-    )(main, before, beyond)
+    )(main, g_turned, seed_turned, before, beyond)
     left1, right1 = both_ways(up, down, "gx")
     (b2,) = call(seed_kernel, [(Q,) + half], [(Q, 2) + tile, (2 * ZTILES,) + tile])(main, before, beyond)
     sides = []

time: 48.8 us -> 48.6 us (level)
  no operation moved by 1% of the time
where the time goes in v8:
time: 48.6 us; the launch traced here: 48.3 us
  starting transfers between devices  24.1 us (50%)
  waiting for transfers between devices  18 us (37%)
  Pallas kernels  5.48 us (11%)
  between operations  0.74 us (2%)
    ppermute x4, starting transfers between devices, both_ways(): lax.ppermute(up, axis, ring)  13.4 us
    ppermute x4, starting transfers between devices, both_ways(): lax.ppermute(down, axis, [(j, i) for i, j in ring])  10.7 us
    ppermute x4, waiting for transfers between devices, both_ways(): lax.ppermute(up, axis, ring)  9.62 us
    ppermute x4, waiting for transfers between devices, both_ways(): lax.ppermute(down, axis, [(j, i) for i, j in ring])  8.37 us
    pallas_call x1, Pallas kernels, body(): call(rows_kernel, [(YTILES, 8, LANES)] * 2 + [block, block, block, (1,) +...  1.2 us
    pallas_call x1, Pallas kernels, body(): call(middle_kernel, [(2, OWN, LANES), (Q,) + half, (Q, 2) + tile, (4,) +...  1 us
    pallas_call x1, Pallas kernels, body(): call(last_kernel, [(2, OWN, LANES), (Q, 2, OWN, LANES)], [(Q, 2, OWN, LAN...  0.98 us
  transfers between devices with their start and end apart: 8, of which 7 were waited for; matrix products, arithmetic and copies ran while one was open for 0% of the time, Pallas kernels for 2%

profile of v8, /device:TPU:24, one launch (start us, length us, event | category | flops | bytes accessed | tf_op | source)
XLA Modules:
  0.0 48.3 jit_solution(2564264218599932730)
XLA Ops:
  0.6 1.2 %shard_map.59 = (f32[27,8,128]{2,1,0:T(8,128)S(1)}, f32[27,8,128]{2,1,0:T(8,128)S(1)}, f32[19,2,16,128]{3,2,1,0:T(8,128)S(1)}, f32[19,2,16,128]{3,2,1,0:T(8,128)...) custom-call(f32[19,2,16,128]{3,2,1,0:T(8,128)} %f_hbm.1, ...), custom_call_target="tpu_custom_call" | custom-call | flops 2000000 | bytes 1000000 | tf_op jit(solution)/shard_map/pallas_call | solution.py:683
  1.8 7.5 %collective-permute-start = (f32[27,8,128]{2,1,0:T(8,128)S(1)}, f32[27,8,128]{2,1,0:T(8,128)S(1)}, u32[]{:S(2)}, u32[]{:S(2)}) collective-permute-start(f32[27,8,128]{2,1,0:T(8,128)S(1)} %get-tuple-element.44), channel_id=1, source_target_pairs={{0,32},{32,64},{64,96},{96,0},{1,33},{33,65},{65,97},{97,1},{2,34}... | collective-permute-start | bytes 331784 | tf_op jit(solution)/shard_map/ppermute | solution.py:675
  9.4 1.9 %collective-permute-start.1 = (f32[27,8,128]{2,1,0:T(8,128)S(1)}, f32[27,8,128]{2,1,0:T(8,128)S(1)}, u32[]{:S(2)}, u32[]{:S(2)}) collective-permute-start(f32[27,8,128]{2,1,0:T(8,128)S(1)} %get-tuple-element.45), channel_id=1, source_target_pairs={{32,0},{64,32},{96,64},{0,96},{33,1},{65,33},{97,65},{1,97},{34,2}... | collective-permute-start | bytes 331784 | tf_op jit(solution)/shard_map/ppermute | solution.py:675
  11.3 0.4 collective-permute-done.below_ref
  11.7 5.5 %collective-permute-done.1.above_ref = f32[27,8,128]{2,1,0:T(8,128)S(1)} collective-permute-done((f32[27,8,128]{2,1,0:T(8,128)S(1)}, f32[27,8,128]{2,1,0:T(8,128)S(1)}, u32[]{:S(2)}, u32[]{:S(2)}) %collective-permute-start.1) | collective-permute-done | bytes 110624 | tf_op jit(solution)/shard_map/ppermute | solution.py:675
  17.2 0.3 shard_map.60
  17.5 0.0 collective-permute-start.2
  17.6 2.9 %collective-permute-start.3 = (f32[3,24,128]{2,1,0:T(8,128)S(1)}, f32[3,24,128]{2,1,0:T(8,128)S(1)}, u32[]{:S(2)}, u32[]{:S(2)}) collective-permute-start(f32[3,24,128]{2,1,0:T(8,128)S(1)} %get-tuple-element.50), channel_id=1, source_target_pairs={{1,0},{2,1},{3,2},{4,3},{5,4},{6,5},{7,6},{8,7},{9,8},{10,9},{11,1... | collective-permute-start | bytes 110600 | tf_op jit(solution)/shard_map/ppermute | solution.py:675
  20.5 0.1 shard_map.61
  20.6 1.5 %collective-permute-done.2.before_ref = f32[3,24,128]{2,1,0:T(8,128)S(1)} collective-permute-done((f32[3,24,128]{2,1,0:T(8,128)S(1)}, f32[3,24,128]{2,1,0:T(8,128)S(1)}, u32[]{:S(2)}, u32[]{:S(2)}) %collective-permute-start.2) | collective-permute-done | bytes 36896 | tf_op jit(solution)/shard_map/ppermute | solution.py:675
  22.2 0.0 collective-permute-done.3.beyond_ref
  22.2 0.5 %shard_map.62 = (f32[19,2,2,24,128]{4,3,2,1,0:T(8,128)S(1)}, f32[19,2,24,128]{3,2,1,0:T(8,128)S(1)}, f32[2,2,24,128]{3,2,1,0:T(8,128)S(1)}, f32[432,128]{1,0:T(8,128)S(1)}, f32[432,128]{1,0:T(8,128)S(1)}) custom-call(f32[39,2,24,128]{3,2,1,0:T(8,128)S(1)} %get-tuple-element.46.main_ref, f32[19,2,24,128]{3,2,1,0:T(8,128)S(1)} %get-tuple-element.47.g_ref, ...), custom_call_target="tpu_custom_call" | custom-call | flops 2000000 | bytes 1000000 | tf_op jit(solution)/shard_map/pallas_call | solution.py:694
  22.6 3.9 %collective-permute-start.5 = (f32[432,128]{1,0:T(8,128)S(1)}, f32[432,128]{1,0:T(8,128)S(1)}, u32[]{:S(2)}, u32[]{:S(2)}) collective-permute-start(f32[432,128]{1,0:T(8,128)S(1)} %get-tuple-element.53), channel_id=1, source_target_pairs={{128,0},{256,128},{384,256},{0,384},{129,1},{257,129},{385,257},{1... | collective-permute-start | bytes 663560 | tf_op jit(solution)/shard_map/ppermute | solution.py:675
  26.6 1.9 %collective-permute-start.4 = (f32[432,128]{1,0:T(8,128)S(1)}, f32[432,128]{1,0:T(8,128)S(1)}, u32[]{:S(2)}, u32[]{:S(2)}) collective-permute-start(f32[432,128]{1,0:T(8,128)S(1)} %get-tuple-element.52), channel_id=1, source_target_pairs={{0,128},{128,256},{256,384},{384,0},{1,129},{129,257},{257,385},{3... | collective-permute-start | bytes 663560 | tf_op jit(solution)/shard_map/ppermute | solution.py:675
  28.5 0.3 shard_map.63.b2_ref
  28.8 1.7 %collective-permute-done.5.got_ref.right_ref.got1_ref = f32[432,128]{1,0:T(8,128)S(1)} collective-permute-done((f32[432,128]{1,0:T(8,128)S(1)}, f32[432,128]{1,0:T(8,128)S(1)}, u32[]{:S(2)}, u32[]{:S(2)}) %collective-permute-start.5) | collective-permute-done | bytes 221216 | tf_op jit(solution)/shard_map/ppermute | solution.py:675
  30.5 0.3 shard_map.65
  30.7 4.9 %collective-permute-done.4.got_ref.left_ref.got1_ref = f32[432,128]{1,0:T(8,128)S(1)} collective-permute-done((f32[432,128]{1,0:T(8,128)S(1)}, f32[432,128]{1,0:T(8,128)S(1)}, u32[]{:S(2)}, u32[]{:S(2)}) %collective-permute-start.4) | collective-permute-done | bytes 221216 | tf_op jit(solution)/shard_map/ppermute | solution.py:675
  35.6 0.2 shard_map.64
  35.9 1.0 %shard_map.66 = (f32[2,16,128]{2,1,0:T(8,128)S(1)}, f32[19,2,2,24,128]{4,3,2,1,0:T(8,128)S(1)}, f32[19,2,24,128]{3,2,1,0:T(8,128)S(1)}, f32[4,2,2,24,128]{4,3,2,...) custom-call(f32[2,2,24,128]{3,2,1,0:T(8,128)S(1)} %get-tuple-element.51.b_ref, ...), custom_call_target="tpu_custom_call" | custom-call | flops 2000000 | bytes 1000000 | tf_op jit(solution)/shard_map/pallas_call | solution.py:711
  36.9 1.9 %collective-permute-start.7 = (f32[35,8,128]{2,1,0:T(8,128)S(1)}, f32[35,8,128]{2,1,0:T(8,128)S(1)}, u32[]{:S(2)}, u32[]{:S(2)}) collective-permute-start(f32[35,8,128]{2,1,0:T(8,128)S(1)} %get-tuple-element.72), channel_id=1, source_target_pairs={{128,0},{256,128},{384,256},{0,384},{129,1},{257,129},{385,257},{1... | collective-permute-start | bytes 430088 | tf_op jit(solution)/shard_map/ppermute | solution.py:675
  38.8 3.9 %collective-permute-start.6 = (f32[35,8,128]{2,1,0:T(8,128)S(1)}, f32[35,8,128]{2,1,0:T(8,128)S(1)}, u32[]{:S(2)}, u32[]{:S(2)}) collective-permute-start(f32[35,8,128]{2,1,0:T(8,128)S(1)} %get-tuple-element.68), channel_id=1, source_target_pairs={{0,128},{128,256},{256,384},{384,0},{1,129},{129,257},{257,385},{3... | collective-permute-start | bytes 430088 | tf_op jit(solution)/shard_map/ppermute | solution.py:675
  42.7 1.1 %collective-permute-done.7.got_ref = f32[35,8,128]{2,1,0:T(8,128)S(1)} collective-permute-done((f32[35,8,128]{2,1,0:T(8,128)S(1)}, f32[35,8,128]{2,1,0:T(8,128)S(1)}, u32[]{:S(2)}, u32[]{:S(2)}) %collective-permute-start.7) | collective-permute-done | bytes 143392 | tf_op jit(solution)/shard_map/ppermute | solution.py:675
  43.9 0.3 shard_map.68
  44.2 2.8 %collective-permute-done.6.got_ref = f32[35,8,128]{2,1,0:T(8,128)S(1)} collective-permute-done((f32[35,8,128]{2,1,0:T(8,128)S(1)}, f32[35,8,128]{2,1,0:T(8,128)S(1)}, u32[]{:S(2)}, u32[]{:S(2)}) %collective-permute-start.6) | collective-permute-done | bytes 143392 | tf_op jit(solution)/shard_map/ppermute | solution.py:675
  47.0 0.3 shard_map.67
  47.3 1.0 %shard_map.69 = (f32[2,16,128]{2,1,0:T(8,128)}, f32[19,2,16,128]{3,2,1,0:T(8,128)}) custom-call(f32[2,2,24,128]{3,2,1,0:T(8,128)S(1)} %get-tuple-element.51.b_ref, f32[16,128]{1,0:T(8,128)S(1)} %get-tuple-element.69.grad0_ref, f32[16,128]{1,0:T(8,128)S(1)} %get-tuple-element.73.grad1_ref, f32[19,2,24,128]{3,2,1,0:T(8,128)S(1)} %get-tuple-element.74.a_left_ref, ...), custom_call_target="tpu_custom_call" | custom-call | flops 2000000 | bytes 1000000 | tf_op jit(solution)/shard_map/pallas_call | solution.py:727
Async XLA Ops:
  1.8 9.8 %collective-permute-start = (f32[27,8,128]{2,1,0:T(8,128)S(1)}, f32[27,8,128]{2,1,0:T(8,128)S(1)}, u32[]{:S(2)}, u32[]{:S(2)}) collective-permute-start(f32[27,8,128]{2,1,0:T(8,128)S(1)} %get-tuple-element.44), channel_id=1, source_target_pairs={{0,32},{32,64},{64,96},{96,0},{1,33},{33,65},{65,97},{97,1},{2,34}... | collective-permute-start | bytes 331784 | tf_op jit(solution)/shard_map/ppermute | solution.py:675
  9.4 7.9 %collective-permute-start.1 = (f32[27,8,128]{2,1,0:T(8,128)S(1)}, f32[27,8,128]{2,1,0:T(8,128)S(1)}, u32[]{:S(2)}, u32[]{:S(2)}) collective-permute-start(f32[27,8,128]{2,1,0:T(8,128)S(1)} %get-tuple-element.45), channel_id=1, source_target_pairs={{32,0},{64,32},{96,64},{0,96},{33,1},{65,33},{97,65},{1,97},{34,2}... | collective-permute-start | bytes 331784 | tf_op jit(solution)/shard_map/ppermute | solution.py:675
  17.5 4.6 %collective-permute-start.2 = (f32[3,24,128]{2,1,0:T(8,128)S(1)}, f32[3,24,128]{2,1,0:T(8,128)S(1)}, u32[]{:S(2)}, u32[]{:S(2)}) collective-permute-start(f32[3,24,128]{2,1,0:T(8,128)S(1)} %get-tuple-element.49), channel_id=1, source_target_pairs={{0,1},{1,2},{2,3},{3,4},{4,5},{5,6},{6,7},{7,8},{8,9},{9,10},{10,1... | collective-permute-start | bytes 110600 | tf_op jit(solution)/shard_map/ppermute | solution.py:675
  17.6 4.6 %collective-permute-start.3 = (f32[3,24,128]{2,1,0:T(8,128)S(1)}, f32[3,24,128]{2,1,0:T(8,128)S(1)}, u32[]{:S(2)}, u32[]{:S(2)}) collective-permute-start(f32[3,24,128]{2,1,0:T(8,128)S(1)} %get-tuple-element.50), channel_id=1, source_target_pairs={{1,0},{2,1},{3,2},{4,3},{5,4},{6,5},{7,6},{8,7},{9,8},{10,9},{11,1... | collective-permute-start | bytes 110600 | tf_op jit(solution)/shard_map/ppermute | solution.py:675
  22.6 7.8 %collective-permute-start.5 = (f32[432,128]{1,0:T(8,128)S(1)}, f32[432,128]{1,0:T(8,128)S(1)}, u32[]{:S(2)}, u32[]{:S(2)}) collective-permute-start(f32[432,128]{1,0:T(8,128)S(1)} %get-tuple-element.53), channel_id=1, source_target_pairs={{128,0},{256,128},{384,256},{0,384},{129,1},{257,129},{385,257},{1... | collective-permute-start | bytes 663560 | tf_op jit(solution)/shard_map/ppermute | solution.py:675
  26.6 9.0 %collective-permute-start.4 = (f32[432,128]{1,0:T(8,128)S(1)}, f32[432,128]{1,0:T(8,128)S(1)}, u32[]{:S(2)}, u32[]{:S(2)}) collective-permute-start(f32[432,128]{1,0:T(8,128)S(1)} %get-tuple-element.52), channel_id=1, source_target_pairs={{0,128},{128,256},{256,384},{384,0},{1,129},{129,257},{257,385},{3... | collective-permute-start | bytes 663560 | tf_op jit(solution)/shard_map/ppermute | solution.py:675
  36.9 7.0 %collective-permute-start.7 = (f32[35,8,128]{2,1,0:T(8,128)S(1)}, f32[35,8,128]{2,1,0:T(8,128)S(1)}, u32[]{:S(2)}, u32[]{:S(2)}) collective-permute-start(f32[35,8,128]{2,1,0:T(8,128)S(1)} %get-tuple-element.72), channel_id=1, source_target_pairs={{128,0},{256,128},{384,256},{0,384},{129,1},{257,129},{385,257},{1... | collective-permute-start | bytes 430088 | tf_op jit(solution)/shard_map/ppermute | solution.py:675
  38.8 8.2 %collective-permute-start.6 = (f32[35,8,128]{2,1,0:T(8,128)S(1)}, f32[35,8,128]{2,1,0:T(8,128)S(1)}, u32[]{:S(2)}, u32[]{:S(2)}) collective-permute-start(f32[35,8,128]{2,1,0:T(8,128)S(1)} %get-tuple-element.68), channel_id=1, source_target_pairs={{0,128},{128,256},{256,384},{384,0},{1,129},{129,257},{257,385},{3... | collective-permute-start | bytes 430088 | tf_op jit(solution)/shard_map/ppermute | solution.py:675

commit v9 on v8

--- a/solution.py
+++ b/solution.py
@@ -665,6 +665,32 @@
         tiles_loop(2, body)
 
 
+def left_middle_kernel(
+    f1_ref, edge_ref, b_ref, b2_ref, left_ref, right_ref, mom1_ref, g1_ref, g_right_ref,
+    mom0_ref, far0_ref, bh0_ref, grad_ref, b1_ref, edge1_ref, sums_ref, up_ref, down_ref,
+    g0_ref, g_left_ref, l_beyond, l_scr, r_beyond, r_scr, f_scr, a_scr, rim_scr,
+):
+    side_kernel(0, f1_ref, edge_ref, b_ref, left_ref, mom0_ref, far0_ref, bh0_ref, g0_ref, g_left_ref, l_beyond, l_scr)
+    middle_kernel(
+        b_ref, b2_ref, left_ref, right_ref, mom0_ref, mom1_ref, g0_ref, g1_ref, g_left_ref, g_right_ref,
+        grad_ref, b1_ref, edge1_ref, sums_ref, up_ref, down_ref,
+        l_beyond, l_scr, r_beyond, r_scr, f_scr, a_scr, rim_scr,
+    )
+
+
+def left_last_kernel(
+    b1_ref, edge1_ref, sums_ref, mom_ref, far_ref, b_ref, bh_ref, f1_ref, got1_ref, grad_ref, got_ref,
+    grad1_ref, a1_ref, a_right_ref, f_ref, fluid_ref,
+    out_grad_ref, out_ref,
+    grad0_ref, a0_ref, a_left_ref, got, b_scr,
+):
+    side_back_kernel(
+        0, b1_ref, edge1_ref, sums_ref, mom_ref, far_ref, b_ref, bh_ref, f1_ref, got1_ref, grad_ref, got_ref,
+        grad0_ref, a0_ref, a_left_ref, got,
+    )
+    last_kernel(b_ref, grad0_ref, grad1_ref, a_left_ref, a0_ref, a1_ref, a_right_ref, f_ref, fluid_ref, out_grad_ref, out_ref, b_scr)
+
+
 def placed(x):
     return x if INTERPRET else pltpu.with_memory_space_constraint(x, pltpu.HBM)
 
@@ -698,35 +724,25 @@
     )(main, g_turned, seed_turned, before, beyond)
     left1, right1 = both_ways(up, down, "gx")
     (b2,) = call(seed_kernel, [(Q,) + half], [(Q, 2) + tile, (2 * ZTILES,) + tile])(main, before, beyond)
-    sides = []
-    for side, got in enumerate((left1, right1)):
-        sides.append(
-            call(
-                functools.partial(side_kernel, side),
-                [(4, 2) + tile, (3, 2) + tile, (2,) + tile, (Q, 2) + tile, (Q, 2) + tile],
-                [(SEND1, 8, LANES), (SEND1,) + tile],
-            )(f1, edge, b, got)
-        )
-    (mom0, far0, bh0, g0, g_left), (mom1, far1, bh1, g1, g_right) = sides
-    grad, b1, edge1, sums, up, down = call(
-        middle_kernel,
-        [(2, OWN, LANES), (Q,) + half, (Q, 2) + tile, (4,) + half] + [(ROWTILES2 + 3, 8, LANES)] * 2,
-        [(SEND1, 8, LANES), (SEND1,) + tile] * 2 + [(Q,) + half, (Q,) + half, (1,) + tile],
-    )(b, b2, left1, right1, mom0, mom1, g0, g1, g_left, g_right)
+    field = (Q, 2) + tile
+    moments_out = [(4, 2) + tile, (3, 2) + tile, (2,) + tile]
+    mom1, far1, bh1, g1, g_right = call(
+        functools.partial(side_kernel, 1), moments_out + [field, field], [(SEND1, 8, LANES), (SEND1,) + tile]
+    )(f1, edge, b, right1)
+    mom0, far0, bh0, grad, b1, edge1, sums, up, down = call(
+        left_middle_kernel,
+        moments_out + [(2, OWN, LANES), (Q,) + half, field, (4,) + half] + [(ROWTILES2 + 3, 8, LANES)] * 2,
+        [field, field] + [(SEND1, 8, LANES), (SEND1,) + tile] * 2 + [(Q,) + half, (Q,) + half, (1,) + tile],
+    )(f1, edge, b, b2, left1, right1, mom1, g1, g_right)
     left, right = both_ways(up, down, "gx")
-    sides = []
-    for side, (mom, far, bh, got1, got) in enumerate(((mom0, far0, bh0, left1, left), (mom1, far1, bh1, right1, right))):
-        sides.append(
-            call(
-                functools.partial(side_back_kernel, side),
-                [(OWN, LANES), (Q, 2) + tile, (Q, 2) + tile],
-                [(SEND2, 2) + tile],
-            )(b1, edge1, sums, mom, far, b, bh, f1, got1, grad, got)
-        )
-    (grad0, a0, a_left), (grad1, a1, a_right) = sides
-    gradient, adjoint_out = call(last_kernel, [(2, OWN, LANES), (Q, 2, OWN, LANES)], [(Q, 2, OWN, LANES)])(
-        b, grad0, grad1, a_left, a0, a1, a_right, f, fluid
-    )
+    grad1, a1, a_right = call(
+        functools.partial(side_back_kernel, 1), [(OWN, LANES), field, field], [(SEND2, 2) + tile]
+    )(b1, edge1, sums, mom1, far1, b, bh1, f1, right1, grad, right)
+    gradient, adjoint_out = call(
+        left_last_kernel,
+        [cells, block],
+        [(OWN, LANES), field, field, (SEND2, 2) + tile, block],
+    )(b1, edge1, sums, mom0, far0, b, bh0, f1, left1, grad, left, grad1, a1, a_right, f, fluid)
     return gradient, adjoint_out
 
 

time: 48.6 us -> 48.5 us (level)
    pallas_call x6 -> x4, Pallas kernels: 3.07 us -> 2.98 us  [the longest x1 1.25 us: body(): call(left_middle_kernel, moments_out + [(2, OWN, LANES), (Q,) + half, fie...]
where the time goes in v9:
time: 48.5 us; the launch traced here: 48.2 us
  starting transfers between devices  24.1 us (50%)
  waiting for transfers between devices  18 us (37%)
  Pallas kernels  5.39 us (11%)
  between operations  0.74 us (2%)
    ppermute x4, starting transfers between devices, both_ways(): lax.ppermute(up, axis, ring)  13.4 us
    ppermute x4, starting transfers between devices, both_ways(): lax.ppermute(down, axis, [(j, i) for i, j in ring])  10.7 us
    ppermute x4, waiting for transfers between devices, both_ways(): lax.ppermute(up, axis, ring)  9.61 us
    ppermute x4, waiting for transfers between devices, both_ways(): lax.ppermute(down, axis, [(j, i) for i, j in ring])  8.37 us
    pallas_call x1, Pallas kernels, body(): call(left_middle_kernel, moments_out + [(2, OWN, LANES), (Q,) + half, fie...  1.25 us
    pallas_call x1, Pallas kernels, body(): call(rows_kernel, [(YTILES, 8, LANES)] * 2 + [block, block, block, (1,) +...  1.2 us
    pallas_call x1, Pallas kernels, body(): call(left_last_kernel, [cells, block], [(OWN, LANES), field, field, (SEND...  1.17 us
  transfers between devices with their start and end apart: 8, of which 7 were waited for; matrix products, arithmetic and copies ran while one was open for 0% of the time, Pallas kernels for 2%

profile of v9, /device:TPU:24, one launch (start us, length us, event | category | flops | bytes accessed | tf_op | source)
XLA Modules:
  0.0 48.2 jit_solution(14417699429299810426)
XLA Ops:
  0.6 1.2 %shard_map.59 = (f32[27,8,128]{2,1,0:T(8,128)S(1)}, f32[27,8,128]{2,1,0:T(8,128)S(1)}, f32[19,2,16,128]{3,2,1,0:T(8,128)S(1)}, f32[19,2,16,128]{3,2,1,0:T(8,128)...) custom-call(f32[19,2,16,128]{3,2,1,0:T(8,128)} %f_hbm.1, ...), custom_call_target="tpu_custom_call" | custom-call | flops 2000000 | bytes 1000000 | tf_op jit(solution)/shard_map/pallas_call | solution.py:709
  1.8 7.5 %collective-permute-start = (f32[27,8,128]{2,1,0:T(8,128)S(1)}, f32[27,8,128]{2,1,0:T(8,128)S(1)}, u32[]{:S(2)}, u32[]{:S(2)}) collective-permute-start(f32[27,8,128]{2,1,0:T(8,128)S(1)} %get-tuple-element.39), channel_id=1, source_target_pairs={{0,32},{32,64},{64,96},{96,0},{1,33},{33,65},{65,97},{97,1},{2,34}... | collective-permute-start | bytes 331784 | tf_op jit(solution)/shard_map/ppermute | solution.py:701
  9.4 1.9 %collective-permute-start.1 = (f32[27,8,128]{2,1,0:T(8,128)S(1)}, f32[27,8,128]{2,1,0:T(8,128)S(1)}, u32[]{:S(2)}, u32[]{:S(2)}) collective-permute-start(f32[27,8,128]{2,1,0:T(8,128)S(1)} %get-tuple-element.40), channel_id=1, source_target_pairs={{32,0},{64,32},{96,64},{0,96},{33,1},{65,33},{97,65},{1,97},{34,2}... | collective-permute-start | bytes 331784 | tf_op jit(solution)/shard_map/ppermute | solution.py:701
  11.3 0.4 collective-permute-done.below_ref
  11.7 5.5 %collective-permute-done.1.above_ref = f32[27,8,128]{2,1,0:T(8,128)S(1)} collective-permute-done((f32[27,8,128]{2,1,0:T(8,128)S(1)}, f32[27,8,128]{2,1,0:T(8,128)S(1)}, u32[]{:S(2)}, u32[]{:S(2)}) %collective-permute-start.1) | collective-permute-done | bytes 110624 | tf_op jit(solution)/shard_map/ppermute | solution.py:701
  17.2 0.3 shard_map.60
  17.5 0.0 collective-permute-start.2
  17.6 2.9 %collective-permute-start.3 = (f32[3,24,128]{2,1,0:T(8,128)S(1)}, f32[3,24,128]{2,1,0:T(8,128)S(1)}, u32[]{:S(2)}, u32[]{:S(2)}) collective-permute-start(f32[3,24,128]{2,1,0:T(8,128)S(1)} %get-tuple-element.45), channel_id=1, source_target_pairs={{1,0},{2,1},{3,2},{4,3},{5,4},{6,5},{7,6},{8,7},{9,8},{10,9},{11,1... | collective-permute-start | bytes 110600 | tf_op jit(solution)/shard_map/ppermute | solution.py:701
  20.5 0.1 shard_map.61
  20.6 1.5 %collective-permute-done.2.before_ref = f32[3,24,128]{2,1,0:T(8,128)S(1)} collective-permute-done((f32[3,24,128]{2,1,0:T(8,128)S(1)}, f32[3,24,128]{2,1,0:T(8,128)S(1)}, u32[]{:S(2)}, u32[]{:S(2)}) %collective-permute-start.2) | collective-permute-done | bytes 36896 | tf_op jit(solution)/shard_map/ppermute | solution.py:701
  22.1 0.0 collective-permute-done.3.beyond_ref
  22.2 0.5 %shard_map.62 = (f32[19,2,2,24,128]{4,3,2,1,0:T(8,128)S(1)}, f32[19,2,24,128]{3,2,1,0:T(8,128)S(1)}, f32[2,2,24,128]{3,2,1,0:T(8,128)S(1)}, f32[432,128]{1,0:T(8,128)S(1)}, f32[432,128]{1,0:T(8,128)S(1)}) custom-call(f32[39,2,24,128]{3,2,1,0:T(8,128)S(1)} %get-tuple-element.41.main_ref, f32[19,2,24,128]{3,2,1,0:T(8,128)S(1)} %get-tuple-element.42.g_ref, ...), custom_call_target="tpu_custom_call" | custom-call | flops 2000000 | bytes 1000000 | tf_op jit(solution)/shard_map/pallas_call | solution.py:720
  22.6 3.9 %collective-permute-start.5 = (f32[432,128]{1,0:T(8,128)S(1)}, f32[432,128]{1,0:T(8,128)S(1)}, u32[]{:S(2)}, u32[]{:S(2)}) collective-permute-start(f32[432,128]{1,0:T(8,128)S(1)} %get-tuple-element.50), channel_id=1, source_target_pairs={{128,0},{256,128},{384,256},{0,384},{129,1},{257,129},{385,257},{1... | collective-permute-start | bytes 663560 | tf_op jit(solution)/shard_map/ppermute | solution.py:701
  26.6 1.9 %collective-permute-start.4 = (f32[432,128]{1,0:T(8,128)S(1)}, f32[432,128]{1,0:T(8,128)S(1)}, u32[]{:S(2)}, u32[]{:S(2)}) collective-permute-start(f32[432,128]{1,0:T(8,128)S(1)} %get-tuple-element.49), channel_id=1, source_target_pairs={{0,128},{128,256},{256,384},{384,0},{1,129},{129,257},{257,385},{3... | collective-permute-start | bytes 663560 | tf_op jit(solution)/shard_map/ppermute | solution.py:701
  28.5 0.3 shard_map.63.b2_ref
  28.8 1.7 %collective-permute-done.5.got_ref.right_ref.got1_ref = f32[432,128]{1,0:T(8,128)S(1)} collective-permute-done((f32[432,128]{1,0:T(8,128)S(1)}, f32[432,128]{1,0:T(8,128)S(1)}, u32[]{:S(2)}, u32[]{:S(2)}) %collective-permute-start.5) | collective-permute-done | bytes 221216 | tf_op jit(solution)/shard_map/ppermute | solution.py:701
  30.5 0.3 shard_map.64
  30.7 4.9 %collective-permute-done.4.left_ref.got1_ref = f32[432,128]{1,0:T(8,128)S(1)} collective-permute-done((f32[432,128]{1,0:T(8,128)S(1)}, f32[432,128]{1,0:T(8,128)S(1)}, u32[]{:S(2)}, u32[]{:S(2)}) %collective-permute-start.4) | collective-permute-done | bytes 221216 | tf_op jit(solution)/shard_map/ppermute | solution.py:701
  35.6 1.3 %shard_map.65 = (f32[4,2,24,128]{3,2,1,0:T(8,128)S(1)}, f32[3,2,24,128]{3,2,1,0:T(8,128)S(1)}, f32[2,24,128]{2,1,0:T(8,128)S(1)}, f32[2,16,128]{2,1,0:T(8,128)S(...) custom-call(f32[19,2,2,24,128]{4,3,2,1,0:T(8,128)S(1)} %get-tuple-el, ...), custom_call_target="tpu_custom_call" | custom-call | flops 2000000 | bytes 1000000 | tf_op jit(solution)/shard_map/pallas_call | solution.py:732
  36.9 1.9 %collective-permute-start.7 = (f32[35,8,128]{2,1,0:T(8,128)S(1)}, f32[35,8,128]{2,1,0:T(8,128)S(1)}, u32[]{:S(2)}, u32[]{:S(2)}) collective-permute-start(f32[35,8,128]{2,1,0:T(8,128)S(1)} %get-tuple-element.64), channel_id=1, source_target_pairs={{128,0},{256,128},{384,256},{0,384},{129,1},{257,129},{385,257},{1... | collective-permute-start | bytes 430088 | tf_op jit(solution)/shard_map/ppermute | solution.py:701
  38.8 3.9 %collective-permute-start.6 = (f32[35,8,128]{2,1,0:T(8,128)S(1)}, f32[35,8,128]{2,1,0:T(8,128)S(1)}, u32[]{:S(2)}, u32[]{:S(2)}) collective-permute-start(f32[35,8,128]{2,1,0:T(8,128)S(1)} %get-tuple-element.61), channel_id=1, source_target_pairs={{0,128},{128,256},{256,384},{384,0},{1,129},{129,257},{257,385},{3... | collective-permute-start | bytes 430088 | tf_op jit(solution)/shard_map/ppermute | solution.py:701
  42.7 1.1 %collective-permute-done.7.got_ref = f32[35,8,128]{2,1,0:T(8,128)S(1)} collective-permute-done((f32[35,8,128]{2,1,0:T(8,128)S(1)}, f32[35,8,128]{2,1,0:T(8,128)S(1)}, u32[]{:S(2)}, u32[]{:S(2)}) %collective-permute-start.7) | collective-permute-done | bytes 143392 | tf_op jit(solution)/shard_map/ppermute | solution.py:701
  43.9 0.3 shard_map.66
  44.2 2.8 %collective-permute-done.6.got_ref = f32[35,8,128]{2,1,0:T(8,128)S(1)} collective-permute-done((f32[35,8,128]{2,1,0:T(8,128)S(1)}, f32[35,8,128]{2,1,0:T(8,128)S(1)}, u32[]{:S(2)}, u32[]{:S(2)}) %collective-permute-start.6) | collective-permute-done | bytes 143392 | tf_op jit(solution)/shard_map/ppermute | solution.py:701
  47.0 1.2 %shard_map.67 = (f32[2,16,128]{2,1,0:T(8,128)}, f32[19,2,16,128]{3,2,1,0:T(8,128)}) custom-call(f32[19,2,2,24,128]{4,3,2,1,0:T(8,128)S(1)} %get-tuple-element.54.b1_ref, f32[19,2,24,128]{3,2,1,0:T(8,128)S(1)} %get-tuple-element.55.edge1_ref, f32[4,2,2,24,128]{4,3,2,1,0:T(8,128)S(1)} %get-tuple-element.56.sums_ref, ...), custom_call_target="tpu_custom_call" | custom-call | flops 2000000 | bytes 1000000 | tf_op jit(solution)/shard_map/pallas_call | solution.py:741
Async XLA Ops:
  1.8 9.8 %collective-permute-start = (f32[27,8,128]{2,1,0:T(8,128)S(1)}, f32[27,8,128]{2,1,0:T(8,128)S(1)}, u32[]{:S(2)}, u32[]{:S(2)}) collective-permute-start(f32[27,8,128]{2,1,0:T(8,128)S(1)} %get-tuple-element.39), channel_id=1, source_target_pairs={{0,32},{32,64},{64,96},{96,0},{1,33},{33,65},{65,97},{97,1},{2,34}... | collective-permute-start | bytes 331784 | tf_op jit(solution)/shard_map/ppermute | solution.py:701
  9.4 7.9 %collective-permute-start.1 = (f32[27,8,128]{2,1,0:T(8,128)S(1)}, f32[27,8,128]{2,1,0:T(8,128)S(1)}, u32[]{:S(2)}, u32[]{:S(2)}) collective-permute-start(f32[27,8,128]{2,1,0:T(8,128)S(1)} %get-tuple-element.40), channel_id=1, source_target_pairs={{32,0},{64,32},{96,64},{0,96},{33,1},{65,33},{97,65},{1,97},{34,2}... | collective-permute-start | bytes 331784 | tf_op jit(solution)/shard_map/ppermute | solution.py:701
  17.5 4.6 %collective-permute-start.2 = (f32[3,24,128]{2,1,0:T(8,128)S(1)}, f32[3,24,128]{2,1,0:T(8,128)S(1)}, u32[]{:S(2)}, u32[]{:S(2)}) collective-permute-start(f32[3,24,128]{2,1,0:T(8,128)S(1)} %get-tuple-element.44), channel_id=1, source_target_pairs={{0,1},{1,2},{2,3},{3,4},{4,5},{5,6},{6,7},{7,8},{8,9},{9,10},{10,1... | collective-permute-start | bytes 110600 | tf_op jit(solution)/shard_map/ppermute | solution.py:701
  17.6 4.6 %collective-permute-start.3 = (f32[3,24,128]{2,1,0:T(8,128)S(1)}, f32[3,24,128]{2,1,0:T(8,128)S(1)}, u32[]{:S(2)}, u32[]{:S(2)}) collective-permute-start(f32[3,24,128]{2,1,0:T(8,128)S(1)} %get-tuple-element.45), channel_id=1, source_target_pairs={{1,0},{2,1},{3,2},{4,3},{5,4},{6,5},{7,6},{8,7},{9,8},{10,9},{11,1... | collective-permute-start | bytes 110600 | tf_op jit(solution)/shard_map/ppermute | solution.py:701
  22.6 7.8 %collective-permute-start.5 = (f32[432,128]{1,0:T(8,128)S(1)}, f32[432,128]{1,0:T(8,128)S(1)}, u32[]{:S(2)}, u32[]{:S(2)}) collective-permute-start(f32[432,128]{1,0:T(8,128)S(1)} %get-tuple-element.50), channel_id=1, source_target_pairs={{128,0},{256,128},{384,256},{0,384},{129,1},{257,129},{385,257},{1... | collective-permute-start | bytes 663560 | tf_op jit(solution)/shard_map/ppermute | solution.py:701
  26.6 9.0 %collective-permute-start.4 = (f32[432,128]{1,0:T(8,128)S(1)}, f32[432,128]{1,0:T(8,128)S(1)}, u32[]{:S(2)}, u32[]{:S(2)}) collective-permute-start(f32[432,128]{1,0:T(8,128)S(1)} %get-tuple-element.49), channel_id=1, source_target_pairs={{0,128},{128,256},{256,384},{384,0},{1,129},{129,257},{257,385},{3... | collective-permute-start | bytes 663560 | tf_op jit(solution)/shard_map/ppermute | solution.py:701
  36.9 7.0 %collective-permute-start.7 = (f32[35,8,128]{2,1,0:T(8,128)S(1)}, f32[35,8,128]{2,1,0:T(8,128)S(1)}, u32[]{:S(2)}, u32[]{:S(2)}) collective-permute-start(f32[35,8,128]{2,1,0:T(8,128)S(1)} %get-tuple-element.64), channel_id=1, source_target_pairs={{128,0},{256,128},{384,256},{0,384},{129,1},{257,129},{385,257},{1... | collective-permute-start | bytes 430088 | tf_op jit(solution)/shard_map/ppermute | solution.py:701
  38.8 8.2 %collective-permute-start.6 = (f32[35,8,128]{2,1,0:T(8,128)S(1)}, f32[35,8,128]{2,1,0:T(8,128)S(1)}, u32[]{:S(2)}, u32[]{:S(2)}) collective-permute-start(f32[35,8,128]{2,1,0:T(8,128)S(1)} %get-tuple-element.61), channel_id=1, source_target_pairs={{0,128},{128,256},{256,384},{384,0},{1,129},{129,257},{257,385},{3... | collective-permute-start | bytes 430088 | tf_op jit(solution)/shard_map/ppermute | solution.py:701
